TPU v7x, 128 devices: a whole 4x4x4 slice. The times are simulated.
128 devices in a mesh: prompt: 8 (over z_hi, x), roll: 16 (over y, z_lo, core).
Axes of the slice: x: 4, y: 4, z: 4 (z_hi: 2, z_lo: 2; z = z_hi * 2 + z_lo), core: 2. Of those that a mesh axis runs over, the one named last changes fastest.
Arguments:
- prompt_cache: bfloat16 [16, 1024, 512], P('prompt', 'roll'), may hold values from -12 to 12
- key_gain: float32 [128], replicated, may hold values from 1 to 2
- query_gain: float32 [128], replicated, may hold values from 1 to 2
- window_cache: bfloat16 [256, 128, 512], P(('prompt', 'roll')), may hold values from -12 to 12
- queries: bfloat16 [256, 128, 4096], P(('prompt', 'roll')), may hold values from -6 to 6
- upstream: bfloat16 [256, 128, 4096], P(('prompt', 'roll')), may hold values from -6 to 6
- rewards: float32 [256], P(('prompt', 'roll')), may hold values from 0 to 3
- assign: int32 [256], P(('prompt', 'roll')), may hold values from 0 to 1, as said below
- offsets: int32 [256], P(('prompt', 'roll')), may hold values from 0 to 3968
Outputs:
- attended: bfloat16 [256, 128, 4096], P(('prompt', 'roll'))
- query_grad: bfloat16 [256, 128, 4096], P(('prompt', 'roll'))
- window_grad: bfloat16 [256, 128, 512], P(('prompt', 'roll'))
- prompt_grad: bfloat16 [16, 1024, 512], P('prompt', 'roll')
Inputs may be any that keep to these rules, and one draw needn't show every extreme that they name: `assign`: within each group of 32 rollouts, each of the 2 prompt indices is named by exactly 16 rollouts.
All inputs are finite; a program needn't handle non-finite values.
Results may differ from a plain program's by a relative error of at most 0.023.
Values may be sent and summed in bfloat16 or wider, within the bound.
No kernel may reach another device: no remote copies, remote signals or barrier semaphores. Data moves between devices by JAX's collectives and lax.ppermute only.
A program may use at most 192 MiB of HBM per device.

v0:
```python
from functools import partial
import math

import jax
import jax.numpy as jnp
from jax import lax
from jax.sharding import PartitionSpec as P

rope_base = 1000000.0
norm_eps = 1e-06
spread_eps = 1e-06


def rotate(values, positions):
    half_size = values.shape[-1] // 2
    frequency = rope_base ** (-(jnp.arange(half_size, dtype=jnp.float32) * 2.0) / values.shape[-1])
    angles = positions.astype(jnp.float32)[:, None] * frequency[None, :]
    cosine = jnp.cos(angles)[:, None, :]
    sine_part = jnp.sin(angles)[:, None, :]
    lower_half = values[..., :half_size]
    upper_half = values[..., half_size:]
    return jnp.concatenate(
        [
            lower_half * cosine - upper_half * sine_part,
            upper_half * cosine + lower_half * sine_part,
        ],
        axis=-1,
    )


def prepare(values, gain, positions):
    inverse = lax.rsqrt(jnp.mean(values * values, axis=-1, keepdims=True) + norm_eps)
    return rotate(values * inverse * gain, positions)


def local(
    prompt_cache, key_gain, query_gain, window_cache, queries, upstream, rewards, assign, offsets
):
    groups = lax.axis_size("prompt")
    members = lax.axis_size("roll")
    roll_count = queries.shape[0]
    prompt_count = prompt_cache.shape[0]
    part_rows = prompt_cache.shape[1]
    head_size = key_gain.shape[0]
    key_width = window_cache.shape[2] // 2
    key_heads = key_width // head_size
    query_heads = queries.shape[2] // head_size
    group_size = query_heads // key_heads
    window = queries.shape[1]
    block_rows = group_size * window
    root_size = math.sqrt(head_size)
    per_prompt = roll_count * members // prompt_count
    total_rolls = roll_count * members * groups
    full_rows = part_rows * members
    chosen_table = (assign[:, None] == jnp.arange(prompt_count, dtype=jnp.int32)[None, :]).astype(
        jnp.float32
    )
    group_totals = lax.psum(jnp.sum(chosen_table * rewards[:, None], axis=0), "roll")
    prompt_means = group_totals / per_prompt
    centred = rewards - jnp.sum(chosen_table * prompt_means[None, :], axis=1)
    spread_total = lax.psum(jnp.sum(centred * centred), ("prompt", "roll"))
    advantage = centred / jnp.sqrt(spread_total / total_rolls + spread_eps)
    owner_pos = lax.axis_index("roll") * part_rows + jnp.arange(part_rows, dtype=jnp.int32)
    raw_keys = (
        prompt_cache[:, :, :key_width]
        .astype(jnp.float32)
        .reshape(prompt_count, part_rows, key_heads, head_size)
    )

    def owner_prepare(features):
        return prepare(features, key_gain, owner_pos)

    ready_keys = (
        jax.vmap(owner_prepare)(raw_keys)
        .reshape(prompt_count, part_rows, key_width)
        .astype(jnp.bfloat16)
    )
    shipped = jnp.concatenate([ready_keys, prompt_cache[:, :, key_width:]], axis=2)
    token_index = jnp.arange(window, dtype=jnp.int32)
    row_token = jnp.arange(block_rows, dtype=jnp.int32) % window
    visible = row_token[:, None] >= token_index[None, :]
    query_rows, query_pulls, window_keys, window_values, window_pulls, grad_out = (
        [],
        [],
        [],
        [],
        [],
        [],
    )
    for rollout in range(roll_count):
        positions = full_rows + offsets[rollout] + token_index
        raw_query = queries[rollout].astype(jnp.float32).reshape(window, query_heads, head_size)
        ready_query, query_pull = jax.vjp(
            partial(prepare, gain=query_gain, positions=positions), raw_query
        )
        query_rows.append(
            ready_query.astype(jnp.bfloat16)
            .reshape(window, key_heads, group_size, head_size)
            .transpose(1, 2, 0, 3)
            .reshape(key_heads, block_rows, head_size)
        )
        query_pulls.append(query_pull)
        raw_window = (
            window_cache[rollout][:, :key_width]
            .astype(jnp.float32)
            .reshape(window, key_heads, head_size)
        )
        ready_window, window_pull = jax.vjp(
            partial(prepare, gain=key_gain, positions=positions), raw_window
        )
        window_keys.append(ready_window.astype(jnp.bfloat16))
        window_pulls.append(window_pull)
        window_values.append(
            window_cache[rollout][:, key_width:].reshape(window, key_heads, head_size)
        )
        scaled = (advantage[rollout] * upstream[rollout].astype(jnp.float32)).astype(jnp.bfloat16)
        grad_out.append(
            scaled.reshape(window, key_heads, group_size, head_size)
            .transpose(1, 2, 0, 3)
            .reshape(key_heads, block_rows, head_size)
        )
    gathered = lax.all_gather(shipped, "roll", axis=1, tiled=True)
    numerator = jnp.zeros((roll_count, key_heads, block_rows, head_size), jnp.float32)
    denominator = jnp.zeros((roll_count, key_heads, block_rows), jnp.float32)
    for rollout in range(roll_count):
        chosen = lax.dynamic_index_in_dim(gathered, assign[rollout], 0, keepdims=False)
        for key_head in range(key_heads):
            keys_here = chosen[:, key_head * head_size : (key_head + 1) * head_size]
            values_here = chosen[
                :, key_width + key_head * head_size : key_width + (key_head + 1) * head_size
            ]
            scores = (
                jnp.einsum(
                    "rd,td->rt",
                    query_rows[rollout][key_head],
                    keys_here,
                    preferred_element_type=jnp.float32,
                )
                / root_size
            )
            exponent = jnp.exp(scores)
            denominator = denominator.at[rollout, key_head].add(jnp.sum(exponent, axis=1))
            numerator = numerator.at[rollout, key_head].add(
                jnp.dot(
                    exponent.astype(jnp.bfloat16), values_here, preferred_element_type=jnp.float32
                )
            )
    for rollout in range(roll_count):
        for key_head in range(key_heads):
            scores = (
                jnp.einsum(
                    "rd,td->rt",
                    query_rows[rollout][key_head],
                    window_keys[rollout][:, key_head],
                    preferred_element_type=jnp.float32,
                )
                / root_size
            )
            exponent = jnp.where(visible, jnp.exp(scores), 0.0)
            denominator = denominator.at[rollout, key_head].add(jnp.sum(exponent, axis=1))
            numerator = numerator.at[rollout, key_head].add(
                jnp.dot(
                    exponent.astype(jnp.bfloat16),
                    window_values[rollout][:, key_head],
                    preferred_element_type=jnp.float32,
                )
            )
    output = numerator / denominator[..., None]
    row_dot = jnp.sum(jnp.stack(grad_out).astype(jnp.float32) * output, axis=-1)
    count = gathered.shape[1]
    anchor = jnp.zeros((), jnp.int32)
    grad_rows = jnp.zeros((roll_count, key_heads, block_rows, head_size), jnp.float32)
    term = jnp.zeros((count, prompt_count, 2 * key_width), jnp.float32)
    for prompt_rollout in range(roll_count):
        chosen = lax.dynamic_index_in_dim(gathered, assign[prompt_rollout], 0, keepdims=False)
        prompt_key_parts, prompt_value_parts = ([], [])
        for prompt_key_head in range(key_heads):
            prompt_keys_here = chosen[
                :, prompt_key_head * head_size : (prompt_key_head + 1) * head_size
            ]
            prompt_values_here = chosen[
                :,
                key_width
                + prompt_key_head * head_size : key_width
                + (prompt_key_head + 1) * head_size,
            ]
            prompt_scores = (
                jnp.einsum(
                    "rd,td->rt",
                    query_rows[prompt_rollout][prompt_key_head],
                    prompt_keys_here,
                    preferred_element_type=jnp.float32,
                )
                / root_size
            )
            prompt_normed_prob = (
                jnp.exp(prompt_scores) / denominator[prompt_rollout, prompt_key_head][:, None]
            )
            prompt_grad_prob = jnp.einsum(
                "rd,td->rt",
                grad_out[prompt_rollout][prompt_key_head],
                prompt_values_here,
                preferred_element_type=jnp.float32,
            )
            prompt_grad_score = (
                prompt_normed_prob
                * (prompt_grad_prob - row_dot[prompt_rollout, prompt_key_head][:, None])
            ).astype(jnp.bfloat16)
            grad_rows = grad_rows.at[prompt_rollout, prompt_key_head].add(
                jnp.dot(prompt_grad_score, prompt_keys_here, preferred_element_type=jnp.float32)
                / root_size
            )
            prompt_key_parts.append(
                jnp.einsum(
                    "rt,rd->td",
                    prompt_grad_score,
                    query_rows[prompt_rollout][prompt_key_head],
                    preferred_element_type=jnp.float32,
                )
                / root_size
            )
            prompt_value_parts.append(
                jnp.einsum(
                    "rt,rd->td",
                    prompt_normed_prob.astype(jnp.bfloat16),
                    grad_out[prompt_rollout][prompt_key_head],
                    preferred_element_type=jnp.float32,
                )
            )
        contribution = jnp.concatenate(prompt_key_parts + prompt_value_parts, axis=1)
        corner = (anchor, assign[prompt_rollout], anchor)
        previous = lax.dynamic_slice(term, corner, (count, 1, 2 * key_width))
        term = lax.dynamic_update_slice(term, previous + contribution[:, None, :], corner)
    grad_rows, term = (grad_rows, term)
    reduced = lax.psum_scatter(
        term.astype(jnp.bfloat16), "roll", scatter_dimension=0, tiled=True
    ).astype(jnp.float32)
    reduced = reduced.transpose(1, 0, 2)
    attended_list, query_list, window_list = ([], [], [])
    for rollout in range(roll_count):
        key_parts, value_parts = ([], [])
        for key_head in range(key_heads):
            keys_here = window_keys[rollout][:, key_head]
            values_here = window_values[rollout][:, key_head]
            scores = (
                jnp.einsum(
                    "rd,td->rt",
                    query_rows[rollout][key_head],
                    keys_here,
                    preferred_element_type=jnp.float32,
                )
                / root_size
            )
            normed_prob = (
                jnp.where(visible, jnp.exp(scores), 0.0) / denominator[rollout, key_head][:, None]
            )
            grad_prob = jnp.einsum(
                "rd,td->rt",
                grad_out[rollout][key_head],
                values_here,
                preferred_element_type=jnp.float32,
            )
            grad_score = (normed_prob * (grad_prob - row_dot[rollout, key_head][:, None])).astype(
                jnp.bfloat16
            )
            grad_rows = grad_rows.at[rollout, key_head].add(
                jnp.dot(grad_score, keys_here, preferred_element_type=jnp.float32) / root_size
            )
            key_parts.append(
                jnp.einsum(
                    "rt,rd->td",
                    grad_score,
                    query_rows[rollout][key_head],
                    preferred_element_type=jnp.float32,
                )
                / root_size
            )
            value_parts.append(
                jnp.einsum(
                    "rt,rd->td",
                    normed_prob.astype(jnp.bfloat16),
                    grad_out[rollout][key_head],
                    preferred_element_type=jnp.float32,
                )
            )
        window_key_grad = window_pulls[rollout](jnp.stack(key_parts, axis=1))[0].reshape(
            window, key_width
        )
        window_list.append(
            jnp.concatenate([window_key_grad] + value_parts, axis=1).astype(jnp.bfloat16)
        )
        attended_list.append(
            output[rollout]
            .reshape(key_heads, group_size, window, head_size)
            .transpose(2, 0, 1, 3)
            .reshape(window, query_heads * head_size)
            .astype(jnp.bfloat16)
        )
        grad_query = (
            grad_rows[rollout]
            .reshape(key_heads, group_size, window, head_size)
            .transpose(2, 0, 1, 3)
            .reshape(window, query_heads, head_size)
        )
        query_list.append(
            query_pulls[rollout](grad_query)[0]
            .reshape(window, query_heads * head_size)
            .astype(jnp.bfloat16)
        )
    key_pull = jax.vjp(jax.vmap(owner_prepare), raw_keys)[1]
    prompt_key_grad = key_pull(
        reduced[:, :, :key_width].reshape(prompt_count, part_rows, key_heads, head_size)
    )[0].reshape(prompt_count, part_rows, key_width)
    prompt_grad = jnp.concatenate([prompt_key_grad, reduced[:, :, key_width:]], axis=2).astype(
        jnp.bfloat16
    )
    return (jnp.stack(attended_list), jnp.stack(query_list), jnp.stack(window_list), prompt_grad)


def solution(mesh):
    return jax.shard_map(
        local,
        mesh=mesh,
        in_specs=(
            P("prompt", "roll", None),
            P(),
            P(),
            P(("prompt", "roll"), None, None),
            P(("prompt", "roll"), None, None),
            P(("prompt", "roll"), None, None),
            P(("prompt", "roll")),
            P(("prompt", "roll")),
            P(("prompt", "roll")),
        ),
        out_specs=(
            P(("prompt", "roll"), None, None),
            P(("prompt", "roll"), None, None),
            P(("prompt", "roll"), None, None),
            P("prompt", "roll", None),
        ),
        check_vma=False,
    )
```

profile of v0, /device:TPU:0, one launch (start us, length us, event | category | flops | bytes accessed | tf_op | source)
XLA Modules:
  0.0 383.5 jit_solution(11747245017122374430)
XLA Ops:
  15.2 3.2 convert_bitcast_fusion
  26.4 3.2 multiply_multiply_fusion
  37.0 31.1 %psum.14 = f32[2]{0:T(128)S(1)} all-reduce(f32[2]{0:T(128)S(1)} %select_reduce_fusion.1), channel_id=1, replica_groups=mesh['prompt'=8,'roll'=16] {'roll'}, use_global_device_ids=true, to_apply=%region_14.15 | all-reduce | flops 2 | bytes 16 | tf_op jit(solution)/shard_map/psum | solution.py:58
  68.9 64.1 %psum.15 = f32[]{:T(128)} all-reduce(f32[]{:T(128)} %get-tuple-element.324), channel_id=1, replica_groups=mesh['prompt'=8,'roll'=16] {'prompt','roll'}, use_global_device_ids=true, to_apply=%region_17.18 | all-reduce | flops 1 | bytes 8 | tf_op jit(solution)/shard_map/psum | solution.py:61
  134.3 3.3 fusion.127
  156.3 4.6 %fusion.1 = (f32[2048]{0:T(1024)S(1)}, f32[2048,1024]{0,1:T(8,128)}) fusion(bf16[2048,128]{1,0:T(8,128)(2,1)S(1)} %bitcast.353, bf16[1024,512]{1,0:T(8,128)(2,1)S(1)} %get-tuple-element.341), kind=kOutput, calls=%fused_computation.9 | convolution fusion | flops 541063168 | bytes 9183232 | tf_op jit(solution)/shard_map/rd,td->rt/dot_general | solution.py:133
  160.9 4.6 %fusion.4 = (f32[2048]{0:T(1024)S(1)}, f32[2048,1024]{0,1:T(8,128)}) fusion(bf16[2048,128]{1,0:T(8,128)(2,1)S(1)} %bitcast.357, bf16[1024,512]{1,0:T(8,128)(2,1)S(1)} %get-tuple-element.341), kind=kOutput, calls=%fused_computation.12 | convolution fusion | flops 541063168 | bytes 9183232 | tf_op jit(solution)/shard_map/rd,td->rt/dot_general | solution.py:133
  165.5 4.6 %fusion.7 = (f32[2048]{0:T(1024)S(1)}, f32[2048,1024]{0,1:T(8,128)}) fusion(bf16[2048,128]{1,0:T(8,128)(2,1)S(1)} %bitcast.365, bf16[1024,512]{1,0:T(8,128)(2,1)S(1)} %get-tuple-element.340), kind=kOutput, calls=%fused_computation.15 | convolution fusion | flops 541063168 | bytes 9183232 | tf_op jit(solution)/shard_map/rd,td->rt/dot_general | solution.py:133
  170.2 4.5 %fusion.10 = (f32[2048]{0:T(1024)S(1)}, f32[2048,1024]{0,1:T(8,128)}) fusion(bf16[2048,128]{1,0:T(8,128)(2,1)S(1)} %bitcast.361, bf16[1024,512]{1,0:T(8,128)(2,1)S(1)} %get-tuple-element.340), kind=kOutput, calls=%fused_computation.18 | convolution fusion | flops 541063168 | bytes 9183232 | tf_op jit(solution)/shard_map/rd,td->rt/dot_general | solution.py:133
  181.0 4.9 %fusion.32 = f32[1,1,2048,128]{3,2,1,0:T(8,128)S(1)} fusion(f32[2048,1024]{0,1:T(8,128)} %get-tuple-element.408, bf16[1024,512]{1,0:T(8,128)(2,1)S(1)} %copy-done.30), kind=kOutput, calls=%fused_computation.39 | convolution fusion | flops 541065216 | bytes 9699328 | tf_op jit(solution)/shard_map/dot_general | solution.py:144
  186.2 7.7 %fusion.87 = f32[2,2,2048,128]{3,2,1,0:T(8,128)S(1)} fusion(f32[2,2,2048,128]{3,2,1,0:T(8,128)S(1)} %scatter-add.80, s32[]{:T(128)} %bitcast.8, s32[]{:T(128)} %bitcast.9, f32[2048,1024]{0,1:T(8,128)} %get-tuple-element.410, f32[1,1,2048,128]{3,2,1,0:T(8,128)S(1)} %fusion.32, bf16[1024,512]{1,0:T(8,128)(2,1)S(1)} %copy-done.30), kind=kOutput, calls=%fused_computation.96 | convolution fusion | flops 541327360 | bytes 10747912 | tf_op jit(solution)/shard_map/dot_general | solution.py:144
  201.1 3.8 multiply_reduce_fusion
  211.1 2.5 fusion.20
  217.3 2.6 fusion.24
  219.9 3.2 multiply_convert_fusion.2
  226.3 2.6 multiply_convert_fusion.3
  245.0 6.3 %copy.340 = bf16[1024,2,512]{2,1,0:T(2,128)(2,1)} copy(bf16[1024,2,512]{0,2,1:T(8,128)(2,1)} %convert_element_type.289) | data formatting | bytes 4194304 | tf_op jit(solution)/shard_map/convert_element_type | solution.py:236
  263.6 3.6 fusion.95
  276.6 2.7 copy.331
  279.3 2.8 multiply_add_fusion.1
  285.0 3.2 multiply_add_fusion.3
  291.1 2.6 multiply_reduce_fusion.2
  294.1 7.8 %fusion.112 = (bf16[128,32,128]{2,1,0:T(8,128)(2,1)}, bf16[128,32,128]{2,1,0:T(8,128)(2,1)S(1)}) fusion(f32[128,32]{1,0:T(8,128)S(1)} %copy.326, f32[128,32]{1,0:T(8,128)S(1)} %copy-done.56, f32[128]{0:T(128)S(1)} %copy-done.126, f32[128,32,64]{2,1,0:T(8,128)} %copy-done.13, f32[128,32,64]{2,1,0:T(8,128)} %copy-done.12, ...), kind=kLoop, calls=%fused_computation.115 | loop fusion | flops 7340032 | bytes 10551808 | tf_op jit(solution)/shard_map/convert_element_type | solution.py:308
  315.7 57.1 %all-reduce.16.cloned.1.call-done = bf16[1024,2,512]{2,1,0:T(2,128)(2,1)} async-done(((bf16[1024,2,512]{2,1,0:T(2,128)(2,1)}), bf16[1024,2,512]{2,1,0:T(2,128)(2,1)}) %all-reduce.16.cloned.1.call-update) | async-done | bytes 2097168
  (464 shorter events, 123.8 us)
Async XLA Ops:
  7.2 147.4 %all-gather.2.cloned.1.call-start = ((), (), s32[]{:S(2)}) async-start(), calls=%async_computation | async-start | bytes 2228224 | tf_op jit(solution)/shard_map/all_gather | solution.py:122
  8.2 10.2 %copy-start.36 = (f32[2,64,2,128]{3,2,1,0:T(2,128)}, f32[2,64,2,128]{3,2,1,0:T(2,128)S(1)}, u32[]{:S(2)}) copy-start(f32[2,64,2,128]{3,2,1,0:T(2,128)S(1)} %reshape.1368) | copy-start | bytes 393220
  11.3 361.5 %all-reduce.16.cloned.1.call-start = ((), (), s32[]{:S(2)}) async-start(), calls=%async_computation.1 | async-start | bytes 4194304
  19.6 10.1 %copy-start.55 = (f32[128,32]{1,0:T(8,128)}, f32[128,32]{1,0:T(8,128)S(1)}, u32[]{:S(2)}) copy-start(f32[128,32]{1,0:T(8,128)S(1)} %copy.289) | copy-start | bytes 49156
  25.9 120.1 %copy-start.72 = (f32[128,64]{0,1:T(8,128)}, f32[128,64]{0,1:T(8,128)S(1)}, u32[]{:S(2)}) copy-start(f32[128,64]{0,1:T(8,128)S(1)} %get-tuple-element.399) | copy-start | bytes 98308
  26.0 120.1 %copy-start.74 = (f32[128,64]{0,1:T(8,128)}, f32[128,64]{0,1:T(8,128)S(1)}, u32[]{:S(2)}) copy-start(f32[128,64]{0,1:T(8,128)S(1)} %get-tuple-element.400) | copy-start | bytes 98308
  26.0 120.1 %copy-start.76 = (f32[128,64]{0,1:T(8,128)}, f32[128,64]{0,1:T(8,128)S(1)}, u32[]{:S(2)}) copy-start(f32[128,64]{0,1:T(8,128)S(1)} %get-tuple-element.383) | copy-start | bytes 98308
  26.0 120.1 %copy-start.78 = (f32[128,64]{0,1:T(8,128)}, f32[128,64]{0,1:T(8,128)S(1)}, u32[]{:S(2)}) copy-start(f32[128,64]{0,1:T(8,128)S(1)} %get-tuple-element.384) | copy-start | bytes 98308
  35.4 110.5 %copy-start.42 = (bf16[1,128,512]{1,2,0:T(8,128)(2,1)}, bf16[1,128,512]{1,2,0:T(8,128)(2,1)S(1)}, u32[]{:S(2)}) copy-start(bf16[1,128,512]{1,2,0:T(8,128)(2,1)S(1)} %copy.364) | copy-start | bytes 393220
  35.6 110.4 %copy-start.44 = (bf16[1,128,512]{1,2,0:T(8,128)(2,1)}, bf16[1,128,512]{1,2,0:T(8,128)(2,1)S(1)}, u32[]{:S(2)}) copy-start(bf16[1,128,512]{1,2,0:T(8,128)(2,1)S(1)} %copy.365) | copy-start | bytes 393220
  146.3 10.0 %copy-start.14 = (bf16[1,16,128,128]{3,2,1,0:T(8,128)(2,1)}, bf16[1,16,128,128]{3,2,1,0:T(8,128)(2,1)S(1)}, u32[]{:S(2)}) copy-start(bf16[1,16,128,128]{3,2,1,0:T(8,128)(2,1)S(1)} %get-tuple-element.355) | copy-start | bytes 1572868
  146.3 14.6 %copy-start.16 = (bf16[1,16,128,128]{3,2,1,0:T(8,128)(2,1)}, bf16[1,16,128,128]{3,2,1,0:T(8,128)(2,1)S(1)}, u32[]{:S(2)}) copy-start(bf16[1,16,128,128]{3,2,1,0:T(8,128)(2,1)S(1)} %get-tuple-element.354) | copy-start | bytes 1572868
  146.4 19.1 %copy-start.20 = (bf16[1,16,128,128]{3,2,1,0:T(8,128)(2,1)}, bf16[1,16,128,128]{3,2,1,0:T(8,128)(2,1)S(1)}, u32[]{:S(2)}) copy-start(bf16[1,16,128,128]{3,2,1,0:T(8,128)(2,1)S(1)} %get-tuple-element.353) | copy-start | bytes 1572868
  146.4 23.7 %copy-start.18 = (bf16[1,16,128,128]{3,2,1,0:T(8,128)(2,1)}, bf16[1,16,128,128]{3,2,1,0:T(8,128)(2,1)S(1)}, u32[]{:S(2)}) copy-start(bf16[1,16,128,128]{3,2,1,0:T(8,128)(2,1)S(1)} %get-tuple-element.352) | copy-start | bytes 1572868
  156.3 13.9 %copy-start.26 = (bf16[1024,512]{1,0:T(8,128)(2,1)}, bf16[1024,512]{1,0:T(8,128)(2,1)S(1)}, u32[]{:S(2)}) copy-start(bf16[1024,512]{1,0:T(8,128)(2,1)S(1)} %get-tuple-element.340) | copy-start | bytes 3145732
  170.2 10.8 %copy-start.30 = (bf16[1024,512]{1,0:T(8,128)(2,1)S(1)}, bf16[1024,512]{1,0:T(8,128)(2,1)}, u32[]{:S(2)}) copy-start(bf16[1024,512]{1,0:T(8,128)(2,1)} %copy-done.29) | copy-start | bytes 3145732
  209.7 30.4 %copy-start.4 = (bf16[2048,1024]{0,1:T(8,128)(2,1)}, bf16[2048,1024]{0,1:T(8,128)(2,1)S(1)}, u32[]{:S(2)}) copy-start(bf16[2048,1024]{0,1:T(8,128)(2,1)S(1)} %multiply_convert_fusion.1) | copy-start | bytes 12582916
  215.9 22.6 %copy-start.6 = (bf16[2048,1024]{0,1:T(8,128)(2,1)}, bf16[2048,1024]{0,1:T(8,128)(2,1)S(1)}, u32[]{:S(2)}) copy-start(bf16[2048,1024]{0,1:T(8,128)(2,1)S(1)} %multiply_convert_fusion) | copy-start | bytes 12582916
  223.1 13.6 %copy-start.8 = (bf16[2048,1024]{0,1:T(8,128)(2,1)}, bf16[2048,1024]{0,1:T(8,128)(2,1)S(1)}, u32[]{:S(2)}) copy-start(bf16[2048,1024]{0,1:T(8,128)(2,1)S(1)} %multiply_convert_fusion.2) | copy-start | bytes 12582916
  312.7 61.6 %copy-start.96 = (f32[64,64]{1,0:T(8,128)S(1)}, f32[64,64]{1,0:T(8,128)}, u32[]{:S(2)}) copy-start(f32[64,64]{1,0:T(8,128)} %copy-done.95) | copy-start | bytes 49156
  312.7 61.6 %copy-start.98 = (f32[64,64]{1,0:T(8,128)S(1)}, f32[64,64]{1,0:T(8,128)}, u32[]{:S(2)}) copy-start(f32[64,64]{1,0:T(8,128)} %copy-done.97) | copy-start | bytes 49156
  312.7 61.8 %copy-start.37 = (f32[2,64,2,128]{3,2,1,0:T(2,128)S(1)}, f32[2,64,2,128]{3,2,1,0:T(2,128)}, u32[]{:S(2)}) copy-start(f32[2,64,2,128]{3,2,1,0:T(2,128)} %copy-done.36) | copy-start | bytes 393220
  314.2 60.7 %copy-start.115 = (f32[2,64,2]{1,2,0:T(2,128)S(1)}, f32[2,64,2]{1,2,0:T(2,128)}, u32[]{:S(2)}) copy-start(f32[2,64,2]{1,2,0:T(2,128)} %copy-done.114) | copy-start | bytes 3076
  314.2 60.8 %copy-start.68 = (f32[2,64,2]{2,1,0:T(8,128)S(1)}, f32[2,64,2]{2,1,0:T(8,128)}, u32[]{:S(2)}) copy-start(f32[2,64,2]{2,1,0:T(8,128)} %copy-done.67) | copy-start | bytes 3076
  (117 other events, 456.7 us)
Sparse Core Ops, SparseCore 0:
  11.4 36.3 all-gather.1
  251.6 121.2 all-reduce.15
where the time goes:
time: 391 us; the launch traced here: 384 us
  blocking collectives  95.2 us (24%)
  matrix products  92.1 us (24%)
  local copies, waits for them, and re-layouts  64.5 us (16%)
  waiting for transfers between devices  57.2 us (15%)
  other arithmetic  51.6 us (13%)
  between operations  22.9 us (6%)
    psum x1, blocking collectives, local(): spread_total = lax.psum(jnp.sum(centred * centred), ('prompt', 'roll'))  64.1 us
    unnamed x3, waiting for transfers between devices  57.2 us
    psum x1, blocking collectives, local(): lax.psum(jnp.sum(chosen_table * rewards[:, None], axis=0), 'roll')  31.1 us
    dot_general x4, matrix products, local(): jnp.einsum('rd,td->rt', query_rows[rollout][key_head], keys_here, preferr...  18.4 us
    unnamed x288, local copies, waits for them, and re-layouts  16.6 us
    dot_general x4, matrix products, local(): jnp.dot(exponent.astype(jnp.bfloat16), values_here, preferred_element_typ...  16.2 us
    dot_general x4, matrix products, local(): jnp.einsum('rd,td->rt', grad_out[prompt_rollout][prompt_key_head], prompt...  10.3 us
    dot_general x4, matrix products, local(): jnp.einsum('rt,rd->td', prompt_normed_prob.astype(jnp.bfloat16), grad_out...  9.38 us
  transfers between devices with their start and end apart: 2, of which 1 were waited for; matrix products, arithmetic and copies ran while one was open for 25% of the time, Pallas kernels for 0%

commit v1 on v0

v1 whole, which is shorter than its diff:
```python
import functools
import math

import jax
import jax.numpy as jnp
from jax import lax
from jax.experimental import pallas as pl
from jax.experimental.pallas import tpu as pltpu
from jax.sharding import PartitionSpec as P

rope_base = 1000000.0
norm_eps = 1e-06
spread_eps = 1e-06
LOG2E = math.log2(math.e)
bf16, f32 = jnp.bfloat16, jnp.float32


def dot(a, b, ca, cb):
    return lax.dot_general(a, b, (((ca,), (cb,)), ((), ())), preferred_element_type=f32)


def helpers():
    i = lax.broadcasted_iota(jnp.int32, (128, 128), 0)
    j = lax.broadcasted_iota(jnp.int32, (128, 128), 1)
    swap = ((i == j + 64) | (j == i + 64)).astype(bf16)
    mean = jnp.full((128, 128), 1.0 / 128, bf16)
    return swap, mean


def unit(raw, mean):
    v = raw.astype(f32)
    return lax.rsqrt(dot((v * v).astype(bf16), mean, 1, 0) + norm_eps)


def prepare(raw, gain, rgain, cos, sin, swap, mean):
    inv = unit(raw, mean)
    u = raw.astype(f32) * inv * gain
    ru = dot(raw, swap, 1, 0) * inv * rgain
    return u * cos + ru * sin, ru * cos - u * sin


def pull(raw, g, rg, gain, cos, sin, mean):
    v = raw.astype(f32)
    inv = unit(raw, mean)
    gw = (g * cos - rg * sin) * gain
    return inv * (gw - v * (inv * inv * dot((gw * v).astype(bf16), mean, 1, 0)))


def attend(
    assign, q_ref, up_ref, ga_ref, gb_ref, wk_ref, wv_ref, qg_ref, kg_ref, cp_ref, sp_ref, cw_ref, sw_ref,
    w_ref, adv_ref, *refs, heads, subs, plen, chips, tok, win,
):
    att_ref, dq_ref, dw_ref, own_ref, oth_ref, kp, va, dk, dv = refs[-9:]
    r, hb = pl.program_id(0), pl.program_id(1)
    root = math.sqrt(128)
    half = plen // 2
    swap, mean = helpers()
    kgain, qgain = kg_ref[...], qg_ref[...]
    rkgain, rqgain = pltpu.roll(kgain, 64, 1), pltpu.roll(qgain, 64, 1)

    @pl.when(hb == 0)
    def _():
        for i, g_ref in enumerate((ga_ref, gb_ref)):
            raw = g_ref[:, 0].reshape(half, 256)
            rows = pl.ds(i * half, half)
            k, rk = prepare(raw[:, :128], kgain, rkgain, cp_ref[rows, :], sp_ref[rows, :], swap, mean)
            kp[rows, :128] = k.astype(bf16)
            kp[rows, 128:] = rk.astype(bf16)
            va[rows, :128] = raw[:, 128:]
        k, rk = prepare(wk_ref[0], kgain, rkgain, cw_ref[0], sw_ref[0], swap, mean)
        kp[plen:, :128] = k.astype(bf16)
        kp[plen:, 128:] = rk.astype(bf16)
        va[plen:, :128] = wv_ref[0]
        va[:, 128:] = jnp.ones_like(va[:, 128:])
        dk[r] = jnp.zeros_like(dk[r])
        dv[r] = jnp.zeros_like(dv[r])

    sh = heads // subs
    cos = jnp.concatenate([cw_ref[0]] * sh, axis=0)
    sin = jnp.concatenate([sw_ref[0]] * sh, axis=0)
    rows = sh * win
    i = lax.broadcasted_iota(jnp.int32, (rows, win), 0) % win
    j = lax.broadcasted_iota(jnp.int32, (rows, win), 1)
    seen = i >= j
    S = range(subs)

    def load(ref, b):
        return jnp.concatenate([ref[0, :, (b * sh + g) * 128 : (b * sh + g + 1) * 128] for g in range(sh)], axis=0)

    def store(ref, b, x):
        for g in range(sh):
            ref[0, :, (b * sh + g) * 128 : (b * sh + g + 1) * 128] = x[g * win : (g + 1) * win]

    q = [load(q_ref, b) for b in S]
    qc = LOG2E / root
    qs = [prepare(q[b], qgain * qc, rqgain * qc, cos, sin, swap, mean)[0].astype(bf16) for b in S]
    s = [dot(qs[b], kp[:, :128], 1, 1) for b in S]
    e = [jnp.exp2(s[b]) for b in S]
    e = [jnp.concatenate([e[b][:, :plen], jnp.where(seen, e[b][:, plen:], 0.0)], axis=1).astype(bf16) for b in S]
    od = [dot(e[b], va[...], 1, 0) for b in S]
    a = []
    for b in S:
        rinv = 1.0 / od[b][:, 128:]
        o = od[b][:, :128] * rinv
        store(att_ref, b, o.astype(bf16))
        do = load(up_ref, b).astype(f32) * rinv
        a.append(jnp.concatenate([do.astype(bf16), (-(do * o)).astype(bf16)], axis=1))
    dp = [dot(a[b], va[...], 1, 1) for b in S]
    ds = [e[b] * dp[b].astype(bf16) for b in S]
    gq = [dot(ds[b], kp[...], 1, 0) for b in S]
    for b in S:
        store(dq_ref, b, pull(q[b], gq[b][:, :128], gq[b][:, 128:], qgain * (adv_ref[r] / root), cos, sin, mean).astype(bf16))
    cat = lambda x: jnp.concatenate(x, axis=0) if subs > 1 else x[0]
    dv[r] += dot(cat(a)[:, :128], cat(e), 0, 0)
    dk[r] += dot(cat(qs), cat(ds), 0, 0)

    @pl.when(hb == pl.num_programs(1) - 1)
    def _():
        ln2 = 1.0 / LOG2E
        gk = dk[r, :, plen:].T * (ln2 * adv_ref[r])
        dw_ref[0, :, :128] = pull(wk_ref[0], gk, pltpu.roll(gk, 64, 1), kgain, cw_ref[0], sw_ref[0], mean).astype(bf16)
        dw_ref[0, :, 128:] = (dv[r, :, plen:].T * adv_ref[r]).astype(bf16)

        @pl.when(r == 1)
        def _():
            for i, out in enumerate((own_ref, oth_ref)):
                cols = pl.ds(i * half, half)
                for p in range(2):
                    for c, (acc, scale) in enumerate(((dk, ln2), (dv, 1.0))):
                        m = (w_ref[p, 0] * scale) * acc[0, :, cols] + (w_ref[p, 1] * scale) * acc[1, :, cols]
                        out[:, p, :, c * 128 : (c + 1) * 128] = m.astype(bf16).T.reshape(chips, tok, 128)


def call(h, heads, subs, assign, q, up, ga, gb, wc, qgain, kgain, cp, sp, cw, sw, w, adv, *before):
    rolls, win, width = q.shape
    chips, prompts, tok, _ = ga.shape
    kvh = wc.shape[2] // 256
    share = width // (128 * kvh)
    plen = 2 * chips * tok
    steps = share // heads
    t = plen + win
    smem = pl.BlockSpec(memory_space=pltpu.SMEM)
    anywhere = pl.BlockSpec(memory_space=pl.ANY)
    vec = pl.BlockSpec((1, 128), lambda r, b, a: (0, 0))
    gspec = pl.BlockSpec((chips, 1, tok, 256), lambda r, b, a: (0, a[r], 0, 0))
    qspec = pl.BlockSpec((1, win, heads * 128), lambda r, b, a: (r, 0, h * steps + b))
    pspec = pl.BlockSpec((plen, 128), lambda r, b, a: (0, 0))
    wspec = pl.BlockSpec((1, win, 128), lambda r, b, a: (r, 0, 0))
    pieces = pl.BlockSpec((chips, prompts, tok, 256), lambda r, b, a: (0, 0, 0, 0))
    return pl.pallas_call(
        functools.partial(attend, heads=heads, subs=subs, plen=plen, chips=chips, tok=tok, win=win),
        grid_spec=pltpu.PrefetchScalarGridSpec(
            num_scalar_prefetch=1,
            grid=(rolls, steps),
            in_specs=[
                qspec,
                qspec,
                gspec,
                gspec,
                pl.BlockSpec((1, win, 128), lambda r, b, a: (r, 0, h)),
                pl.BlockSpec((1, win, 128), lambda r, b, a: (r, 0, kvh + h)),
                vec,
                vec,
                pspec,
                pspec,
                wspec,
                wspec,
                smem,
                smem,
            ]
            + [anywhere] * len(before),
            out_specs=[qspec, qspec, pl.BlockSpec((1, win, 256), lambda r, b, a: (r, 0, 0)), pieces, pieces],
            scratch_shapes=[
                pltpu.VMEM((t, 256), bf16),
                pltpu.VMEM((t, 256), bf16),
                pltpu.VMEM((rolls, 128, t), f32),
                pltpu.VMEM((rolls, 128, t), f32),
            ],
        ),
        out_shape=[
            jax.ShapeDtypeStruct(q.shape, bf16),
            jax.ShapeDtypeStruct(q.shape, bf16),
            jax.ShapeDtypeStruct((rolls, win, 256), bf16),
            jax.ShapeDtypeStruct((chips, prompts, tok, 256), bf16),
            jax.ShapeDtypeStruct((chips, prompts, tok, 256), bf16),
        ],
        input_output_aliases={15: 0, 16: 1} if before else {},
        compiler_params=pltpu.CompilerParams(vmem_limit_bytes=56 * 1024 * 1024),
        cost_estimate=pl.CostEstimate(
            flops=12 * rolls * share * win * t * 128, bytes_accessed=8 * rolls * share * win * 128, transcendentals=rolls * share * win * t
        ),
        name="attend",
    )(assign, q, up, ga, gb, wc, wc, qgain, kgain, cp, sp, cw, sw, w, adv, *before)


def tables(positions):
    frequency = rope_base ** (-(jnp.arange(64, dtype=f32) * 2.0) / 128)
    angles = positions.astype(f32)[..., None] * frequency
    c, s = jnp.cos(angles), jnp.sin(angles)
    return jnp.concatenate([c, c], axis=-1), jnp.concatenate([-s, s], axis=-1)


def local(prompt_cache, key_gain, query_gain, window_cache, queries, upstream, rewards, assign, offsets):
    groups, members = lax.axis_size("prompt"), lax.axis_size("roll")
    rolls, win, width = queries.shape
    prompts, tok, _ = prompt_cache.shape
    kvh = window_cache.shape[2] // 256
    chips = members // 2
    devices = groups * members
    mine = lax.axis_index("roll")
    core = mine % 2
    same_core = [[2 * c + k for c in range(chips)] for k in range(2)]
    other_core = [(m, m ^ 1) for m in range(members)]

    def flip(x):
        return lax.ppermute(x, "roll", other_core)

    def exchange(x):
        return lax.all_to_all(x, "roll", 0, 0, tiled=True, axis_index_groups=same_core)

    sent = []
    for h in range(kvh):
        part = jnp.concatenate(
            [prompt_cache[:, :, h * 128 : (h + 1) * 128], prompt_cache[:, :, (kvh + h) * 128 : (kvh + h + 1) * 128]], axis=2
        )
        sent.append(exchange(jnp.broadcast_to(part[None], (chips,) + part.shape)))
    facts = jnp.concatenate([rewards, assign.astype(f32), jnp.zeros((128 - 2 * rolls,), f32)])
    facts = lax.all_to_all(jnp.broadcast_to(facts, (devices, 1, 128)), ("prompt", "roll"), 0, 0, tiled=True)[:, 0]
    held = [(g, flip(g)) for g in sent]

    all_rewards = facts[:, :rolls].reshape(-1)
    group = jnp.arange(devices * rolls) // (members * rolls)
    prompt_of = group * prompts + facts[:, rolls : 2 * rolls].reshape(-1).astype(jnp.int32)
    member = (prompt_of[:, None] == jnp.arange(groups * prompts)[None, :]).astype(f32)
    per_prompt = rolls * members // prompts
    means = jnp.sum(member * all_rewards[:, None], axis=0) / per_prompt
    centred = all_rewards - jnp.sum(member * means[None, :], axis=1)
    spread = jnp.sum(centred * centred) / (devices * rolls)
    here = (lax.axis_index("prompt") * members + mine) * rolls
    adv = lax.dynamic_slice(centred, (here,), (rolls,)) / jnp.sqrt(spread + spread_eps)
    w = (assign[None, :] == jnp.arange(prompts, dtype=jnp.int32)[:, None]).astype(f32) * adv[None, :]

    token = jnp.arange(tok)
    chip = jnp.arange(chips)[:, None]
    spots = jnp.stack([(chip * 2 + core) * tok + token, (chip * 2 + 1 - core) * tok + token]).reshape(-1)
    cp, sp = tables(spots)
    cw, sw = tables(2 * chips * tok + offsets[:, None] + jnp.arange(win)[None, :])
    qgain, kgain = query_gain[None], key_gain[None]

    before, window_parts, reduced = [], [], []
    for h in range(kvh):
        att, dq, dw, own, other = call(
            h, 8, 2, assign, queries, upstream, held[h][0], held[h][1], window_cache, qgain, kgain, cp, sp, cw, sw, w, adv, *before
        )
        before = [att, dq]
        window_parts.append(dw)
        merged = (own.astype(f32) + flip(other).astype(f32)).astype(bf16)
        reduced.append(jnp.sum(exchange(merged).astype(f32), axis=0))

    co, so = tables(mine * tok + token)
    raw = jnp.concatenate([prompt_cache[:, :, None, h * 128 : (h + 1) * 128] for h in range(kvh)], axis=2).astype(f32)
    g = jnp.stack([x[:, :, :128] for x in reduced], axis=2)
    co, so = co[None, :, None], so[None, :, None]
    inv = lax.rsqrt(jnp.mean(raw * raw, axis=-1, keepdims=True) + norm_eps)
    gw = (g * co - jnp.roll(g, 64, axis=-1) * so) * key_gain
    gk = inv * (gw - raw * (inv * inv * jnp.mean(gw * raw, axis=-1, keepdims=True)))
    prompt_grad = jnp.concatenate([gk.reshape(prompts, tok, kvh * 128)] + [x[:, :, 128:] for x in reduced], axis=2).astype(bf16)
    window_grad = jnp.concatenate([x[:, :, :128] for x in window_parts] + [x[:, :, 128:] for x in window_parts], axis=2)
    return att, dq, window_grad, prompt_grad


def solution(mesh):
    both = P(("prompt", "roll"))
    return jax.shard_map(
        local,
        mesh=mesh,
        in_specs=(P("prompt", "roll", None), P(), P(), both, both, both, both, both, both),
        out_specs=(both, both, both, P("prompt", "roll", None)),
        check_vma=False,
    )
```

time: 391 us -> 127 us (0.32); the launches traced: 384 us -> 126 us
  blocking collectives: 95.2 us -> 0 us
  matrix products: 92.1 us -> 0 us
  local copies, waits for them, and re-layouts: 64.5 us -> 6.08 us
  Pallas kernels: 0 us -> 43 us
  other arithmetic: 51.6 us -> 12.7 us
  starting transfers between devices: 0.08 us -> 26.1 us
  between operations: 22.9 us -> 1.78 us
  waiting for transfers between devices: 57.2 us -> 36.8 us
    psum x2 -> x0, blocking collectives: 95.2 us -> none  [the longest x1 64.1 us: local(): spread_total = lax.psum(jnp.sum(centred * centred), ('prompt', 'roll'))]
    dot_general x48 -> x0, matrix products: 92.1 us -> none  [the longest x4 18.4 us: local(): jnp.einsum('rd,td->rt', query_rows[rollout][key_head], keys_here, preferr...]
    unnamed x3 -> x0, waiting for transfers between devices: 57.2 us -> none
    pallas_call x0 -> x2, Pallas kernels: none -> 43 us  [call(): pl.pallas_call(functools.partial(attend, heads=heads, subs=subs, plen=ple...]
    all_to_all x0 -> x5, waiting for transfers between devices: none -> 36.8 us  [the longest x4 33.9 us: exchange(): lax.all_to_all(x, 'roll', 0, 0, tiled=True, axis_index_groups=same_core)]
    all_to_all x0 -> x5, starting transfers between devices: none -> 25.1 us  [the longest x4 14 us: exchange(): lax.all_to_all(x, 'roll', 0, 0, tiled=True, axis_index_groups=same_core)]
    convert_element_type x10 -> x2, local copies, waits for them, and re-layouts: 17 us -> 0.21 us  [the longest x1 0.14 us: local(): facts[:, rolls:2 * rolls].reshape(-1).astype(jnp.int32)]
    unnamed x288 -> x28, local copies, waits for them, and re-layouts: 16.6 us -> 1.64 us
  transfers between devices with their start and end apart: 2 -> 9, of which waited for: 1 -> 5; matrix products, arithmetic and copies ran while one was open for 25% -> 9% of each run, Pallas kernels for 0% -> 34%
where the time goes in v1:
time: 127 us; the launch traced here: 126 us
  Pallas kernels  43 us (34%)
  waiting for transfers between devices  36.8 us (29%)
  starting transfers between devices  26.1 us (21%)
  other arithmetic  12.7 us (10%)
  local copies, waits for them, and re-layouts  6.08 us (5%)
  between operations  1.78 us (1%)
    pallas_call x2, Pallas kernels, call(): pl.pallas_call(functools.partial(attend, heads=heads, subs=subs, plen=ple...  43 us
    all_to_all x4, waiting for transfers between devices, exchange(): lax.all_to_all(x, 'roll', 0, 0, tiled=True, axis_index_groups=same_core)  33.9 us
    all_to_all x4, starting transfers between devices, exchange(): lax.all_to_all(x, 'roll', 0, 0, tiled=True, axis_index_groups=same_core)  14 us
    all_to_all x1, starting transfers between devices, local(): lax.all_to_all(jnp.broadcast_to(facts, (devices, 1, 128)), ('prompt', 'ro...  11.1 us
    concatenate x4, other arithmetic, tables(): return (jnp.concatenate([c, c], axis=-1), jnp.concatenate([-s, s], axis=-1))  2.93 us
    all_to_all x1, waiting for transfers between devices, local(): lax.all_to_all(jnp.broadcast_to(facts, (devices, 1, 128)), ('prompt', 'ro...  2.88 us
  transfers between devices with their start and end apart: 9, of which 5 were waited for; matrix products, arithmetic and copies ran while one was open for 9% of the time, Pallas kernels for 34%

profile of v1, /device:TPU:0, one launch (start us, length us, event | category | flops | bytes accessed | tf_op | source)
XLA Modules:
  0.0 126.4 jit_solution(12232548239934875017)
XLA Ops:
  2.7 11.1 %all-to-all-start.1 = ((f32[128,1,128]{2,1,0:T(1,128)}), f32[128,1,128]{2,1,0:T(1,128)S(1)}, u32[]{:S(2)}, u32[]{:S(2)}) async-start(f32[128,1,128]{2,1,0:T(1,128)} %broadcast_in_dim.20), calls=%async_computation.1 | async-start | bytes 131072 | tf_op jit(solution)/shard_map/all_to_all | solution.py:228
  14.2 1.9 %fusion = (f32[1024,64]{1,0:T(8,128)S(1)}, f32[1024,64]{1,0:T(8,128)S(1)}, f32[1024,64]{1,0:T(8,128)S(1)}) fusion(f32[64]{0:T(128)S(1)} %multiply_power_fusion, f32[1024]{0:T(1024)S(1)} %convert_element_type.70), kind=kLoop, calls=%fused_computation.19 | loop fusion | flops 131072 | bytes 790784 | tf_op jit(solution)/shard_map/neg | solution.py:200
  16.1 1.0 pad_maximum_fusion.cp_ref
  18.2 1.0 pad_maximum_fusion.1.sp_ref
  19.2 0.8 pad_maximum_fusion.4
  20.1 2.9 %all-to-all-done.1 = f32[128,1,128]{2,1,0:T(1,128)S(1)} async-done(((f32[128,1,128]{2,1,0:T(1,128)}), f32[128,1,128]{2,1,0:T(1,128)S(1)}, u32[]{:S(2)}, u32[]{:S(2)}) %all-to-all-start.1) | async-done | bytes 65568 | tf_op jit(solution)/shard_map/all_to_all | solution.py:228
  22.9 0.8 broadcast_in_dim.21
  23.8 3.5 %all-to-all-start.2 = ((bf16[8,2,64,256]{3,2,1,0:T(8,128)(2,1)}), bf16[8,2,64,256]{3,2,1,0:T(8,128)(2,1)S(1)}, u32[]{:S(2)}, u32[]{:S(2)}) async-start(bf16[8,2,64,256]{3,2,1,0:T(8,128)(2,1)} %broadcast_in_dim.21), calls=%async_computation.2 | async-start | bytes 1048576 | tf_op jit(solution)/shard_map/all_to_all | solution.py:219
  27.8 9.2 %all-to-all-done.2.ga_ref = bf16[8,2,64,256]{3,2,1,0:T(8,128)(2,1)S(1)} async-done(((bf16[8,2,64,256]{3,2,1,0:T(8,128)(2,1)}), bf16[8,2,64,256]{3,2,1,0:T(8,128)(2,1)S(1)}, u32[]{:S(2)}, u32[]{:S(2)}) %all-to-all-start.2) | async-done | bytes 524320 | tf_op jit(solution)/shard_map/all_to_all | solution.py:219
  37.0 0.9 broadcast_in_dim.16
  38.0 3.5 %all-to-all-start = ((bf16[8,2,64,256]{3,2,1,0:T(8,128)(2,1)}), bf16[8,2,64,256]{3,2,1,0:T(8,128)(2,1)S(1)}, u32[]{:S(2)}, u32[]{:S(2)}) async-start(bf16[8,2,64,256]{3,2,1,0:T(8,128)(2,1)} %broadcast_in_dim.16), calls=%async_computation | async-start | bytes 1048576 | tf_op jit(solution)/shard_map/all_to_all | solution.py:219
  43.8 6.9 %all-to-all-done.ga_ref = bf16[8,2,64,256]{3,2,1,0:T(8,128)(2,1)S(1)} async-done(((bf16[8,2,64,256]{3,2,1,0:T(8,128)(2,1)}), bf16[8,2,64,256]{3,2,1,0:T(8,128)(2,1)S(1)}, u32[]{:S(2)}, u32[]{:S(2)}) %all-to-all-start) | async-done | bytes 524320 | tf_op jit(solution)/shard_map/all_to_all | solution.py:219
  50.7 0.8 copy-done.10
  51.5 21.4 %attend.2 = (bf16[2,128,4096]{2,1,0:T(8,128)(2,1)}, bf16[2,128,4096]{2,1,0:T(8,128)(2,1)}, bf16[2,128,256]{2,1,0:T(8,128)(2,1)}, bf16[8,2,64,256]{3,2,1,0:T(8,128)(2,1)}, bf16[8,2,64,256]{3,2,1,0:T(8,128)(2,1)}) custom-call(s32[2]{0:T(128)} %assign.3, bf16[2,128,4096]{2,1,0:T(8,128)(2,1)} %q_ref.3, bf16[2,128,4096]{2,1,0:T(8,128)(2,1)} %up_ref.3, ...), custom_call_target="tpu_custom_call" | custom-call | flops 7247757312 | bytes 4194304 | tf_op jit(solution)/shard_map/attend/pallas_call | solution.py:150
  73.7 0.8 copy-done.11
  74.5 21.5 %attend.3 = (bf16[2,128,4096]{2,1,0:T(8,128)(2,1)}, bf16[2,128,4096]{2,1,0:T(8,128)(2,1)}, bf16[2,128,256]{2,1,0:T(8,128)(2,1)}, bf16[8,2,64,256]{3,2,1,0:T(8,128)(2,1)}, bf16[8,2,64,256]{3,2,1,0:T(8,128)(2,1)}) custom-call(s32[2]{0:T(128)} %assign.3, bf16[2,128,4096]{2,1,0:T(8,128)(2,1)} %q_ref.3, ...), custom_call_target="tpu_custom_call", output_to_operand_aliasing={{0}: (15, {}), {1}: (16, {})} | custom-call | flops 7247757312 | bytes 4194304 | tf_op jit(solution)/shard_map/attend/pallas_call | solution.py:150
  96.2 1.0 fusion.17
  97.1 1.0 add_convert_fusion.1
  98.1 3.5 %all-to-all-start.3 = ((bf16[8,2,64,256]{3,2,1,0:T(8,128)(2,1)}), bf16[8,2,64,256]{3,2,1,0:T(8,128)(2,1)S(1)}, u32[]{:S(2)}, u32[]{:S(2)}) async-start(bf16[8,2,64,256]{3,2,1,0:T(8,128)(2,1)} %add_convert_fusion.1), calls=%async_computation.3 | async-start | bytes 1048576 | tf_op jit(solution)/shard_map/all_to_all | solution.py:219
  101.7 0.9 add_convert_fusion
  102.6 9.2 %all-to-all-done.3 = bf16[8,2,64,256]{3,2,1,0:T(8,128)(2,1)S(1)} async-done(((bf16[8,2,64,256]{3,2,1,0:T(8,128)(2,1)}), bf16[8,2,64,256]{3,2,1,0:T(8,128)(2,1)S(1)}, u32[]{:S(2)}, u32[]{:S(2)}) %all-to-all-start.3) | async-done | bytes 524320 | tf_op jit(solution)/shard_map/all_to_all | solution.py:219
  111.8 3.5 %all-to-all-start.4 = ((bf16[8,2,64,256]{3,2,1,0:T(8,128)(2,1)}), bf16[8,2,64,256]{3,2,1,0:T(8,128)(2,1)S(1)}, u32[]{:S(2)}, u32[]{:S(2)}) async-start(bf16[8,2,64,256]{3,2,1,0:T(8,128)(2,1)} %add_convert_fusion), calls=%async_computation.4 | async-start | bytes 1048576 | tf_op jit(solution)/shard_map/all_to_all | solution.py:219
  115.3 0.7 pad_maximum_fusion.2
  116.2 8.6 %all-to-all-done.4 = bf16[8,2,64,256]{3,2,1,0:T(8,128)(2,1)S(1)} async-done(((bf16[8,2,64,256]{3,2,1,0:T(8,128)(2,1)}), bf16[8,2,64,256]{3,2,1,0:T(8,128)(2,1)S(1)}, u32[]{:S(2)}, u32[]{:S(2)}) %all-to-all-start.4) | async-done | bytes 524320 | tf_op jit(solution)/shard_map/all_to_all | solution.py:219
  (83 shorter events, 8.1 us)
Async XLA Ops:
  0.6 16.5 %copy-start.12 = (s32[2]{0:T(128)S(1)}, s32[2]{0:T(128)}, u32[]{:S(2)}) copy-start(s32[2]{0:T(128)} %param.17) | copy-start | bytes 28
  0.6 17.1 %copy-start.4 = (bf16[2,64,512]{2,1,0:T(8,128)(2,1)S(1)}, bf16[2,64,512]{2,1,0:T(8,128)(2,1)}, u32[]{:S(2)}) copy-start(bf16[2,64,512]{2,1,0:T(8,128)(2,1)} %param.9) | copy-start | bytes 393220
  2.7 20.2 %all-to-all-start.1 = ((f32[128,1,128]{2,1,0:T(1,128)}), f32[128,1,128]{2,1,0:T(1,128)S(1)}, u32[]{:S(2)}, u32[]{:S(2)}) async-start(f32[128,1,128]{2,1,0:T(1,128)} %broadcast_in_dim.20), calls=%async_computation.1 | async-start | bytes 131072 | tf_op jit(solution)/shard_map/all_to_all | solution.py:228
  13.9 4.3 %copy-start.8 = (f32[128]{0:T(128)S(1)}, f32[128]{0:T(128)}, u32[]{:S(2)}) copy-start(f32[128]{0:T(128)} %param.10) | copy-start | bytes 1540
  20.0 23.1 %copy-start.7 = (s32[2]{0:T(128)S(1)}, s32[2]{0:T(128)}, u32[]{:S(2)}) copy-start(s32[2]{0:T(128)} %assign.3) | copy-start | bytes 28
  23.8 13.2 %all-to-all-start.2 = ((bf16[8,2,64,256]{3,2,1,0:T(8,128)(2,1)}), bf16[8,2,64,256]{3,2,1,0:T(8,128)(2,1)S(1)}, u32[]{:S(2)}, u32[]{:S(2)}) async-start(bf16[8,2,64,256]{3,2,1,0:T(8,128)(2,1)} %broadcast_in_dim.21), calls=%async_computation.2 | async-start | bytes 1048576 | tf_op jit(solution)/shard_map/all_to_all | solution.py:219
  37.0 13.7 %copy-start.2 = (bf16[8,2,64,256]{3,2,1,0:T(8,128)(2,1)}, bf16[8,2,64,256]{3,2,1,0:T(8,128)(2,1)S(1)}, u32[]{:S(2)}) copy-start(bf16[8,2,64,256]{3,2,1,0:T(8,128)(2,1)S(1)} %all-to-all-done.2.ga_ref) | copy-start | bytes 1572868
  38.0 12.7 %all-to-all-start = ((bf16[8,2,64,256]{3,2,1,0:T(8,128)(2,1)}), bf16[8,2,64,256]{3,2,1,0:T(8,128)(2,1)S(1)}, u32[]{:S(2)}, u32[]{:S(2)}) async-start(bf16[8,2,64,256]{3,2,1,0:T(8,128)(2,1)} %broadcast_in_dim.16), calls=%async_computation | async-start | bytes 1048576 | tf_op jit(solution)/shard_map/all_to_all | solution.py:219
  41.5 9.2 %collective-permute-start.1 = (bf16[8,2,64,256]{3,2,1,0:T(8,128)(2,1)S(1)}, bf16[8,2,64,256]{3,2,1,0:T(8,128)(2,1)S(1)}, u32[]{:S(2)}, u32[]{:S(2)}) collective-permute-start(bf16[8,2,64,256]{3,2,1,0:T(8,128)(2,1)S(1)} %all-to-all-done.2.ga_ref), channel_id=1, source_target_pairs={{0,1},{1,0},{2,3},{3,2},{4,5},{5,4},{6,7},{7,6},{8,9},{9,8},{10,11... | collective-permute-start | bytes 1572872 | tf_op jit(solution)/shard_map/ppermute | solution.py:216
  43.2 7.5 %copy-start.6 = (f32[2]{0:T(128)}, f32[2]{0:T(128)S(1)}, u32[]{:S(2)}) copy-start(f32[2]{0:T(128)S(1)} %dynamic-slice_divide_fusion.adv_ref) | copy-start | bytes 28
  50.7 22.3 %copy-start.3 = (bf16[8,2,64,256]{3,2,1,0:T(8,128)(2,1)}, bf16[8,2,64,256]{3,2,1,0:T(8,128)(2,1)S(1)}, u32[]{:S(2)}) copy-start(bf16[8,2,64,256]{3,2,1,0:T(8,128)(2,1)S(1)} %all-to-all-done.ga_ref) | copy-start | bytes 1572868
  50.7 23.0 %collective-permute-start = (bf16[8,2,64,256]{3,2,1,0:T(8,128)(2,1)S(1)}, bf16[8,2,64,256]{3,2,1,0:T(8,128)(2,1)S(1)}, u32[]{:S(2)}, u32[]{:S(2)}) collective-permute-start(bf16[8,2,64,256]{3,2,1,0:T(8,128)(2,1)S(1)} %all-to-all-done.ga_ref), channel_id=1, source_target_pairs={{0,1},{1,0},{2,3},{3,2},{4,5},{5,4},{6,7},{7,6},{8,9},{9,8},{10,11... | collective-permute-start | bytes 1572872 | tf_op jit(solution)/shard_map/ppermute | solution.py:216
  50.7 0.8 copy-start.10
  72.9 24.2 %collective-permute-start.2 = (bf16[8,2,64,256]{3,2,1,0:T(8,128)(2,1)}, bf16[8,2,64,256]{3,2,1,0:T(8,128)(2,1)S(1)}, u32[]{:S(2)}, u32[]{:S(2)}) collective-permute-start(bf16[8,2,64,256]{3,2,1,0:T(8,128)(2,1)} %get-tuple-element.21), channel_id=1, source_target_pairs={{0,1},{1,0},{2,3},{3,2},{4,5},{5,4},{6,7},{7,6},{8,9},{9,8},{10,11... | collective-permute-start | bytes 1572872 | tf_op jit(solution)/shard_map/ppermute | solution.py:216
  73.7 0.8 copy-start.11
  74.5 22.7 %copy-start.1 = (bf16[8,2,64,256]{3,2,1,0:T(8,128)(2,1)S(1)}, bf16[8,2,64,256]{3,2,1,0:T(8,128)(2,1)}, u32[]{:S(2)}) copy-start(bf16[8,2,64,256]{3,2,1,0:T(8,128)(2,1)} %get-tuple-element.20) | copy-start | bytes 1572868
  96.0 5.6 %copy-start.5 = (bf16[2,128,256]{2,1,0:T(8,128)(2,1)S(1)}, bf16[2,128,256]{2,1,0:T(8,128)(2,1)}, u32[]{:S(2)}) copy-start(bf16[2,128,256]{2,1,0:T(8,128)(2,1)} %get-tuple-element.18) | copy-start | bytes 393220
  96.0 5.6 %copy-start = (bf16[8,2,64,256]{3,2,1,0:T(8,128)(2,1)S(1)}, bf16[8,2,64,256]{3,2,1,0:T(8,128)(2,1)}, u32[]{:S(2)}) copy-start(bf16[8,2,64,256]{3,2,1,0:T(8,128)(2,1)} %get-tuple-element.22) | copy-start | bytes 1572868
  96.0 5.6 %collective-permute-start.3 = (bf16[8,2,64,256]{3,2,1,0:T(8,128)(2,1)}, bf16[8,2,64,256]{3,2,1,0:T(8,128)(2,1)S(1)}, u32[]{:S(2)}, u32[]{:S(2)}) collective-permute-start(bf16[8,2,64,256]{3,2,1,0:T(8,128)(2,1)} %get-tuple-element.23), channel_id=1, source_target_pairs={{0,1},{1,0},{2,3},{3,2},{4,5},{5,4},{6,7},{7,6},{8,9},{9,8},{10,11... | collective-permute-start | bytes 1572872 | tf_op jit(solution)/shard_map/ppermute | solution.py:216
  98.1 13.7 %all-to-all-start.3 = ((bf16[8,2,64,256]{3,2,1,0:T(8,128)(2,1)}), bf16[8,2,64,256]{3,2,1,0:T(8,128)(2,1)S(1)}, u32[]{:S(2)}, u32[]{:S(2)}) async-start(bf16[8,2,64,256]{3,2,1,0:T(8,128)(2,1)} %add_convert_fusion.1), calls=%async_computation.3 | async-start | bytes 1048576 | tf_op jit(solution)/shard_map/all_to_all | solution.py:219
  102.6 22.3 %copy-start.9 = (f32[128]{0:T(128)S(1)}, f32[128]{0:T(128)}, u32[]{:S(2)}) copy-start(f32[128]{0:T(128)} %param.10) | copy-start | bytes 1540
  111.8 12.9 %all-to-all-start.4 = ((bf16[8,2,64,256]{3,2,1,0:T(8,128)(2,1)}), bf16[8,2,64,256]{3,2,1,0:T(8,128)(2,1)S(1)}, u32[]{:S(2)}, u32[]{:S(2)}) async-start(bf16[8,2,64,256]{3,2,1,0:T(8,128)(2,1)} %add_convert_fusion), calls=%async_computation.4 | async-start | bytes 1048576 | tf_op jit(solution)/shard_map/all_to_all | solution.py:219

commit v2 on v1

v2 whole, which is shorter than its diff:
```python
import functools
import math

import jax
import jax.numpy as jnp
import numpy as np
from jax import lax
from jax.experimental import pallas as pl
from jax.experimental.pallas import tpu as pltpu
from jax.sharding import PartitionSpec as P

rope_base = 1000000.0
norm_eps = 1e-06
spread_eps = 1e-06
LOG2E = math.log2(math.e)
bf16, f32 = jnp.bfloat16, jnp.float32
LIMIT = 56 * 1024 * 1024
frequency = np.tile(rope_base ** (-np.arange(64) * 2.0 / 128), 2).astype(np.float32)[None]


def dot(a, b, ca, cb):
    return lax.dot_general(a, b, (((ca,), (cb,)), ((), ())), preferred_element_type=f32)


def helpers():
    i = lax.broadcasted_iota(jnp.int32, (128, 128), 0)
    j = lax.broadcasted_iota(jnp.int32, (128, 128), 1)
    swap = ((i == j + 64) | (j == i + 64)).astype(bf16)
    mean = jnp.full((128, 128), 1.0 / 128, bf16)
    return swap, mean


def unit(raw, mean):
    v = raw.astype(f32)
    return lax.rsqrt(dot((v * v).astype(bf16), mean, 1, 0) + norm_eps)


def prepare(raw, gain, cos, sin, swap, mean):
    inv = unit(raw, mean)
    u = raw.astype(f32) * inv * gain
    ru = dot(raw, swap, 1, 0) * inv * pltpu.roll(gain, 64, 1)
    return u * cos + ru * sin, ru * cos - u * sin


def pull(raw, g, rg, gain, cos, sin, mean):
    v = raw.astype(f32)
    inv = unit(raw, mean)
    gw = (g * cos - rg * sin) * gain
    return inv * (gw - v * (inv * inv * dot((gw * v).astype(bf16), mean, 1, 0)))


def turns(start, count, freq):
    positions = (start + lax.broadcasted_iota(jnp.int32, (count, 128), 0)).astype(f32)
    angles = positions * freq
    upper = lax.broadcasted_iota(jnp.int32, (count, 128), 1) >= 64
    sine = jnp.sin(angles)
    return jnp.cos(angles), jnp.where(upper, sine, -sine)


def ready(q_ref, gain_ref, freq_ref, off_ref, qs_ref, cw_ref, sw_ref, *, heads, plen):
    swap, mean = helpers()
    gain = gain_ref[...] * (LOG2E / math.sqrt(128))
    win = cw_ref.shape[1]
    cw, sw = turns(plen + off_ref[pl.program_id(0)], win, freq_ref[...])
    cw_ref[0] = cw
    sw_ref[0] = sw
    cos, sin = (jnp.concatenate([x] * heads, axis=0) for x in (cw, sw))
    q = jnp.concatenate([q_ref[0, :, g * 128 : (g + 1) * 128] for g in range(heads)], axis=0)
    qs_ref[0] = prepare(q, gain, cos, sin, swap, mean)[0].astype(bf16).reshape(heads, win, 128)


def attend(
    scalar, qs_ref, q_ref, up_ref, ga_ref, gb_ref, fa_ref, fb_ref, wk_ref, wv_ref, qg_ref, kg_ref, cw_ref, sw_ref, rw_ref, *refs,
    heads, subs, tc, merge, tok, win
):
    n_out = 4 + (1 if merge else 2)
    att_ref, dq_ref, dwin_ref, stat_ref, *outs = refs[-6 - n_out : -6]
    kp, va, dk, dv, e_ref, ds_ref = refs[-6:]
    r, hb = pl.program_id(0), pl.program_id(1)
    core = scalar[2]
    chips = ga_ref.shape[0]
    half = chips * tok
    plen = 2 * half
    t = plen + win
    root = math.sqrt(128)
    kgain = kg_ref[...]
    swap, mean = helpers()

    @pl.when(hb == 0)
    def _():
        for i, g_ref in enumerate((ga_ref, gb_ref)):
            raw = g_ref[...].reshape(half, 256)
            rows = pl.ds(i * half, half)
            kp[rows, :128] = raw[:, :128]
            kp[rows, 128:] = dot(raw[:, :128], swap, 1, 0).astype(bf16)
            va[rows, :128] = raw[:, 128:]
        k, rk = prepare(wk_ref[0], kgain, cw_ref[0], sw_ref[0], swap, mean)
        kp[plen:, :128] = k.astype(bf16)
        kp[plen:, 128:] = rk.astype(bf16)
        va[plen:, :128] = wv_ref[0]
        va[:, 128:] = jnp.ones_like(va[:, 128:])
        dk[r] = jnp.zeros_like(dk[r])
        dv[r] = jnp.zeros_like(dv[r])

    sh = heads // subs
    rows = sh * win
    i = lax.broadcasted_iota(jnp.int32, (rows, win), 0) % win
    j = lax.broadcasted_iota(jnp.int32, (rows, win), 1)
    seen = i >= j
    S = range(subs)
    chunks = [slice(c, min(c + tc, plen)) for c in range(0, plen, tc)] + [slice(plen, t)]
    block = [slice(b * rows, (b + 1) * rows) for b in S]
    qs = [qs_ref[0, b * sh : (b + 1) * sh].reshape(rows, 128) for b in S]
    for b in S:
        for c in chunks:
            e = jnp.exp2(dot(qs[b], kp[c, :128], 1, 1))
            if c.start == plen:
                e = jnp.where(seen, e, 0.0)
            e_ref[block[b], c] = e.astype(bf16)
    od = [dot(e_ref[block[b]], va[...], 1, 0) for b in S]
    a = []
    for b in S:
        rinv = 1.0 / od[b][:, 128:]
        o = od[b][:, :128] * rinv
        ob = o.astype(bf16)
        up = []
        for g in range(sh):
            cols = slice((b * sh + g) * 128, (b * sh + g + 1) * 128)
            att_ref[0, :, cols] = ob[g * win : (g + 1) * win]
            up.append(up_ref[0, :, cols])
        do = jnp.concatenate(up, axis=0).astype(f32) * rinv
        a.append(jnp.concatenate([do.astype(bf16), (-(do * o)).astype(bf16)], axis=1))
    for b in S:
        for c in chunks:
            ds_ref[block[b], c] = e_ref[block[b], c] * dot(a[b], va[c], 1, 1).astype(bf16)
    gq = [dot(ds_ref[block[b]], kp[...], 1, 0) for b in S]
    cos, sin = (jnp.concatenate([x[0]] * sh, axis=0) for x in (cw_ref, sw_ref))
    for b in S:
        q = jnp.concatenate([q_ref[0, :, (b * sh + g) * 128 : (b * sh + g + 1) * 128] for g in range(sh)], axis=0)
        dq = pull(q, gq[b][:, :128], gq[b][:, 128:], qg_ref[...] * (1.0 / root), cos, sin, mean).astype(bf16)
        for g in range(sh):
            dq_ref[0, :, (b * sh + g) * 128 : (b * sh + g + 1) * 128] = dq[g * win : (g + 1) * win]
    cat = lambda x: jnp.concatenate(x, axis=0) if subs > 1 else x[0]
    dv[r] += dot(cat(a)[:, :128], e_ref[...], 0, 0)
    dk[r] += dot(cat(qs), ds_ref[...], 0, 0)

    @pl.when(hb == pl.num_programs(1) - 1)
    def _():
        ln2 = 1.0 / LOG2E
        gk = dk[r, :, plen:].T * ln2
        dwin_ref[0, :, :128] = pull(wk_ref[0], gk, pltpu.roll(gk, 64, 1), kgain, cw_ref[0], sw_ref[0], mean)
        dwin_ref[0, :, 128:] = dv[r, :, plen:].T

        @pl.when(r == 1)
        def _():
            f = jnp.concatenate([fa_ref[:, 0], fb_ref[:, 0]], axis=0).astype(f32)
            reward = [f[:, 3 * n : 3 * n + 1] + f[:, 3 * n + 1 : 3 * n + 2] + f[:, 3 * n + 2 : 3 * n + 3] for n in range(2)]
            place = [f[:, 6 + n : 7 + n] for n in range(2)]
            per_prompt = f.shape[0]
            means = [
                sum(jnp.sum(jnp.where(place[n] == p, reward[n], 0.0), axis=0, keepdims=True) for n in range(2)) / per_prompt
                for p in range(2)
            ]
            spread = sum(
                jnp.sum((reward[n] - jnp.where(place[n] == 0, means[0], means[1])) ** 2, axis=0, keepdims=True) for n in range(2)
            )
            centred = [rw_ref[n] - jnp.where(scalar[n] == 0, means[0], means[1]) for n in range(2)]
            lane = lax.broadcasted_iota(jnp.int32, stat_ref.shape, 1)
            stat_ref[...] = jnp.where(lane == 0, spread, jnp.where(lane == 1, centred[0], centred[1]))
            for i in range(2):
                cols = pl.ds(i * half, half)
                for p in range(2):
                    for c, (acc, scale) in enumerate(((dk, ln2), (dv, 1.0))):
                        w = [jnp.where(scalar[n] == p, centred[n], 0.0) * scale for n in range(2)]
                        m = (w[0] * acc[0, :, cols] + w[1] * acc[1, :, cols]).astype(bf16).T.reshape(chips, tok, 128)
                        if merge:
                            outs[0][:, lax.rem(core + i, 2), p, :, c * 128 : (c + 1) * 128] = m
                        else:
                            outs[i][:, p, :, c * 128 : (c + 1) * 128] = m


def call(h, heads, subs, tc, merge, scalar, qs, q, up, ga, gb, fa, fb, wc, qgain, kgain, cw, sw, rewards, tok, prompts, *before):
    rolls, win, width = up.shape
    chips = ga.shape[0]
    kvh = wc.shape[2] // 256
    share = width // (128 * kvh)
    half = chips * tok
    plen = 2 * half
    steps = share // heads
    t = plen + win
    smem = pl.BlockSpec(memory_space=pltpu.SMEM)
    anywhere = pl.BlockSpec(memory_space=pl.ANY)
    if ga.ndim == 3:
        gspecs = [pl.BlockSpec((chips, tok, 256), lambda r, b, a: (0, a[r], 0))] * 2
    else:
        gspecs = [
            pl.BlockSpec((chips, 1, 1, tok, 256), lambda r, b, a: (0, a[2], a[r], 0, 0)),
            pl.BlockSpec((chips, 1, 1, tok, 256), lambda r, b, a: (0, 1 - a[2], a[r], 0, 0)),
        ]
    fspec = pl.BlockSpec((chips, 16, 256), lambda r, b, a: (0, prompts * tok // 16, 0))
    ospec = pl.BlockSpec((1, win, heads * 128), lambda r, b, a: (r, 0, h * steps + b))
    vec = pl.BlockSpec((1, 128), lambda r, b, a: (0, 0))
    wspec = pl.BlockSpec((1, win, 128), lambda r, b, a: (r, 0, 0))
    piece = (chips, 2, prompts, tok, 256) if merge else (chips, prompts, tok, 256)
    pieces = pl.BlockSpec(piece, lambda r, b, a: (0,) * len(piece))
    return pl.pallas_call(
        functools.partial(attend, heads=heads, subs=subs, tc=tc, merge=merge, tok=tok, win=win),
        grid_spec=pltpu.PrefetchScalarGridSpec(
            num_scalar_prefetch=1,
            grid=(rolls, steps),
            in_specs=[
                pl.BlockSpec((1, heads, win, 128), lambda r, b, a: (r, h * steps + b, 0, 0)),
                ospec,
                ospec,
                *gspecs,
                fspec,
                fspec,
                pl.BlockSpec((1, win, 128), lambda r, b, a: (r, 0, h)),
                pl.BlockSpec((1, win, 128), lambda r, b, a: (r, 0, kvh + h)),
                vec,
                vec,
                wspec,
                wspec,
                smem,
            ]
            + [anywhere] * len(before),
            out_specs=[
                ospec,
                ospec,
                pl.BlockSpec((1, win, 256), lambda r, b, a: (r, 0, 0)),
                pl.BlockSpec((8, 128), lambda r, b, a: (0, 0)),
            ]
            + [pieces] * (1 if merge else 2),
            scratch_shapes=[
                pltpu.VMEM((t, 256), bf16),
                pltpu.VMEM((t, 256), bf16),
                pltpu.VMEM((rolls, 128, t), f32),
                pltpu.VMEM((rolls, 128, t), f32),
                pltpu.VMEM((heads * win, t), bf16),
                pltpu.VMEM((heads * win, t), bf16),
            ],
        ),
        out_shape=[
            jax.ShapeDtypeStruct(up.shape, bf16),
            jax.ShapeDtypeStruct(up.shape, bf16),
            jax.ShapeDtypeStruct((rolls, win, 256), f32),
            jax.ShapeDtypeStruct((8, 128), f32),
        ]
        + [jax.ShapeDtypeStruct(piece, bf16)] * (1 if merge else 2),
        input_output_aliases={15: 0, 16: 1} if before else {},
        compiler_params=pltpu.CompilerParams(vmem_limit_bytes=LIMIT),
        cost_estimate=pl.CostEstimate(
            flops=36 * rolls * share * win * t * 128, bytes_accessed=10 * rolls * share * win * 128, transcendentals=rolls * share * win * t
        ),
        name="attend",
    )(scalar, qs, q, up, ga, gb, fa, fb, wc, wc, qgain, kgain, cw, sw, rewards, *before)


def make_ready(q, gain, offsets, plen):
    rolls, win, width = q.shape
    heads = width // 128
    wspec = pl.BlockSpec((1, win, 128), lambda r: (r, 0, 0))
    vec = pl.BlockSpec((1, 128), lambda r: (0, 0))
    return pl.pallas_call(
        functools.partial(ready, heads=heads, plen=plen),
        grid=(rolls,),
        in_specs=[pl.BlockSpec((1, win, width), lambda r: (r, 0, 0)), vec, vec, pl.BlockSpec(memory_space=pltpu.SMEM)],
        out_specs=[pl.BlockSpec((1, heads, win, 128), lambda r: (r, 0, 0, 0)), wspec, wspec],
        out_shape=[jax.ShapeDtypeStruct((rolls, heads, win, 128), bf16)] + [jax.ShapeDtypeStruct((rolls, win, 128), f32)] * 2,
        compiler_params=pltpu.CompilerParams(vmem_limit_bytes=LIMIT),
        name="ready",
    )(q, gain, frequency, offsets)


def pack(cache_ref, reward_ref, assign_ref, kg_ref, freq_ref, mine_ref, first_ref, second_ref):
    prompts, tok, width = cache_ref.shape
    kvh = width // 256
    lane = lax.broadcasted_iota(jnp.int32, (16, 256), 1)
    facts = jnp.zeros((16, 256), f32)
    for n in range(2):
        rest = jnp.full((16, 256), reward_ref[n], f32)
        for k in range(3):
            piece = rest.astype(bf16).astype(f32)
            facts = jnp.where(lane == 3 * n + k, piece, facts)
            rest = rest - piece
        facts = jnp.where(lane == 6 + n, assign_ref[n].astype(f32), facts)
    swap, mean = helpers()
    cos, sin = turns(mine_ref[0] * tok, tok, freq_ref[...])
    order = [(p, h) for p in range(prompts) for h in range(kvh)]
    raw = jnp.concatenate([cache_ref[p, :, h * 128 : (h + 1) * 128] for p, h in order], axis=0)
    cos, sin = (jnp.concatenate([x] * len(order), axis=0) for x in (cos, sin))
    keys = prepare(raw, kg_ref[...], cos, sin, swap, mean)[0].astype(bf16)
    for n, (p, h) in enumerate(order):
        key, value = keys[n * tok : (n + 1) * tok], cache_ref[p, :, (kvh + h) * 128 : (kvh + h + 1) * 128]
        if h == 0:
            for c in range(first_ref.shape[0]):
                first_ref[c, p * tok : (p + 1) * tok, :128] = key
                first_ref[c, p * tok : (p + 1) * tok, 128:] = value
        else:
            second_ref[p, :, :128] = key
            second_ref[p, :, 128:] = value
    for c in range(first_ref.shape[0]):
        first_ref[c, prompts * tok :] = facts.astype(bf16)


def make_pack(cache, rewards, assign, kgain, mine, chips):
    prompts, tok, _ = cache.shape
    smem, vmem = pl.BlockSpec(memory_space=pltpu.SMEM), pl.BlockSpec(memory_space=pltpu.VMEM)
    return pl.pallas_call(
        pack,
        in_specs=[vmem, smem, smem, vmem, vmem, smem],
        out_specs=[vmem, vmem],
        out_shape=[jax.ShapeDtypeStruct((chips, prompts * tok + 16, 256), bf16), jax.ShapeDtypeStruct((prompts, tok, 256), bf16)],
        name="pack",
    )(cache, rewards, assign, kgain, frequency, mine)


def global_scale(sums_ref, count):
    return 1.0 / jnp.sqrt(sums_ref[0:1, 0:1] / count + spread_eps)


def rescale(dq_ref, dw0_ref, dw1_ref, sums_ref, stat_ref, dq_out, dw_out, *, count):
    r = pl.program_id(0)
    adv = jnp.where(r == 0, stat_ref[0:1, 1:2], stat_ref[0:1, 2:3]) * global_scale(sums_ref, count)
    dq_out[...] = (dq_ref[...].astype(f32) * adv).astype(bf16)
    for n, part in enumerate((dw0_ref, dw1_ref)):
        for c in range(2):
            dw_out[0, :, (2 * c + n) * 128 : (2 * c + n + 1) * 128] = (part[0, :, c * 128 : (c + 1) * 128] * adv).astype(bf16)


def make_rescale(dq, dw0, dw1, sums, stat, count):
    rolls, win, width = dq.shape
    half = pl.BlockSpec((1, win, 256), lambda r, b: (r, 0, 0))
    qspec = pl.BlockSpec((1, win, width // 2), lambda r, b: (r, 0, b))
    return pl.pallas_call(
        functools.partial(rescale, count=count),
        grid=(rolls, 2),
        in_specs=[
            qspec,
            half,
            half,
            pl.BlockSpec((8, 128), lambda r, b: (0, 0)),
            pl.BlockSpec((8, 128), lambda r, b: (0, 0)),
        ],
        out_specs=[qspec, pl.BlockSpec((1, win, 512), lambda r, b: (r, 0, 0))],
        out_shape=[jax.ShapeDtypeStruct(dq.shape, bf16), jax.ShapeDtypeStruct((rolls, win, 512), bf16)],
        input_output_aliases={0: 0},
        compiler_params=pltpu.CompilerParams(vmem_limit_bytes=LIMIT),
        name="rescale",
    )(dq, dw0, dw1, sums, stat)


def settle(d0_ref, d1_ref, cache_ref, kg_ref, freq_ref, mine_ref, sums_ref, out_ref, *, count):
    prompts, tok, width = cache_ref.shape
    scale = global_scale(sums_ref, count)
    _, mean = helpers()
    cos, sin = turns(mine_ref[0] * tok, tok, freq_ref[...])
    for h, d_ref in enumerate((d0_ref, d1_ref)):
        for p in range(prompts):
            g = d_ref[0, p].astype(f32)
            for m in range(1, d_ref.shape[0]):
                g += d_ref[m, p].astype(f32)
            g *= scale
            key = pull(cache_ref[p, :, h * 128 : (h + 1) * 128], g[:, :128], pltpu.roll(g[:, :128], 64, 1), kg_ref[...], cos, sin, mean)
            out_ref[p, :, h * 128 : (h + 1) * 128] = key.astype(bf16)
            out_ref[p, :, (2 + h) * 128 : (3 + h) * 128] = g[:, 128:].astype(bf16)


def make_settle(d0, d1, cache, kgain, mine, sums, count):
    smem, vmem = pl.BlockSpec(memory_space=pltpu.SMEM), pl.BlockSpec(memory_space=pltpu.VMEM)
    return pl.pallas_call(
        functools.partial(settle, count=count),
        grid=(1,),
        in_specs=[vmem, vmem, vmem, vmem, vmem, smem, vmem],
        out_specs=vmem,
        out_shape=jax.ShapeDtypeStruct(cache.shape, bf16),
        compiler_params=pltpu.CompilerParams(vmem_limit_bytes=LIMIT),
        name="settle",
    )(d0, d1, cache, kgain, frequency, mine, sums)


def local(prompt_cache, key_gain, query_gain, window_cache, queries, upstream, rewards, assign, offsets):
    groups, members = lax.axis_size("prompt"), lax.axis_size("roll")
    rolls = queries.shape[0]
    prompts, tok, _ = prompt_cache.shape
    chips = members // 2
    mine = lax.axis_index("roll")
    same_core = [[2 * c + k for c in range(chips)] for k in range(2)]
    other_core = [(m, m ^ 1) for m in range(members)]

    def flip(x):
        return lax.ppermute(x, "roll", other_core)

    mine = mine.astype(jnp.int32)[None]
    qgain, kgain = query_gain[None], key_gain[None]
    first, second = make_pack(prompt_cache, rewards, assign, kgain, mine, chips)
    ga = lax.all_to_all(first, "roll", 0, 0, tiled=True, axis_index_groups=same_core)
    scalar = jnp.concatenate([assign, mine % 2])
    qs, cw, sw = make_ready(queries, qgain, offsets, members * tok)
    ga, qs, cw, sw, scalar = lax.optimization_barrier((ga, qs, cw, sw, scalar))
    gb = flip(ga)
    second, _ = lax.optimization_barrier((second, ga))
    g1 = lax.all_to_all(jnp.broadcast_to(second, (members,) + second.shape), "roll", 0, 0, tiled=True).reshape(chips, 2, prompts, tok, 256)

    def add_far(x, step):
        return x + lax.ppermute(x, "prompt", [(i, i ^ step) for i in range(groups)])

    def attention(h, merge, a, b, *before):
        return call(
            h, 16, 4, 512, merge, scalar, qs, queries, upstream, a, b, ga, gb, window_cache, qgain, kgain, cw, sw, rewards, tok, prompts, *before
        )

    att, dq, dw0, stat, pieces = attention(0, True, ga, gb)
    pieces, g1 = lax.optimization_barrier((pieces, g1))
    sum0 = lax.all_to_all(pieces.reshape(members, prompts, tok, 256), "roll", 0, 0, tiled=True)
    sums = add_far(stat, 1)
    att, dq, dw1, _, own, other = attention(1, False, g1, g1, att, dq)
    own, other, sum0, sums = lax.optimization_barrier((own, other, sum0, sums))
    merged = (own.astype(f32) + flip(other).astype(f32)).astype(bf16)
    sums = add_far(sums, 2)
    sum1 = lax.all_to_all(merged, "roll", 0, 0, tiled=True, axis_index_groups=same_core)
    sums, _ = lax.optimization_barrier((sums, merged))
    sums = add_far(sums, 4)
    count = groups * members * rolls
    dq, window_grad = make_rescale(dq, dw0, dw1, sums, stat, count)
    prompt_grad = make_settle(sum0, sum1, prompt_cache, kgain, mine, sums, count)
    return att, dq, window_grad, prompt_grad


def solution(mesh):
    both = P(("prompt", "roll"))
    return jax.shard_map(
        local,
        mesh=mesh,
        in_specs=(P("prompt", "roll", None), P(), P(), both, both, both, both, both, both),
        out_specs=(both, both, both, P("prompt", "roll", None)),
        check_vma=False,
    )
```

time: 127 us -> 105 us (0.83)
  waiting for transfers between devices: 36.8 us -> 12.7 us
  Pallas kernels: 43 us -> 54 us
  other arithmetic: 12.7 us -> 3.91 us
  starting transfers between devices: 26.1 us -> 29.6 us
  local copies, waits for them, and re-layouts: 6.08 us -> 2.85 us
    all_to_all x5 -> x4, waiting for transfers between devices: 36.8 us -> 4.95 us  [the longest x1 4.94 us: local(): lax.all_to_all(first, 'roll', 0, 0, tiled=True, axis_index_groups=same_core)]
    pallas_call x2 -> x6, Pallas kernels: 43 us -> 54 us  [the longest x2 40.3 us: call(): pl.pallas_call(functools.partial(attend, heads=heads, subs=subs, tc=tc, m...]
    ppermute x0 -> x3, starting transfers between devices: none -> 8.16 us  [add_far(): return x + lax.ppermute(x, 'prompt', [(i, i ^ step) for i in range(groups)])]
    ppermute x0 -> x3, waiting for transfers between devices: none -> 6.03 us  [add_far(): return x + lax.ppermute(x, 'prompt', [(i, i ^ step) for i in range(groups)])]
    concatenate x9 -> x1, other arithmetic: 5.08 us -> 0.66 us  [local(): scalar = jnp.concatenate([assign, mine % 2])]
    all_to_all x5 -> x4, starting transfers between devices: 25.1 us -> 20.9 us  [the longest x1 6.04 us: local(): lax.all_to_all(first, 'roll', 0, 0, tiled=True, axis_index_groups=same_core)]
    neg x2 -> x0, other arithmetic: 2.44 us -> none  [tables(): return (jnp.concatenate([c, c], axis=-1), jnp.concatenate([-s, s], axis=-1))]
    ppermute x4 -> x2, waiting for transfers between devices: 0.01 us -> 1.75 us  [flip(): return lax.ppermute(x, 'roll', other_core)]
  transfers between devices with their start and end apart: 9 -> 9, of which waited for: 5 -> 5; matrix products, arithmetic and copies ran while one was open for 9% -> 3% of each run, Pallas kernels for 34% -> 48%
where the time goes in v2:
time: 105 us; the launch traced here: 104 us
  Pallas kernels  54 us (51%)
  starting transfers between devices  29.6 us (28%)
  waiting for transfers between devices  12.7 us (12%)
  other arithmetic  3.91 us (4%)
  local copies, waits for them, and re-layouts  2.85 us (3%)
    pallas_call x2, Pallas kernels, call(): pl.pallas_call(functools.partial(attend, heads=heads, subs=subs, tc=tc, m...  40.3 us
    ppermute x3, starting transfers between devices, add_far(): return x + lax.ppermute(x, 'prompt', [(i, i ^ step) for i in range(groups)])  8.16 us
    all_to_all x1, starting transfers between devices, local(): lax.all_to_all(first, 'roll', 0, 0, tiled=True, axis_index_groups=same_core)  6.04 us
    ppermute x3, waiting for transfers between devices, add_far(): return x + lax.ppermute(x, 'prompt', [(i, i ^ step) for i in range(groups)])  6.03 us
    all_to_all x1, starting transfers between devices, local(): lax.all_to_all(pieces.reshape(members, prompts, tok, 256), 'roll', 0, 0,...  5.66 us
    all_to_all x1, starting transfers between devices, local(): lax.all_to_all(merged, 'roll', 0, 0, tiled=True, axis_index_groups=same_c...  5.59 us
    all_to_all x1, waiting for transfers between devices, local(): lax.all_to_all(first, 'roll', 0, 0, tiled=True, axis_index_groups=same_core)  4.94 us
    pallas_call x1, Pallas kernels, make_ready(): pl.pallas_call(functools.partial(ready, heads=heads, plen=plen), grid=(ro...  4.57 us
  transfers between devices with their start and end apart: 9, of which 5 were waited for; matrix products, arithmetic and copies ran while one was open for 3% of the time, Pallas kernels for 48%

profile of v2, /device:TPU:0, one launch (start us, length us, event | category | flops | bytes accessed | tf_op | source)
XLA Modules:
  0.0 103.8 jit_solution(901951516066458498)
XLA Ops:
  0.6 2.0 %pack.1 = (bf16[8,144,256]{2,1,0:T(8,128)(2,1)}, bf16[2,64,256]{2,1,0:T(8,128)(2,1)}) custom-call(bf16[2,64,512]{2,1,0:T(8,128)(2,1)} %cache_ref.3, f32[2]{0:T(128)} %rw_ref.3, s32[2]{0:T(128)} %assign_ref.1, f32[1,128]{1,0:T(1,128)} %bitcast.8, f32[1,128]{1,0:T(1,128)} %constant.25.clone.freq_ref, s32[1]{0:T(128)} %bitcast.1.mine_ref), custom_call_target="tpu_custom_call" | custom-call | tf_op jit(solution)/shard_map/pack/pallas_call | solution.py:309
  2.6 6.0 %all-to-all-start = ((bf16[8,144,256]{2,1,0:T(8,128)(2,1)}), bf16[8,144,256]{2,1,0:T(8,128)(2,1)S(1)}, u32[]{:S(2)}, u32[]{:S(2)}) async-start(bf16[8,144,256]{2,1,0:T(8,128)(2,1)} %get-tuple-element.34), calls=%async_computation | async-start | bytes 1179648 | tf_op jit(solution)/shard_map/all_to_all | solution.py:397
  8.7 4.6 %ready.1 = (bf16[2,32,128,128]{3,2,1,0:T(8,128)(2,1)}, f32[2,128,128]{2,1,0:T(8,128)}, f32[2,128,128]{2,1,0:T(8,128)}) custom-call(bf16[2,128,4096]{2,1,0:T(8,128)(2,1)} %q_ref.5, f32[1,128]{1,0:T(1,128)} %bitcast.12, f32[1,128]{1,0:T(1,128)} %constant.25.clone.freq_ref, s32[2]{0:T(128)} %off_ref.1), custom_call_target="tpu_custom_call" | custom-call | tf_op jit(solution)/shard_map/ready/pallas_call | solution.py:264
  13.3 0.7 pad_add_fusion.scalar
  13.9 4.9 %all-to-all-done.ga_ref.fa_ref = bf16[8,144,256]{2,1,0:T(8,128)(2,1)S(1)} async-done(((bf16[8,144,256]{2,1,0:T(8,128)(2,1)}), bf16[8,144,256]{2,1,0:T(8,128)(2,1)S(1)}, u32[]{:S(2)}, u32[]{:S(2)}) %all-to-all-start) | async-done | bytes 589856 | tf_op jit(solution)/shard_map/all_to_all | solution.py:397
  18.9 1.2 %broadcast_in_dim.15 = bf16[16,2,64,256]{3,2,1,0:T(8,128)(2,1)} broadcast(bf16[2,64,256]{2,1,0:T(8,128)(2,1)S(1)} %copy-done.4), dimensions={1,2,3} | broadcast | bytes 1114112 | tf_op jit(solution)/shard_map/broadcast_in_dim | solution.py:403
  20.1 3.7 %all-to-all-start.1 = ((bf16[16,2,64,256]{3,2,1,0:T(8,128)(2,1)}), bf16[16,2,64,256]{3,2,1,0:T(8,128)(2,1)S(1)}, u32[]{:S(2)}, u32[]{:S(2)}) async-start(bf16[16,2,64,256]{3,2,1,0:T(8,128)(2,1)} %broadcast_in_dim.15), calls=%async_computation.1 | async-start | bytes 2097152 | tf_op jit(solution)/shard_map/all_to_all | solution.py:403
  23.8 0.8 copy-done.6
  24.6 20.1 %attend.2 = (bf16[2,128,4096]{2,1,0:T(8,128)(2,1)}, bf16[2,128,4096]{2,1,0:T(8,128)(2,1)}, f32[2,128,256]{2,1,0:T(8,128)}, f32[8,128]{1,0:T(8,128)}, bf16[8,2,2,64,256]{4,3,2,1,0:T(8,128)(2,1)}) custom-call(s32[3]{0:T(128)} %pad_add_fusion.scalar, bf16[2,32,128,128]{3,2,1,0:T(8,128)(2,1)} %get-tuple-element.39.qs_ref, bf16[2,128,4096]{2,1,0:T(8,128)(2,1)} %q_ref.5, ...), custom_call_target="tpu_custom_call" | custom-call | flops 21743271936 | bytes 5242880 | tf_op jit(solution)/shard_map/attend/pallas_call | solution.py:206
  44.8 1.6 %collective-permute-start.1 = (f32[8,128]{1,0:T(8,128)}, f32[8,128]{1,0:T(8,128)S(1)}, u32[]{:S(2)}, u32[]{:S(2)}) collective-permute-start(f32[8,128]{1,0:T(8,128)} %get-tuple-element.56.stat_ref), channel_id=1, source_target_pairs={{0,16},{16,0},{32,48},{48,32},{64,80},{80,64},{96,112},{112,96},{1... | collective-permute-start | bytes 12296 | tf_op jit(solution)/shard_map/ppermute | solution.py:406
  46.3 2.3 %collective-permute-done.1 = f32[8,128]{1,0:T(8,128)S(1)} collective-permute-done((f32[8,128]{1,0:T(8,128)}, f32[8,128]{1,0:T(8,128)S(1)}, u32[]{:S(2)}, u32[]{:S(2)}) %collective-permute-start.1) | collective-permute-done | bytes 4128 | tf_op jit(solution)/shard_map/ppermute | solution.py:406
  48.6 0.7 add.19
  49.3 5.7 %all-to-all-start.2 = ((bf16[16,2,64,256]{3,2,1,0:T(8,128)(2,1)}), bf16[16,2,64,256]{3,2,1,0:T(8,128)(2,1)S(1)}, u32[]{:S(2)}, u32[]{:S(2)}) async-start(bf16[16,2,64,256]{3,2,1,0:T(8,128)(2,1)} %bitcast.7), calls=%async_computation.2 | async-start | bytes 2097152 | tf_op jit(solution)/shard_map/all_to_all | solution.py:415
  55.0 20.2 %attend.3 = (bf16[2,128,4096]{2,1,0:T(8,128)(2,1)}, bf16[2,128,4096]{2,1,0:T(8,128)(2,1)}, f32[2,128,256]{2,1,0:T(8,128)}, f32[8,128]{1,0:T(8,128)}, bf16[8,2,64...) custom-call(s32[3]{0:T(128)} %pad_add_fusion.scalar, ...), custom_call_target="tpu_custom_call", output_to_operand_aliasing={{0}: (15, {}), {1}: (16, {})} | custom-call | flops 21743271936 | bytes 5242880 | tf_op jit(solution)/shard_map/attend/pallas_call | solution.py:206
  75.7 1.7 %collective-permute-done.3 = bf16[8,2,64,256]{3,2,1,0:T(8,128)(2,1)S(1)} collective-permute-done((bf16[8,2,64,256]{3,2,1,0:T(8,128)(2,1)}, bf16[8,2,64,256]{3,2,1,0:T(8,128)(2,1)S(1)}, u32[]{:S(2)}, u32[]{:S(2)}) %collective-permute-start.3) | collective-permute-done | bytes 524320 | tf_op jit(solution)/shard_map/ppermute | solution.py:392
  77.4 2.0 %add_convert_fusion = bf16[8,2,64,256]{3,2,1,0:T(8,128)(2,1)} fusion(bf16[8,2,64,256]{3,2,1,0:T(8,128)(2,1)S(1)} %collective-permute-done.3, bf16[8,2,64,256]{3,2,1,0:T(8,128)(2,1)} %get-tuple-element.58), kind=kLoop, calls=%fused_computation | loop fusion | flops 1048576 | bytes 1572864 | tf_op jit(solution)/shard_map/convert_element_type | solution.py:419
  79.4 5.6 %all-to-all-start.3 = ((bf16[8,2,64,256]{3,2,1,0:T(8,128)(2,1)}), bf16[8,2,64,256]{3,2,1,0:T(8,128)(2,1)S(1)}, u32[]{:S(2)}, u32[]{:S(2)}) async-start(bf16[8,2,64,256]{3,2,1,0:T(8,128)(2,1)} %add_convert_fusion), calls=%async_computation.3 | async-start | bytes 1048576 | tf_op jit(solution)/shard_map/all_to_all | solution.py:421
  85.0 3.0 %collective-permute-start.2 = (f32[8,128]{1,0:T(8,128)S(1)}, f32[8,128]{1,0:T(8,128)S(1)}, u32[]{:S(2)}, u32[]{:S(2)}) collective-permute-start(f32[8,128]{1,0:T(8,128)S(1)} %add.19), channel_id=1, source_target_pairs={{0,32},{16,48},{32,0},{48,16},{64,96},{80,112},{96,64},{112,80},{1... | collective-permute-start | bytes 12296 | tf_op jit(solution)/shard_map/ppermute | solution.py:406
  88.0 2.1 %collective-permute-done.2 = f32[8,128]{1,0:T(8,128)S(1)} collective-permute-done((f32[8,128]{1,0:T(8,128)S(1)}, f32[8,128]{1,0:T(8,128)S(1)}, u32[]{:S(2)}, u32[]{:S(2)}) %collective-permute-start.2) | collective-permute-done | bytes 4128 | tf_op jit(solution)/shard_map/ppermute | solution.py:406
  90.1 3.6 %collective-permute-start.4 = (f32[8,128]{1,0:T(8,128)S(1)}, f32[8,128]{1,0:T(8,128)S(1)}, u32[]{:S(2)}, u32[]{:S(2)}) collective-permute-start(f32[8,128]{1,0:T(8,128)S(1)} %add.20), channel_id=1, source_target_pairs={{0,64},{16,80},{32,96},{48,112},{64,0},{80,16},{96,32},{112,48},{1... | collective-permute-start | bytes 12296 | tf_op jit(solution)/shard_map/ppermute | solution.py:406
  93.7 1.6 %collective-permute-done.4 = f32[8,128]{1,0:T(8,128)S(1)} collective-permute-done((f32[8,128]{1,0:T(8,128)S(1)}, f32[8,128]{1,0:T(8,128)S(1)}, u32[]{:S(2)}, u32[]{:S(2)}) %collective-permute-start.4) | collective-permute-done | bytes 4128 | tf_op jit(solution)/shard_map/ppermute | solution.py:406
  95.9 4.5 %rescale.1 = (bf16[2,128,4096]{2,1,0:T(8,128)(2,1)}, bf16[2,128,512]{2,1,0:T(8,128)(2,1)}) custom-call(bf16[2,128,4096]{2,1,0:T(8,128)(2,1)} %get-tuple-element.50.dq_ref, f32[2,128,256]{2,1,0:T(8,128)} %get-tuple-element.51.dw0_ref, f32[2,128,256]{2,1,0:T(8,128)} %get-tuple-element.52.dw1_ref, ...), custom_call_target="tpu_custom_call", output_to_operand_aliasing={{0}: (0, {})} | custom-call | tf_op jit(solution)/shard_map/rescale/pallas_call | solution.py:335
  100.4 0.8 copy-done.1
  101.2 2.6 %settle.1 = bf16[2,64,512]{2,1,0:T(8,128)(2,1)} custom-call(bf16[16,2,64,256]{3,2,1,0:T(8,128)(2,1)} %copy-done, bf16[8,2,64,256]{3,2,1,0:T(8,128)(2,1)} %copy-done.1, bf16[2,64,512]{2,1,0:T(8,128)(2,1)} %cache_ref.3, f32[1,128]{1,0:T(1,128)} %bitcast.11, f32[1,128]{1,0:T(1,128)} %constant.25.clone.freq_ref, s32[1]{0:T(128)} %bitcast.1.mine_ref, ...), custom_call_target="tpu_custom_call" | custom-call | tf_op jit(solution)/shard_map/settle/pallas_call | solution.py:371
  (20 shorter events, 1.1 us)
Async XLA Ops:
  0.6 12.6 %copy-start.5 = (s32[2]{0:T(128)S(1)}, s32[2]{0:T(128)}, u32[]{:S(2)}) copy-start(s32[2]{0:T(128)} %assign_ref.1) | copy-start | bytes 28
  2.6 16.2 %copy-start.4 = (bf16[2,64,256]{2,1,0:T(8,128)(2,1)S(1)}, bf16[2,64,256]{2,1,0:T(8,128)(2,1)}, u32[]{:S(2)}) copy-start(bf16[2,64,256]{2,1,0:T(8,128)(2,1)} %get-tuple-element.45) | copy-start | bytes 196612
  2.6 16.2 %all-to-all-start = ((bf16[8,144,256]{2,1,0:T(8,128)(2,1)}), bf16[8,144,256]{2,1,0:T(8,128)(2,1)S(1)}, u32[]{:S(2)}, u32[]{:S(2)}) async-start(bf16[8,144,256]{2,1,0:T(8,128)(2,1)} %get-tuple-element.34), calls=%async_computation | async-start | bytes 1179648 | tf_op jit(solution)/shard_map/all_to_all | solution.py:397
  18.9 4.9 %copy-start.3 = (bf16[8,144,256]{2,1,0:T(8,128)(2,1)}, bf16[8,144,256]{2,1,0:T(8,128)(2,1)S(1)}, u32[]{:S(2)}) copy-start(bf16[8,144,256]{2,1,0:T(8,128)(2,1)S(1)} %all-to-all-done.ga_ref.fa_ref) | copy-start | bytes 1769476
  18.9 4.9 %collective-permute-start = (bf16[8,144,256]{2,1,0:T(8,128)(2,1)S(1)}, bf16[8,144,256]{2,1,0:T(8,128)(2,1)S(1)}, u32[]{:S(2)}, u32[]{:S(2)}) collective-permute-start(bf16[8,144,256]{2,1,0:T(8,128)(2,1)S(1)} %all-to-all-done.ga_ref.fa_ref), channel_id=1, source_target_pairs={{0,1},{1,0},{2,3},{3,2},{4,5},{5,4},{6,7},{7,6},{8,9},{9,8},{10,11... | collective-permute-start | bytes 1769480 | tf_op jit(solution)/shard_map/ppermute | solution.py:392
  20.1 29.2 %all-to-all-start.1 = ((bf16[16,2,64,256]{3,2,1,0:T(8,128)(2,1)}), bf16[16,2,64,256]{3,2,1,0:T(8,128)(2,1)S(1)}, u32[]{:S(2)}, u32[]{:S(2)}) async-start(bf16[16,2,64,256]{3,2,1,0:T(8,128)(2,1)} %broadcast_in_dim.15), calls=%async_computation.1 | async-start | bytes 2097152 | tf_op jit(solution)/shard_map/all_to_all | solution.py:403
  23.8 0.8 copy-start.6
  44.8 3.9 %collective-permute-start.1 = (f32[8,128]{1,0:T(8,128)}, f32[8,128]{1,0:T(8,128)S(1)}, u32[]{:S(2)}, u32[]{:S(2)}) collective-permute-start(f32[8,128]{1,0:T(8,128)} %get-tuple-element.56.stat_ref), channel_id=1, source_target_pairs={{0,16},{16,0},{32,48},{48,32},{64,80},{80,64},{96,112},{112,96},{1... | collective-permute-start | bytes 12296 | tf_op jit(solution)/shard_map/ppermute | solution.py:406
  49.3 5.7 %copy-start.2 = (bf16[16,2,64,256]{3,2,1,0:T(8,128)(2,1)}, bf16[16,2,64,256]{3,2,1,0:T(8,128)(2,1)S(1)}, u32[]{:S(2)}) copy-start(bf16[16,2,64,256]{3,2,1,0:T(8,128)(2,1)S(1)} %all-to-all-done.1) | copy-start | bytes 3145732
  49.3 25.9 %all-to-all-start.2 = ((bf16[16,2,64,256]{3,2,1,0:T(8,128)(2,1)}), bf16[16,2,64,256]{3,2,1,0:T(8,128)(2,1)S(1)}, u32[]{:S(2)}, u32[]{:S(2)}) async-start(bf16[16,2,64,256]{3,2,1,0:T(8,128)(2,1)} %bitcast.7), calls=%async_computation.2 | async-start | bytes 2097152 | tf_op jit(solution)/shard_map/all_to_all | solution.py:415
  75.2 25.2 %copy-start = (bf16[16,2,64,256]{3,2,1,0:T(8,128)(2,1)}, bf16[16,2,64,256]{3,2,1,0:T(8,128)(2,1)S(1)}, u32[]{:S(2)}) copy-start(bf16[16,2,64,256]{3,2,1,0:T(8,128)(2,1)S(1)} %all-to-all-done.2.d0_ref) | copy-start | bytes 3145732
  75.2 2.2 %collective-permute-start.3 = (bf16[8,2,64,256]{3,2,1,0:T(8,128)(2,1)}, bf16[8,2,64,256]{3,2,1,0:T(8,128)(2,1)S(1)}, u32[]{:S(2)}, u32[]{:S(2)}) collective-permute-start(bf16[8,2,64,256]{3,2,1,0:T(8,128)(2,1)} %get-tuple-element.59), channel_id=1, source_target_pairs={{0,1},{1,0},{2,3},{3,2},{4,5},{5,4},{6,7},{7,6},{8,9},{9,8},{10,11... | collective-permute-start | bytes 1572872 | tf_op jit(solution)/shard_map/ppermute | solution.py:392
  79.4 21.0 %all-to-all-start.3 = ((bf16[8,2,64,256]{3,2,1,0:T(8,128)(2,1)}), bf16[8,2,64,256]{3,2,1,0:T(8,128)(2,1)S(1)}, u32[]{:S(2)}, u32[]{:S(2)}) async-start(bf16[8,2,64,256]{3,2,1,0:T(8,128)(2,1)} %add_convert_fusion), calls=%async_computation.3 | async-start | bytes 1048576 | tf_op jit(solution)/shard_map/all_to_all | solution.py:421
  85.0 5.1 %collective-permute-start.2 = (f32[8,128]{1,0:T(8,128)S(1)}, f32[8,128]{1,0:T(8,128)S(1)}, u32[]{:S(2)}, u32[]{:S(2)}) collective-permute-start(f32[8,128]{1,0:T(8,128)S(1)} %add.19), channel_id=1, source_target_pairs={{0,32},{16,48},{32,0},{48,16},{64,96},{80,112},{96,64},{112,80},{1... | collective-permute-start | bytes 12296 | tf_op jit(solution)/shard_map/ppermute | solution.py:406
  90.1 5.2 %collective-permute-start.4 = (f32[8,128]{1,0:T(8,128)S(1)}, f32[8,128]{1,0:T(8,128)S(1)}, u32[]{:S(2)}, u32[]{:S(2)}) collective-permute-start(f32[8,128]{1,0:T(8,128)S(1)} %add.20), channel_id=1, source_target_pairs={{0,64},{16,80},{32,96},{48,112},{64,0},{80,16},{96,32},{112,48},{1... | collective-permute-start | bytes 12296 | tf_op jit(solution)/shard_map/ppermute | solution.py:406
  100.4 0.8 copy-start.1

commit v3 on v2

--- a/solution.py
+++ b/solution.py
@@ -14,7 +14,7 @@
 spread_eps = 1e-06
 LOG2E = math.log2(math.e)
 bf16, f32 = jnp.bfloat16, jnp.float32
-LIMIT = 56 * 1024 * 1024
+LIMIT = 62 * 1024 * 1024
 frequency = np.tile(rope_base ** (-np.arange(64) * 2.0 / 128), 2).astype(np.float32)[None]
 
 
@@ -57,7 +57,13 @@
     return jnp.cos(angles), jnp.where(upper, sine, -sine)
 
 
-def ready(q_ref, gain_ref, freq_ref, off_ref, qs_ref, cw_ref, sw_ref, *, heads, plen):
+def ready(q_ref, gain_ref, freq_ref, off_ref, second_ref, facts_ref, far_ref, qs_ref, cw_ref, sw_ref, copies_ref, *, heads, plen):
+    count = second_ref.shape[0]
+    pair = jnp.concatenate([facts_ref[0:1], far_ref[0:1], jnp.zeros((14, 256), bf16)], axis=0)
+    for c in range(copies_ref.shape[0]):
+        copies_ref[c, :count] = second_ref[...]
+        copies_ref[c, count:] = pair
+
     swap, mean = helpers()
     gain = gain_ref[...] * (LOG2E / math.sqrt(128))
     win = cw_ref.shape[1]
@@ -69,15 +75,23 @@
     qs_ref[0] = prepare(q, gain, cos, sin, swap, mean)[0].astype(bf16).reshape(heads, win, 128)
 
 
+def summary(f):
+    reward = [f[:, 3 * n : 3 * n + 1] + f[:, 3 * n + 1 : 3 * n + 2] + f[:, 3 * n + 2 : 3 * n + 3] for n in range(2)]
+    place = [f[:, 6 + n : 7 + n] for n in range(2)]
+    means = [
+        sum(jnp.sum(jnp.where(place[n] == p, reward[n], 0.0), axis=0, keepdims=True) for n in range(2)) / f.shape[0] for p in range(2)
+    ]
+    spread = sum(jnp.sum((reward[n] - jnp.where(place[n] == 0, means[0], means[1])) ** 2, axis=0, keepdims=True) for n in range(2))
+    return means, spread
+
+
 def attend(
     scalar, qs_ref, q_ref, up_ref, ga_ref, gb_ref, fa_ref, fb_ref, wk_ref, wv_ref, qg_ref, kg_ref, cw_ref, sw_ref, rw_ref, *refs,
-    heads, subs, tc, merge, tok, win
+    heads, subs, tc, tok, win
 ):
-    n_out = 4 + (1 if merge else 2)
-    att_ref, dq_ref, dwin_ref, stat_ref, *outs = refs[-6 - n_out : -6]
+    att_ref, dq_ref, dwin_ref, stat_ref, *outs = refs[-12:-6]
     kp, va, dk, dv, e_ref, ds_ref = refs[-6:]
     r, hb = pl.program_id(0), pl.program_id(1)
-    core = scalar[2]
     chips = ga_ref.shape[0]
     half = chips * tok
     plen = 2 * half
@@ -153,17 +167,9 @@
 
         @pl.when(r == 1)
         def _():
-            f = jnp.concatenate([fa_ref[:, 0], fb_ref[:, 0]], axis=0).astype(f32)
-            reward = [f[:, 3 * n : 3 * n + 1] + f[:, 3 * n + 1 : 3 * n + 2] + f[:, 3 * n + 2 : 3 * n + 3] for n in range(2)]
-            place = [f[:, 6 + n : 7 + n] for n in range(2)]
-            per_prompt = f.shape[0]
-            means = [
-                sum(jnp.sum(jnp.where(place[n] == p, reward[n], 0.0), axis=0, keepdims=True) for n in range(2)) / per_prompt
-                for p in range(2)
-            ]
-            spread = sum(
-                jnp.sum((reward[n] - jnp.where(place[n] == 0, means[0], means[1])) ** 2, axis=0, keepdims=True) for n in range(2)
-            )
+            f = jnp.concatenate([fa_ref[...].reshape(chips, 16, 256), fb_ref[...].reshape(chips, 16, 256)], axis=0).astype(f32)
+            means, spread = summary(f[:, 0])
+            spread += summary(f[:, 1])[1]
             centred = [rw_ref[n] - jnp.where(scalar[n] == 0, means[0], means[1]) for n in range(2)]
             lane = lax.broadcasted_iota(jnp.int32, stat_ref.shape, 1)
             stat_ref[...] = jnp.where(lane == 0, spread, jnp.where(lane == 1, centred[0], centred[1]))
@@ -173,13 +179,10 @@
                     for c, (acc, scale) in enumerate(((dk, ln2), (dv, 1.0))):
                         w = [jnp.where(scalar[n] == p, centred[n], 0.0) * scale for n in range(2)]
                         m = (w[0] * acc[0, :, cols] + w[1] * acc[1, :, cols]).astype(bf16).T.reshape(chips, tok, 128)
-                        if merge:
-                            outs[0][:, lax.rem(core + i, 2), p, :, c * 128 : (c + 1) * 128] = m
-                        else:
-                            outs[i][:, p, :, c * 128 : (c + 1) * 128] = m
-
-
-def call(h, heads, subs, tc, merge, scalar, qs, q, up, ga, gb, fa, fb, wc, qgain, kgain, cw, sw, rewards, tok, prompts, *before):
+                        outs[i][:, p * tok : (p + 1) * tok, c * 128 : (c + 1) * 128] = m
+
+
+def call(h, heads, subs, tc, scalar, qs, q, up, ga, gb, wc, qgain, kgain, cw, sw, rewards, tok, prompts, *before):
     rolls, win, width = up.shape
     chips = ga.shape[0]
     kvh = wc.shape[2] // 256
@@ -190,21 +193,24 @@
     t = plen + win
     smem = pl.BlockSpec(memory_space=pltpu.SMEM)
     anywhere = pl.BlockSpec(memory_space=pl.ANY)
+    spot = prompts * tok // 16
     if ga.ndim == 3:
         gspecs = [pl.BlockSpec((chips, tok, 256), lambda r, b, a: (0, a[r], 0))] * 2
+        gspecs += [pl.BlockSpec((chips, 16, 256), lambda r, b, a: (0, spot, 0))] * 2
     else:
         gspecs = [
-            pl.BlockSpec((chips, 1, 1, tok, 256), lambda r, b, a: (0, a[2], a[r], 0, 0)),
-            pl.BlockSpec((chips, 1, 1, tok, 256), lambda r, b, a: (0, 1 - a[2], a[r], 0, 0)),
+            pl.BlockSpec((chips, 1, tok, 256), lambda r, b, a: (0, a[2], a[r], 0)),
+            pl.BlockSpec((chips, 1, tok, 256), lambda r, b, a: (0, 1 - a[2], a[r], 0)),
+            pl.BlockSpec((chips, 1, 16, 256), lambda r, b, a: (0, a[2], spot, 0)),
+            pl.BlockSpec((chips, 1, 16, 256), lambda r, b, a: (0, 1 - a[2], spot, 0)),
         ]
-    fspec = pl.BlockSpec((chips, 16, 256), lambda r, b, a: (0, prompts * tok // 16, 0))
     ospec = pl.BlockSpec((1, win, heads * 128), lambda r, b, a: (r, 0, h * steps + b))
     vec = pl.BlockSpec((1, 128), lambda r, b, a: (0, 0))
     wspec = pl.BlockSpec((1, win, 128), lambda r, b, a: (r, 0, 0))
-    piece = (chips, 2, prompts, tok, 256) if merge else (chips, prompts, tok, 256)
+    piece = (chips, prompts * tok, 256)
     pieces = pl.BlockSpec(piece, lambda r, b, a: (0,) * len(piece))
     return pl.pallas_call(
-        functools.partial(attend, heads=heads, subs=subs, tc=tc, merge=merge, tok=tok, win=win),
+        functools.partial(attend, heads=heads, subs=subs, tc=tc, tok=tok, win=win),
         grid_spec=pltpu.PrefetchScalarGridSpec(
             num_scalar_prefetch=1,
             grid=(rolls, steps),
@@ -213,8 +219,6 @@
                 ospec,
                 ospec,
                 *gspecs,
-                fspec,
-                fspec,
                 pl.BlockSpec((1, win, 128), lambda r, b, a: (r, 0, h)),
                 pl.BlockSpec((1, win, 128), lambda r, b, a: (r, 0, kvh + h)),
                 vec,
@@ -230,7 +234,7 @@
                 pl.BlockSpec((1, win, 256), lambda r, b, a: (r, 0, 0)),
                 pl.BlockSpec((8, 128), lambda r, b, a: (0, 0)),
             ]
-            + [pieces] * (1 if merge else 2),
+            + [pieces] * 2,
             scratch_shapes=[
                 pltpu.VMEM((t, 256), bf16),
                 pltpu.VMEM((t, 256), bf16),
@@ -246,33 +250,41 @@
             jax.ShapeDtypeStruct((rolls, win, 256), f32),
             jax.ShapeDtypeStruct((8, 128), f32),
         ]
-        + [jax.ShapeDtypeStruct(piece, bf16)] * (1 if merge else 2),
+        + [jax.ShapeDtypeStruct(piece, bf16)] * 2,
         input_output_aliases={15: 0, 16: 1} if before else {},
         compiler_params=pltpu.CompilerParams(vmem_limit_bytes=LIMIT),
         cost_estimate=pl.CostEstimate(
             flops=36 * rolls * share * win * t * 128, bytes_accessed=10 * rolls * share * win * 128, transcendentals=rolls * share * win * t
         ),
         name="attend",
-    )(scalar, qs, q, up, ga, gb, fa, fb, wc, wc, qgain, kgain, cw, sw, rewards, *before)
-
-
-def make_ready(q, gain, offsets, plen):
+    )(scalar, qs, q, up, ga, gb, ga, gb, wc, wc, qgain, kgain, cw, sw, rewards, *before)
+
+
+def make_ready(q, gain, offsets, second, facts, far, plen, members):
     rolls, win, width = q.shape
     heads = width // 128
     wspec = pl.BlockSpec((1, win, 128), lambda r: (r, 0, 0))
     vec = pl.BlockSpec((1, 128), lambda r: (0, 0))
+    fspec = pl.BlockSpec((16, 256), lambda r: (0, 0))
     return pl.pallas_call(
         functools.partial(ready, heads=heads, plen=plen),
         grid=(rolls,),
-        in_specs=[pl.BlockSpec((1, win, width), lambda r: (r, 0, 0)), vec, vec, pl.BlockSpec(memory_space=pltpu.SMEM)],
-        out_specs=[pl.BlockSpec((1, heads, win, 128), lambda r: (r, 0, 0, 0)), wspec, wspec],
-        out_shape=[jax.ShapeDtypeStruct((rolls, heads, win, 128), bf16)] + [jax.ShapeDtypeStruct((rolls, win, 128), f32)] * 2,
+        in_specs=[pl.BlockSpec((1, win, width), lambda r: (r, 0, 0)), vec, vec, pl.BlockSpec(memory_space=pltpu.SMEM), pl.BlockSpec(second.shape, lambda r: (0, 0)), fspec, fspec],
+        out_specs=[
+            pl.BlockSpec((1, heads, win, 128), lambda r: (r, 0, 0, 0)),
+            wspec,
+            wspec,
+            pl.BlockSpec((members // rolls, second.shape[0] + 16, 256), lambda r: (r, 0, 0)),
+        ],
+        out_shape=[jax.ShapeDtypeStruct((rolls, heads, win, 128), bf16)]
+        + [jax.ShapeDtypeStruct((rolls, win, 128), f32)] * 2
+        + [jax.ShapeDtypeStruct((members, second.shape[0] + 16, 256), bf16)],
         compiler_params=pltpu.CompilerParams(vmem_limit_bytes=LIMIT),
         name="ready",
-    )(q, gain, frequency, offsets)
-
-
-def pack(cache_ref, reward_ref, assign_ref, kg_ref, freq_ref, mine_ref, first_ref, second_ref):
+    )(q, gain, frequency, offsets, second, facts, far)
+
+
+def pack(cache_ref, reward_ref, assign_ref, kg_ref, freq_ref, mine_ref, first_ref, second_ref, facts_ref):
     prompts, tok, width = cache_ref.shape
     kvh = width // 256
     lane = lax.broadcasted_iota(jnp.int32, (16, 256), 1)
@@ -297,10 +309,12 @@
                 first_ref[c, p * tok : (p + 1) * tok, :128] = key
                 first_ref[c, p * tok : (p + 1) * tok, 128:] = value
         else:
-            second_ref[p, :, :128] = key
-            second_ref[p, :, 128:] = value
+            second_ref[p * tok : (p + 1) * tok, :128] = key
+            second_ref[p * tok : (p + 1) * tok, 128:] = value
+    facts = jnp.where(lax.broadcasted_iota(jnp.int32, (16, 256), 0) == 0, facts, 0.0).astype(bf16)
+    facts_ref[...] = facts
     for c in range(first_ref.shape[0]):
-        first_ref[c, prompts * tok :] = facts.astype(bf16)
+        first_ref[c, prompts * tok :] = facts
 
 
 def make_pack(cache, rewards, assign, kgain, mine, chips):
@@ -309,8 +323,12 @@
     return pl.pallas_call(
         pack,
         in_specs=[vmem, smem, smem, vmem, vmem, smem],
-        out_specs=[vmem, vmem],
-        out_shape=[jax.ShapeDtypeStruct((chips, prompts * tok + 16, 256), bf16), jax.ShapeDtypeStruct((prompts, tok, 256), bf16)],
+        out_specs=[vmem, vmem, vmem],
+        out_shape=[
+            jax.ShapeDtypeStruct((chips, prompts * tok + 16, 256), bf16),
+            jax.ShapeDtypeStruct((prompts * tok, 256), bf16),
+            jax.ShapeDtypeStruct((16, 256), bf16),
+        ],
         name="pack",
     )(cache, rewards, assign, kgain, frequency, mine)
 
@@ -330,19 +348,19 @@
 
 def make_rescale(dq, dw0, dw1, sums, stat, count):
     rolls, win, width = dq.shape
-    half = pl.BlockSpec((1, win, 256), lambda r, b: (r, 0, 0))
-    qspec = pl.BlockSpec((1, win, width // 2), lambda r, b: (r, 0, b))
+    half = pl.BlockSpec((1, win, 256), lambda r: (r, 0, 0))
+    qspec = pl.BlockSpec((1, win, width), lambda r: (r, 0, 0))
     return pl.pallas_call(
         functools.partial(rescale, count=count),
-        grid=(rolls, 2),
+        grid=(rolls,),
         in_specs=[
             qspec,
             half,
             half,
-            pl.BlockSpec((8, 128), lambda r, b: (0, 0)),
-            pl.BlockSpec((8, 128), lambda r, b: (0, 0)),
+            pl.BlockSpec((8, 128), lambda r: (0, 0)),
+            pl.BlockSpec((8, 128), lambda r: (0, 0)),
         ],
-        out_specs=[qspec, pl.BlockSpec((1, win, 512), lambda r, b: (r, 0, 0))],
+        out_specs=[qspec, pl.BlockSpec((1, win, 512), lambda r: (r, 0, 0))],
         out_shape=[jax.ShapeDtypeStruct(dq.shape, bf16), jax.ShapeDtypeStruct((rolls, win, 512), bf16)],
         input_output_aliases={0: 0},
         compiler_params=pltpu.CompilerParams(vmem_limit_bytes=LIMIT),
@@ -350,33 +368,34 @@
     )(dq, dw0, dw1, sums, stat)
 
 
-def settle(d0_ref, d1_ref, cache_ref, kg_ref, freq_ref, mine_ref, sums_ref, out_ref, *, count):
+def settle(d_ref, cache_ref, kg_ref, freq_ref, mine_ref, sums_ref, out_ref, *, count):
     prompts, tok, width = cache_ref.shape
     scale = global_scale(sums_ref, count)
     _, mean = helpers()
     cos, sin = turns(mine_ref[0] * tok, tok, freq_ref[...])
-    for h, d_ref in enumerate((d0_ref, d1_ref)):
+    for h in range(width // 256):
         for p in range(prompts):
-            g = d_ref[0, p].astype(f32)
+            cut = slice((h * prompts + p) * tok, (h * prompts + p + 1) * tok)
+            g = d_ref[0, cut].astype(f32)
             for m in range(1, d_ref.shape[0]):
-                g += d_ref[m, p].astype(f32)
+                g += d_ref[m, cut].astype(f32)
             g *= scale
             key = pull(cache_ref[p, :, h * 128 : (h + 1) * 128], g[:, :128], pltpu.roll(g[:, :128], 64, 1), kg_ref[...], cos, sin, mean)
             out_ref[p, :, h * 128 : (h + 1) * 128] = key.astype(bf16)
             out_ref[p, :, (2 + h) * 128 : (3 + h) * 128] = g[:, 128:].astype(bf16)
 
 
-def make_settle(d0, d1, cache, kgain, mine, sums, count):
+def make_settle(d, cache, kgain, mine, sums, count):
     smem, vmem = pl.BlockSpec(memory_space=pltpu.SMEM), pl.BlockSpec(memory_space=pltpu.VMEM)
     return pl.pallas_call(
         functools.partial(settle, count=count),
         grid=(1,),
-        in_specs=[vmem, vmem, vmem, vmem, vmem, smem, vmem],
+        in_specs=[vmem, vmem, vmem, vmem, smem, vmem],
         out_specs=vmem,
         out_shape=jax.ShapeDtypeStruct(cache.shape, bf16),
         compiler_params=pltpu.CompilerParams(vmem_limit_bytes=LIMIT),
         name="settle",
-    )(d0, d1, cache, kgain, frequency, mine, sums)
+    )(d, cache, kgain, frequency, mine, sums)
 
 
 def local(prompt_cache, key_gain, query_gain, window_cache, queries, upstream, rewards, assign, offsets):
@@ -391,39 +410,37 @@
     def flip(x):
         return lax.ppermute(x, "roll", other_core)
 
+    def far(x, step):
+        return lax.ppermute(x, "prompt", [(i, i ^ step) for i in range(groups)])
+
     mine = mine.astype(jnp.int32)[None]
     qgain, kgain = query_gain[None], key_gain[None]
-    first, second = make_pack(prompt_cache, rewards, assign, kgain, mine, chips)
+    first, second, facts = make_pack(prompt_cache, rewards, assign, kgain, mine, chips)
     ga = lax.all_to_all(first, "roll", 0, 0, tiled=True, axis_index_groups=same_core)
     scalar = jnp.concatenate([assign, mine % 2])
-    qs, cw, sw = make_ready(queries, qgain, offsets, members * tok)
+    qs, cw, sw, copies = make_ready(queries, qgain, offsets, second, facts, far(facts, 1), members * tok, members)
     ga, qs, cw, sw, scalar = lax.optimization_barrier((ga, qs, cw, sw, scalar))
     gb = flip(ga)
-    second, _ = lax.optimization_barrier((second, ga))
-    g1 = lax.all_to_all(jnp.broadcast_to(second, (members,) + second.shape), "roll", 0, 0, tiled=True).reshape(chips, 2, prompts, tok, 256)
-
-    def add_far(x, step):
-        return x + lax.ppermute(x, "prompt", [(i, i ^ step) for i in range(groups)])
-
-    def attention(h, merge, a, b, *before):
+    copies, _ = lax.optimization_barrier((copies, ga))
+    g1 = lax.all_to_all(copies, "roll", 0, 0, tiled=True).reshape(chips, 2, prompts * tok + 16, 256)
+
+    def attention(h, a, b, *before):
         return call(
-            h, 16, 4, 512, merge, scalar, qs, queries, upstream, a, b, ga, gb, window_cache, qgain, kgain, cw, sw, rewards, tok, prompts, *before
+            h, 16, 4, 512, scalar, qs, queries, upstream, a, b, window_cache, qgain, kgain, cw, sw, rewards, tok, prompts, *before
         )
 
-    att, dq, dw0, stat, pieces = attention(0, True, ga, gb)
-    pieces, g1 = lax.optimization_barrier((pieces, g1))
-    sum0 = lax.all_to_all(pieces.reshape(members, prompts, tok, 256), "roll", 0, 0, tiled=True)
-    sums = add_far(stat, 1)
-    att, dq, dw1, _, own, other = attention(1, False, g1, g1, att, dq)
-    own, other, sum0, sums = lax.optimization_barrier((own, other, sum0, sums))
-    merged = (own.astype(f32) + flip(other).astype(f32)).astype(bf16)
-    sums = add_far(sums, 2)
-    sum1 = lax.all_to_all(merged, "roll", 0, 0, tiled=True, axis_index_groups=same_core)
-    sums, _ = lax.optimization_barrier((sums, merged))
-    sums = add_far(sums, 4)
+    att, dq, dw0, _, own0, other0 = attention(0, ga, gb)
+    att, dq, dw1, stat, own1, other1 = attention(1, g1, g1, att, dq)
+    merged = [(own.astype(f32) + flip(other).astype(f32)).astype(bf16) for own, other in ((own0, other0), (own1, other1))]
+    merged = jnp.concatenate(merged, axis=1)
+    parts = lax.all_to_all(merged, "roll", 0, 0, tiled=True, axis_index_groups=same_core)
+    sums, step = stat, 2
+    while step < groups:
+        sums = sums + far(sums, step)
+        step *= 2
     count = groups * members * rolls
     dq, window_grad = make_rescale(dq, dw0, dw1, sums, stat, count)
-    prompt_grad = make_settle(sum0, sum1, prompt_cache, kgain, mine, sums, count)
+    prompt_grad = make_settle(parts, prompt_cache, kgain, mine, sums, count)
     return att, dq, window_grad, prompt_grad
 
 

time: 105 us -> 99.8 us (0.950)
  the two profiles are of different devices: /device:TPU:0 before, /device:TPU:22 now
where the time goes in v3:
time: 99.8 us; the launch traced here: 99.2 us
  Pallas kernels  53 us (53%)
  starting transfers between devices  24.4 us (24%)
  waiting for transfers between devices  13.2 us (13%)
  other arithmetic  5.26 us (5%)
  local copies, waits for them, and re-layouts  2.62 us (3%)
    pallas_call x2, Pallas kernels, call(): pl.pallas_call(functools.partial(attend, heads=heads, subs=subs, tc=tc, t...  40.4 us
    ppermute x3, waiting for transfers between devices, far(): return lax.ppermute(x, 'prompt', [(i, i ^ step) for i in range(groups)])  12.6 us
    all_to_all x1, starting transfers between devices, local(): lax.all_to_all(first, 'roll', 0, 0, tiled=True, axis_index_groups=same_core)  6.16 us
    all_to_all x1, starting transfers between devices, local(): lax.all_to_all(copies, 'roll', 0, 0, tiled=True)  5.83 us
    ppermute x3, starting transfers between devices, far(): return lax.ppermute(x, 'prompt', [(i, i ^ step) for i in range(groups)])  5.81 us
    all_to_all x1, starting transfers between devices, local(): lax.all_to_all(merged, 'roll', 0, 0, tiled=True, axis_index_groups=same_c...  5.71 us
    pallas_call x1, Pallas kernels, make_ready(): pl.pallas_call(functools.partial(ready, heads=heads, plen=plen), grid=(ro...  4.84 us
    pallas_call x1, Pallas kernels, make_rescale(): pl.pallas_call(functools.partial(rescale, count=count), grid=(rolls,), in...  3.35 us
  transfers between devices with their start and end apart: 9, of which 4 were waited for; matrix products, arithmetic and copies ran while one was open for 3% of the time, Pallas kernels for 49%

profile of v3, /device:TPU:22, one launch (start us, length us, event | category | flops | bytes accessed | tf_op | source)
XLA Modules:
  0.0 99.2 jit_solution(7307402883502588849)
XLA Ops:
  0.6 2.0 %pack.1 = (bf16[8,144,256]{2,1,0:T(8,128)(2,1)}, bf16[128,256]{1,0:T(8,128)(2,1)}, bf16[16,256]{1,0:T(8,128)(2,1)}) custom-call(bf16[2,64,512]{2,1,0:T(8,128)(2,1)} %cache_ref.3, f32[2]{0:T(128)} %rw_ref.3, s32[2]{0:T(128)} %assign_ref.1, f32[1,128]{1,0:T(1,128)} %bitcast.8, f32[1,128]{1,0:T(1,128)} %constant.25.clone.freq_ref, s32[1]{0:T(128)} %bitcast.1.mine_ref), custom_call_target="tpu_custom_call" | custom-call | tf_op jit(solution)/shard_map/pack/pallas_call | solution.py:323
  2.6 6.2 %all-to-all-start = ((bf16[8,144,256]{2,1,0:T(8,128)(2,1)}), bf16[8,144,256]{2,1,0:T(8,128)(2,1)S(1)}, u32[]{:S(2)}, u32[]{:S(2)}) async-start(bf16[8,144,256]{2,1,0:T(8,128)(2,1)} %get-tuple-element.30), calls=%async_computation | async-start | bytes 1179648 | tf_op jit(solution)/shard_map/all_to_all | solution.py:419
  8.8 0.8 collective-permute-start
  9.6 1.3 %pad_add_fusion.scalar = s32[3]{0:T(128)} fusion(s32[1]{0:T(128)S(6)} %select_n.7, s32[2]{0:T(128)} %assign_ref.1), kind=kLoop, calls=%fused_computation.3 | loop fusion | flops 3 | bytes 24 | tf_op jit(solution)/shard_map/concatenate | solution.py:420
  10.9 1.8 %collective-permute-done.far_ref = bf16[16,256]{1,0:T(8,128)(2,1)S(1)} collective-permute-done((bf16[16,256]{1,0:T(8,128)(2,1)}, bf16[16,256]{1,0:T(8,128)(2,1)S(1)}, u32[]{:S(2)}, u32[]{:S(2)}) %collective-permute-start) | collective-permute-done | bytes 8224 | tf_op jit(solution)/shard_map/ppermute | solution.py:414
  12.6 0.6 copy-done.5
  13.2 4.8 %ready.1 = (bf16[2,32,128,128]{3,2,1,0:T(8,128)(2,1)}, f32[2,128,128]{2,1,0:T(8,128)}, f32[2,128,128]{2,1,0:T(8,128)}, bf16[16,144,256]{2,1,0:T(8,128)(2,1)}) custom-call(bf16[2,128,4096]{2,1,0:T(8,128)(2,1)} %q_ref.5, f32[1,128]{1,0:T(1,128)} %bitcast.12, f32[1,128]{1,0:T(1,128)} %constant.25.clone.freq_ref, s32[2]{0:T(128)} %off_ref.1, ...), custom_call_target="tpu_custom_call" | custom-call | tf_op jit(solution)/shard_map/ready/pallas_call | solution.py:269
  18.2 5.8 %all-to-all-start.1 = ((bf16[16,144,256]{2,1,0:T(8,128)(2,1)}), bf16[16,144,256]{2,1,0:T(8,128)(2,1)S(1)}, u32[]{:S(2)}, u32[]{:S(2)}) async-start(bf16[16,144,256]{2,1,0:T(8,128)(2,1)} %get-tuple-element.40), calls=%async_computation.1 | async-start | bytes 2359296 | tf_op jit(solution)/shard_map/all_to_all | solution.py:425
  24.0 20.1 %attend.2 = (bf16[2,128,4096]{2,1,0:T(8,128)(2,1)}, bf16[2,128,4096]{2,1,0:T(8,128)(2,1)}, f32[2,128,256]{2,1,0:T(8,128)}, f32[8,128]{1,0:T(8,128)}, bf16[8,128,...) custom-call(s32[3]{0:T(128)} %pad_add_fusion.scalar, bf16[2,32,128,128]{3,2,1,0:T(8,128)(2,1)} %get-tuple-element.37.qs_ref, ...), custom_call_target="tpu_custom_call" | custom-call | flops 21743271936 | bytes 5242880 | tf_op jit(solution)/shard_map/attend/pallas_call | solution.py:212
  44.6 1.0 %copy-done.1 = bf16[16,144,256]{2,1,0:T(8,128)(2,1)} copy-done((bf16[16,144,256]{2,1,0:T(8,128)(2,1)}, bf16[16,144,256]{2,1,0:T(8,128)(2,1)S(1)}, u32[]{:S(2)}) %copy-start.1) | copy-done | bytes 1179672
  45.6 20.3 %attend.3 = (bf16[2,128,4096]{2,1,0:T(8,128)(2,1)}, bf16[2,128,4096]{2,1,0:T(8,128)(2,1)}, f32[2,128,256]{2,1,0:T(8,128)}, f32[8,128]{1,0:T(8,128)}, bf16[8,128,...) custom-call(s32[3]{0:T(128)} %pad_add_fusion.scalar, ...), custom_call_target="tpu_custom_call", output_to_operand_aliasing={{0}: (15, {}), {1}: (16, {})} | custom-call | flops 21743271936 | bytes 5242880 | tf_op jit(solution)/shard_map/attend/pallas_call | solution.py:212
  66.3 1.2 %add_convert_fusion.1 = bf16[8,128,256]{2,1,0:T(8,128)(2,1)S(1)} fusion(bf16[8,128,256]{2,1,0:T(8,128)(2,1)} %collective-permute-done.4, bf16[8,128,256]{2,1,0:T(8,128)(2,1)S(1)} %copy-done.3), kind=kLoop, calls=%fused_computation.2 | loop fusion | flops 1048576 | bytes 1572864 | tf_op jit(solution)/shard_map/convert_element_type | solution.py:434
  67.5 0.6 collective-permute-done.5
  68.1 1.2 %add_convert_fusion = bf16[8,128,256]{2,1,0:T(8,128)(2,1)S(1)} fusion(bf16[8,128,256]{2,1,0:T(8,128)(2,1)S(1)} %collective-permute-done.5, bf16[8,128,256]{2,1,0:T(8,128)(2,1)} %get-tuple-element.54), kind=kLoop, calls=%fused_computation.1 | loop fusion | flops 1048576 | bytes 1572864 | tf_op jit(solution)/shard_map/convert_element_type | solution.py:434
  69.3 1.1 %pad_maximum_fusion = bf16[8,256,256]{2,1,0:T(8,128)(2,1)} fusion(bf16[8,128,256]{2,1,0:T(8,128)(2,1)S(1)} %add_convert_fusion, bf16[8,128,256]{2,1,0:T(8,128)(2,1)S(1)} %add_convert_fusion.1), kind=kLoop, calls=%fused_computation | loop fusion | flops 2097152 | bytes 2097152 | tf_op jit(solution)/shard_map/concatenate | solution.py:435
  70.4 5.7 %all-to-all-start.2 = ((bf16[8,256,256]{2,1,0:T(8,128)(2,1)}), bf16[8,256,256]{2,1,0:T(8,128)(2,1)S(1)}, u32[]{:S(2)}, u32[]{:S(2)}) async-start(bf16[8,256,256]{2,1,0:T(8,128)(2,1)} %pad_maximum_fusion), calls=%async_computation.2 | async-start | bytes 2097152 | tf_op jit(solution)/shard_map/all_to_all | solution.py:436
  76.1 1.4 %collective-permute-start.2 = (f32[8,128]{1,0:T(8,128)S(1)}, f32[8,128]{1,0:T(8,128)S(1)}, u32[]{:S(2)}, u32[]{:S(2)}) collective-permute-start(f32[8,128]{1,0:T(8,128)S(1)} %copy-done.4), channel_id=1, source_target_pairs={{0,32},{16,48},{32,0},{48,16},{64,96},{80,112},{96,64},{112,80},{1... | collective-permute-start | bytes 12296 | tf_op jit(solution)/shard_map/ppermute | solution.py:414
  77.5 3.7 %collective-permute-done.2 = f32[8,128]{1,0:T(8,128)S(1)} collective-permute-done((f32[8,128]{1,0:T(8,128)S(1)}, f32[8,128]{1,0:T(8,128)S(1)}, u32[]{:S(2)}, u32[]{:S(2)}) %collective-permute-start.2) | collective-permute-done | bytes 4128 | tf_op jit(solution)/shard_map/ppermute | solution.py:414
  81.2 3.6 %collective-permute-start.3 = (f32[8,128]{1,0:T(8,128)S(1)}, f32[8,128]{1,0:T(8,128)S(1)}, u32[]{:S(2)}, u32[]{:S(2)}) collective-permute-start(f32[8,128]{1,0:T(8,128)S(1)} %add.19), channel_id=1, source_target_pairs={{0,64},{16,80},{32,96},{48,112},{64,0},{80,16},{96,32},{112,48},{1... | collective-permute-start | bytes 12296 | tf_op jit(solution)/shard_map/ppermute | solution.py:414
  84.8 7.1 %collective-permute-done.3 = f32[8,128]{1,0:T(8,128)S(1)} collective-permute-done((f32[8,128]{1,0:T(8,128)S(1)}, f32[8,128]{1,0:T(8,128)S(1)}, u32[]{:S(2)}, u32[]{:S(2)}) %collective-permute-start.3) | collective-permute-done | bytes 4128 | tf_op jit(solution)/shard_map/ppermute | solution.py:414
  91.8 0.6 add.20.sums_ref
  92.4 3.4 %rescale.1 = (bf16[2,128,4096]{2,1,0:T(8,128)(2,1)}, bf16[2,128,512]{2,1,0:T(8,128)(2,1)}) custom-call(bf16[2,128,4096]{2,1,0:T(8,128)(2,1)} %get-tuple-element.46.dq_ref, f32[2,128,256]{2,1,0:T(8,128)} %get-tuple-element.47.dw0_ref, f32[2,128,256]{2,1,0:T(8,128)} %get-tuple-element.48.dw1_ref, ...), custom_call_target="tpu_custom_call", output_to_operand_aliasing={{0}: (0, {})} | custom-call | tf_op jit(solution)/shard_map/rescale/pallas_call | solution.py:353
  95.8 1.0 %copy-done = bf16[8,256,256]{2,1,0:T(8,128)(2,1)} copy-done((bf16[8,256,256]{2,1,0:T(8,128)(2,1)}, bf16[8,256,256]{2,1,0:T(8,128)(2,1)S(1)}, u32[]{:S(2)}) %copy-start) | copy-done | bytes 1048600
  96.8 2.4 %settle.1 = bf16[2,64,512]{2,1,0:T(8,128)(2,1)} custom-call(bf16[8,256,256]{2,1,0:T(8,128)(2,1)} %copy-done, bf16[2,64,512]{2,1,0:T(8,128)(2,1)} %cache_ref.3, f32[1,128]{1,0:T(1,128)} %bitcast.11, f32[1,128]{1,0:T(1,128)} %constant.25.clone.freq_ref, s32[1]{0:T(128)} %bitcast.1.mine_ref, f32[8,128]{1,0:T(8,128)} %add.20.sums_ref), custom_call_target="tpu_custom_call" | custom-call | tf_op jit(solution)/shard_map/settle/pallas_call | solution.py:390
  (18 shorter events, 1.0 us)
Async XLA Ops:
  2.6 15.5 %all-to-all-start = ((bf16[8,144,256]{2,1,0:T(8,128)(2,1)}), bf16[8,144,256]{2,1,0:T(8,128)(2,1)S(1)}, u32[]{:S(2)}, u32[]{:S(2)}) async-start(bf16[8,144,256]{2,1,0:T(8,128)(2,1)} %get-tuple-element.30), calls=%async_computation | async-start | bytes 1179648 | tf_op jit(solution)/shard_map/all_to_all | solution.py:419
  8.8 3.9 %collective-permute-start = (bf16[16,256]{1,0:T(8,128)(2,1)}, bf16[16,256]{1,0:T(8,128)(2,1)S(1)}, u32[]{:S(2)}, u32[]{:S(2)}) collective-permute-start(bf16[16,256]{1,0:T(8,128)(2,1)} %get-tuple-element.32.facts_ref), channel_id=1, source_target_pairs={{0,16},{16,0},{32,48},{48,32},{64,80},{80,64},{96,112},{112,96},{1... | collective-permute-start | bytes 24584 | tf_op jit(solution)/shard_map/ppermute | solution.py:414
  12.6 0.6 copy-start.5
  18.1 5.9 %copy-start.2 = (bf16[8,144,256]{2,1,0:T(8,128)(2,1)}, bf16[8,144,256]{2,1,0:T(8,128)(2,1)S(1)}, u32[]{:S(2)}) copy-start(bf16[8,144,256]{2,1,0:T(8,128)(2,1)S(1)} %all-to-all-done.ga_ref.fa_ref) | copy-start | bytes 1769476
  18.1 5.9 %collective-permute-start.1 = (bf16[8,144,256]{2,1,0:T(8,128)(2,1)S(1)}, bf16[8,144,256]{2,1,0:T(8,128)(2,1)}, u32[]{:S(2)}, u32[]{:S(2)}) collective-permute-start(bf16[8,144,256]{2,1,0:T(8,128)(2,1)S(1)} %all-to-all-done.ga_ref.fa_ref), channel_id=1, source_target_pairs={{0,1},{1,0},{2,3},{3,2},{4,5},{5,4},{6,7},{7,6},{8,9},{9,8},{10,11... | collective-permute-start | bytes 1769480 | tf_op jit(solution)/shard_map/ppermute | solution.py:411
  18.2 26.4 %all-to-all-start.1 = ((bf16[16,144,256]{2,1,0:T(8,128)(2,1)}), bf16[16,144,256]{2,1,0:T(8,128)(2,1)S(1)}, u32[]{:S(2)}, u32[]{:S(2)}) async-start(bf16[16,144,256]{2,1,0:T(8,128)(2,1)} %get-tuple-element.40), calls=%async_computation.1 | async-start | bytes 2359296 | tf_op jit(solution)/shard_map/all_to_all | solution.py:425
  44.2 22.1 %collective-permute-start.4 = (bf16[8,128,256]{2,1,0:T(8,128)(2,1)}, bf16[8,128,256]{2,1,0:T(8,128)(2,1)}, u32[]{:S(2)}, u32[]{:S(2)}) collective-permute-start(bf16[8,128,256]{2,1,0:T(8,128)(2,1)} %get-tuple-element.53), channel_id=1, source_target_pairs={{0,1},{1,0},{2,3},{3,2},{4,5},{5,4},{6,7},{7,6},{8,9},{9,8},{10,11... | collective-permute-start | bytes 1572872 | tf_op jit(solution)/shard_map/ppermute | solution.py:411
  44.6 1.0 %copy-start.1 = (bf16[16,144,256]{2,1,0:T(8,128)(2,1)}, bf16[16,144,256]{2,1,0:T(8,128)(2,1)S(1)}, u32[]{:S(2)}) copy-start(bf16[16,144,256]{2,1,0:T(8,128)(2,1)S(1)} %all-to-all-done.1) | copy-start | bytes 3538948
  45.6 20.7 %copy-start.3 = (bf16[8,128,256]{2,1,0:T(8,128)(2,1)S(1)}, bf16[8,128,256]{2,1,0:T(8,128)(2,1)}, u32[]{:S(2)}) copy-start(bf16[8,128,256]{2,1,0:T(8,128)(2,1)} %get-tuple-element.52) | copy-start | bytes 1572868
  65.9 2.2 %collective-permute-start.5 = (bf16[8,128,256]{2,1,0:T(8,128)(2,1)}, bf16[8,128,256]{2,1,0:T(8,128)(2,1)S(1)}, u32[]{:S(2)}, u32[]{:S(2)}) collective-permute-start(bf16[8,128,256]{2,1,0:T(8,128)(2,1)} %get-tuple-element.55), channel_id=1, source_target_pairs={{0,1},{1,0},{2,3},{3,2},{4,5},{5,4},{6,7},{7,6},{8,9},{9,8},{10,11... | collective-permute-start | bytes 1572872 | tf_op jit(solution)/shard_map/ppermute | solution.py:411
  69.3 6.8 %copy-start.4 = (f32[8,128]{1,0:T(8,128)S(1)}, f32[8,128]{1,0:T(8,128)}, u32[]{:S(2)}) copy-start(f32[8,128]{1,0:T(8,128)} %get-tuple-element.49.stat_ref) | copy-start | bytes 12292
  70.4 25.4 %all-to-all-start.2 = ((bf16[8,256,256]{2,1,0:T(8,128)(2,1)}), bf16[8,256,256]{2,1,0:T(8,128)(2,1)S(1)}, u32[]{:S(2)}, u32[]{:S(2)}) async-start(bf16[8,256,256]{2,1,0:T(8,128)(2,1)} %pad_maximum_fusion), calls=%async_computation.2 | async-start | bytes 2097152 | tf_op jit(solution)/shard_map/all_to_all | solution.py:436
  76.1 5.1 %collective-permute-start.2 = (f32[8,128]{1,0:T(8,128)S(1)}, f32[8,128]{1,0:T(8,128)S(1)}, u32[]{:S(2)}, u32[]{:S(2)}) collective-permute-start(f32[8,128]{1,0:T(8,128)S(1)} %copy-done.4), channel_id=1, source_target_pairs={{0,32},{16,48},{32,0},{48,16},{64,96},{80,112},{96,64},{112,80},{1... | collective-permute-start | bytes 12296 | tf_op jit(solution)/shard_map/ppermute | solution.py:414
  81.2 10.6 %collective-permute-start.3 = (f32[8,128]{1,0:T(8,128)S(1)}, f32[8,128]{1,0:T(8,128)S(1)}, u32[]{:S(2)}, u32[]{:S(2)}) collective-permute-start(f32[8,128]{1,0:T(8,128)S(1)} %add.19), channel_id=1, source_target_pairs={{0,64},{16,80},{32,96},{48,112},{64,0},{80,16},{96,32},{112,48},{1... | collective-permute-start | bytes 12296 | tf_op jit(solution)/shard_map/ppermute | solution.py:414
  95.8 1.0 %copy-start = (bf16[8,256,256]{2,1,0:T(8,128)(2,1)}, bf16[8,256,256]{2,1,0:T(8,128)(2,1)S(1)}, u32[]{:S(2)}) copy-start(bf16[8,256,256]{2,1,0:T(8,128)(2,1)S(1)} %all-to-all-done.2.d_ref) | copy-start | bytes 3145732

commit v4 on v3

--- a/solution.py
+++ b/solution.py
@@ -14,7 +14,7 @@
 spread_eps = 1e-06
 LOG2E = math.log2(math.e)
 bf16, f32 = jnp.bfloat16, jnp.float32
-LIMIT = 62 * 1024 * 1024
+LIMIT = 63 * 1024 * 1024
 frequency = np.tile(rope_base ** (-np.arange(64) * 2.0 / 128), 2).astype(np.float32)[None]
 
 
@@ -113,8 +113,6 @@
         kp[plen:, 128:] = rk.astype(bf16)
         va[plen:, :128] = wv_ref[0]
         va[:, 128:] = jnp.ones_like(va[:, 128:])
-        dk[r] = jnp.zeros_like(dk[r])
-        dv[r] = jnp.zeros_like(dv[r])
 
     sh = heads // subs
     rows = sh * win
@@ -155,8 +153,8 @@
         for g in range(sh):
             dq_ref[0, :, (b * sh + g) * 128 : (b * sh + g + 1) * 128] = dq[g * win : (g + 1) * win]
     cat = lambda x: jnp.concatenate(x, axis=0) if subs > 1 else x[0]
-    dv[r] += dot(cat(a)[:, :128], e_ref[...], 0, 0)
-    dk[r] += dot(cat(qs), ds_ref[...], 0, 0)
+    dv[r] = dot(cat(a)[:, :128], e_ref[...], 0, 0)
+    dk[r] = dot(cat(qs), ds_ref[...], 0, 0)
 
     @pl.when(hb == pl.num_programs(1) - 1)
     def _():
@@ -182,14 +180,14 @@
                         outs[i][:, p * tok : (p + 1) * tok, c * 128 : (c + 1) * 128] = m
 
 
-def call(h, heads, subs, tc, scalar, qs, q, up, ga, gb, wc, qgain, kgain, cw, sw, rewards, tok, prompts, *before):
+def call(h, subs, tc, scalar, qs, q, up, ga, gb, wc, qgain, kgain, cw, sw, rewards, tok, prompts, *before):
     rolls, win, width = up.shape
     chips = ga.shape[0]
     kvh = wc.shape[2] // 256
     share = width // (128 * kvh)
     half = chips * tok
     plen = 2 * half
-    steps = share // heads
+    heads, steps = share, 1
     t = plen + win
     smem = pl.BlockSpec(memory_space=pltpu.SMEM)
     anywhere = pl.BlockSpec(memory_space=pl.ANY)
@@ -279,7 +277,7 @@
         out_shape=[jax.ShapeDtypeStruct((rolls, heads, win, 128), bf16)]
         + [jax.ShapeDtypeStruct((rolls, win, 128), f32)] * 2
         + [jax.ShapeDtypeStruct((members, second.shape[0] + 16, 256), bf16)],
-        compiler_params=pltpu.CompilerParams(vmem_limit_bytes=LIMIT),
+        compiler_params=pltpu.CompilerParams(vmem_limit_bytes=LIMIT - 3 * 1024 * 1024),
         name="ready",
     )(q, gain, frequency, offsets, second, facts, far)
 
@@ -363,9 +361,29 @@
         out_specs=[qspec, pl.BlockSpec((1, win, 512), lambda r: (r, 0, 0))],
         out_shape=[jax.ShapeDtypeStruct(dq.shape, bf16), jax.ShapeDtypeStruct((rolls, win, 512), bf16)],
         input_output_aliases={0: 0},
-        compiler_params=pltpu.CompilerParams(vmem_limit_bytes=LIMIT),
+        compiler_params=pltpu.CompilerParams(vmem_limit_bytes=LIMIT - 3 * 1024 * 1024),
         name="rescale",
     )(dq, dw0, dw1, sums, stat)
+
+
+def merge(own0, far0, own1, far1, stat_ref, there_ref, out_ref, sums_ref):
+    rows = own0.shape[1]
+    for h, (own, far) in enumerate(((own0, far0), (own1, far1))):
+        out_ref[:, h * rows : (h + 1) * rows] = (own[...].astype(f32) + far[...].astype(f32)).astype(bf16)
+    sums_ref[...] = stat_ref[...] + there_ref[...]
+
+
+def make_merge(own0, far0, own1, far1, stat, there):
+    chips, rows, width = own0.shape
+    vmem = pl.BlockSpec(memory_space=pltpu.VMEM)
+    return pl.pallas_call(
+        merge,
+        in_specs=[vmem] * 6,
+        out_specs=[vmem, vmem],
+        out_shape=[jax.ShapeDtypeStruct((chips, 2 * rows, width), bf16), jax.ShapeDtypeStruct(stat.shape, f32)],
+        compiler_params=pltpu.CompilerParams(vmem_limit_bytes=16 * 1024 * 1024),
+        name="merge",
+    )(own0, far0, own1, far1, stat, there)
 
 
 def settle(d_ref, cache_ref, kg_ref, freq_ref, mine_ref, sums_ref, out_ref, *, count):
@@ -393,7 +411,7 @@
         in_specs=[vmem, vmem, vmem, vmem, smem, vmem],
         out_specs=vmem,
         out_shape=jax.ShapeDtypeStruct(cache.shape, bf16),
-        compiler_params=pltpu.CompilerParams(vmem_limit_bytes=LIMIT),
+        compiler_params=pltpu.CompilerParams(vmem_limit_bytes=16 * 1024 * 1024),
         name="settle",
     )(d, cache, kgain, frequency, mine, sums)
 
@@ -426,16 +444,15 @@
 
     def attention(h, a, b, *before):
         return call(
-            h, 16, 4, 512, scalar, qs, queries, upstream, a, b, window_cache, qgain, kgain, cw, sw, rewards, tok, prompts, *before
+            h, 4, 512, scalar, qs, queries, upstream, a, b, window_cache, qgain, kgain, cw, sw, rewards, tok, prompts, *before
         )
 
     att, dq, dw0, _, own0, other0 = attention(0, ga, gb)
     att, dq, dw1, stat, own1, other1 = attention(1, g1, g1, att, dq)
-    merged = [(own.astype(f32) + flip(other).astype(f32)).astype(bf16) for own, other in ((own0, other0), (own1, other1))]
-    merged = jnp.concatenate(merged, axis=1)
+    merged, sums = make_merge(own0, flip(other0), own1, flip(other1), stat, far(stat, groups // 2))
     parts = lax.all_to_all(merged, "roll", 0, 0, tiled=True, axis_index_groups=same_core)
-    sums, step = stat, 2
-    while step < groups:
+    step = 2
+    while step < groups // 2:
         sums = sums + far(sums, step)
         step *= 2
     count = groups * members * rolls

time: 99.8 us -> 96.7 us (0.969)
  the two profiles are of different devices: /device:TPU:22 before, /device:TPU:0 now
where the time goes in v4:
time: 96.7 us; the launch traced here: 96.2 us
  Pallas kernels  54.2 us (56%)
  starting transfers between devices  25.7 us (27%)
  waiting for transfers between devices  11.4 us (12%)
  local copies, waits for them, and re-layouts  2.33 us (2%)
  other arithmetic  1.86 us (2%)
    pallas_call x2, Pallas kernels, call(): pl.pallas_call(functools.partial(attend, heads=heads, subs=subs, tc=tc, t...  40.4 us
    ppermute x3, starting transfers between devices, far(): return lax.ppermute(x, 'prompt', [(i, i ^ step) for i in range(groups)])  8.12 us
    all_to_all x1, starting transfers between devices, local(): lax.all_to_all(first, 'roll', 0, 0, tiled=True, axis_index_groups=same_core)  5.91 us
    all_to_all x1, starting transfers between devices, local(): lax.all_to_all(merged, 'roll', 0, 0, tiled=True, axis_index_groups=same_c...  5.61 us
    all_to_all x1, waiting for transfers between devices, local(): lax.all_to_all(merged, 'roll', 0, 0, tiled=True, axis_index_groups=same_c...  5.49 us
    all_to_all x1, starting transfers between devices, local(): lax.all_to_all(copies, 'roll', 0, 0, tiled=True)  5.2 us
    ppermute x3, waiting for transfers between devices, far(): return lax.ppermute(x, 'prompt', [(i, i ^ step) for i in range(groups)])  4.99 us
    pallas_call x1, Pallas kernels, make_ready(): pl.pallas_call(functools.partial(ready, heads=heads, plen=plen), grid=(ro...  4.86 us
  transfers between devices with their start and end apart: 9, of which 5 were waited for; matrix products, arithmetic and copies ran while one was open for 2% of the time, Pallas kernels for 51%

profile of v4, /device:TPU:0, one launch (start us, length us, event | category | flops | bytes accessed | tf_op | source)
XLA Modules:
  0.0 96.2 jit_solution(13397186553525170756)
XLA Ops:
  0.6 2.0 %pack.1 = (bf16[8,144,256]{2,1,0:T(8,128)(2,1)}, bf16[128,256]{1,0:T(8,128)(2,1)}, bf16[16,256]{1,0:T(8,128)(2,1)}) custom-call(bf16[2,64,512]{2,1,0:T(8,128)(2,1)} %cache_ref.3, f32[2]{0:T(128)} %rw_ref.3, s32[2]{0:T(128)} %assign_ref.1, f32[1,128]{1,0:T(1,128)} %bitcast.4, f32[1,128]{1,0:T(1,128)} %constant.25.clone.freq_ref, s32[1]{0:T(128)} %bitcast.1.mine_ref), custom_call_target="tpu_custom_call" | custom-call | tf_op jit(solution)/shard_map/pack/pallas_call | solution.py:321
  2.6 5.9 %all-to-all-start = ((bf16[8,144,256]{2,1,0:T(8,128)(2,1)}), bf16[8,144,256]{2,1,0:T(8,128)(2,1)S(1)}, u32[]{:S(2)}, u32[]{:S(2)}) async-start(bf16[8,144,256]{2,1,0:T(8,128)(2,1)} %get-tuple-element.32), calls=%async_computation | async-start | bytes 1179648 | tf_op jit(solution)/shard_map/all_to_all | solution.py:437
  8.5 1.5 %collective-permute-start = (bf16[16,256]{1,0:T(8,128)(2,1)}, bf16[16,256]{1,0:T(8,128)(2,1)S(1)}, u32[]{:S(2)}, u32[]{:S(2)}) collective-permute-start(bf16[16,256]{1,0:T(8,128)(2,1)} %get-tuple-element.34.facts_ref), channel_id=1, source_target_pairs={{0,16},{16,0},{32,48},{48,32},{64,80},{80,64},{96,112},{112,96},{1... | collective-permute-start | bytes 24584 | tf_op jit(solution)/shard_map/ppermute | solution.py:432
  10.0 1.3 %pad_add_fusion.scalar = s32[3]{0:T(128)} fusion(s32[1]{0:T(128)S(6)} %select_n.7, s32[2]{0:T(128)} %assign_ref.1), kind=kLoop, calls=%fused_computation | loop fusion | flops 3 | bytes 24 | tf_op jit(solution)/shard_map/concatenate | solution.py:438
  11.3 1.1 %collective-permute-done.far_ref = bf16[16,256]{1,0:T(8,128)(2,1)S(1)} collective-permute-done((bf16[16,256]{1,0:T(8,128)(2,1)}, bf16[16,256]{1,0:T(8,128)(2,1)S(1)}, u32[]{:S(2)}, u32[]{:S(2)}) %collective-permute-start) | collective-permute-done | bytes 8224 | tf_op jit(solution)/shard_map/ppermute | solution.py:432
  12.4 0.6 copy-done.8
  13.0 4.9 %ready.1 = (bf16[2,32,128,128]{3,2,1,0:T(8,128)(2,1)}, f32[2,128,128]{2,1,0:T(8,128)}, f32[2,128,128]{2,1,0:T(8,128)}, bf16[16,144,256]{2,1,0:T(8,128)(2,1)}) custom-call(bf16[2,128,4096]{2,1,0:T(8,128)(2,1)} %q_ref.5, f32[1,128]{1,0:T(1,128)} %bitcast.8, f32[1,128]{1,0:T(1,128)} %constant.25.clone.freq_ref, s32[2]{0:T(128)} %off_ref.1, ...), custom_call_target="tpu_custom_call" | custom-call | tf_op jit(solution)/shard_map/ready/pallas_call | solution.py:267
  17.9 0.9 all-to-all-done.ga_ref.fa_ref
  18.7 5.2 %all-to-all-start.1 = ((bf16[16,144,256]{2,1,0:T(8,128)(2,1)}), bf16[16,144,256]{2,1,0:T(8,128)(2,1)}, u32[]{:S(2)}, u32[]{:S(2)}) async-start(bf16[16,144,256]{2,1,0:T(8,128)(2,1)} %get-tuple-element.42), calls=%async_computation.1 | async-start | bytes 2359296 | tf_op jit(solution)/shard_map/all_to_all | solution.py:443
  23.9 20.1 %attend.2 = (bf16[2,128,4096]{2,1,0:T(8,128)(2,1)}, bf16[2,128,4096]{2,1,0:T(8,128)(2,1)}, f32[2,128,256]{2,1,0:T(8,128)}, f32[8,128]{1,0:T(8,128)}, bf16[8,128,...) custom-call(s32[3]{0:T(128)} %pad_add_fusion.scalar, bf16[2,32,128,128]{3,2,1,0:T(8,128)(2,1)} %get-tuple-element.39.qs_ref, ...), custom_call_target="tpu_custom_call" | custom-call | flops 21743271936 | bytes 5242880 | tf_op jit(solution)/shard_map/attend/pallas_call | solution.py:210
  44.1 0.6 collective-permute-start.2
  44.7 20.3 %attend.3 = (bf16[2,128,4096]{2,1,0:T(8,128)(2,1)}, bf16[2,128,4096]{2,1,0:T(8,128)(2,1)}, f32[2,128,256]{2,1,0:T(8,128)}, f32[8,128]{1,0:T(8,128)}, bf16[8,128,...) custom-call(s32[3]{0:T(128)} %pad_add_fusion.scalar, ...), custom_call_target="tpu_custom_call", output_to_operand_aliasing={{0}: (15, {}), {1}: (16, {})} | custom-call | flops 21743271936 | bytes 5242880 | tf_op jit(solution)/shard_map/attend/pallas_call | solution.py:210
  65.2 3.6 %collective-permute-start.4 = (f32[8,128]{1,0:T(8,128)}, f32[8,128]{1,0:T(8,128)S(1)}, u32[]{:S(2)}, u32[]{:S(2)}) collective-permute-start(f32[8,128]{1,0:T(8,128)} %get-tuple-element.55.stat_ref), channel_id=1, source_target_pairs={{0,64},{16,80},{32,96},{48,112},{64,0},{80,16},{96,32},{112,48},{1... | collective-permute-start | bytes 12296 | tf_op jit(solution)/shard_map/ppermute | solution.py:432
  68.8 1.8 %collective-permute-done.4.there_ref = f32[8,128]{1,0:T(8,128)S(1)} collective-permute-done((f32[8,128]{1,0:T(8,128)}, f32[8,128]{1,0:T(8,128)S(1)}, u32[]{:S(2)}, u32[]{:S(2)}) %collective-permute-start.4) | collective-permute-done | bytes 4128 | tf_op jit(solution)/shard_map/ppermute | solution.py:432
  70.6 1.0 %copy-done.1 = bf16[8,128,256]{2,1,0:T(8,128)(2,1)S(1)} copy-done((bf16[8,128,256]{2,1,0:T(8,128)(2,1)S(1)}, bf16[8,128,256]{2,1,0:T(8,128)(2,1)}, u32[]{:S(2)}) %copy-start.1) | copy-done | bytes 524312
  71.7 0.7 copy-done.4
  72.4 2.3 %merge.1 = (bf16[8,256,256]{2,1,0:T(8,128)(2,1)}, f32[8,128]{1,0:T(8,128)S(1)}) custom-call(bf16[8,128,256]{2,1,0:T(8,128)(2,1)S(1)} %copy-done, bf16[8,128,256]{2,1,0:T(8,128)(2,1)} %collective-permute-done.2.far0, bf16[8,128,256]{2,1,0:T(8,128)(2,1)S(1)} %copy-done.1, bf16[8,128,256]{2,1,0:T(8,128)(2,1)S(1)} %collective-permute-done.3.far1, ...), custom_call_target="tpu_custom_call" | custom-call | tf_op jit(solution)/shard_map/merge/pallas_call | solution.py:379
  74.7 5.6 %all-to-all-start.2 = ((bf16[8,256,256]{2,1,0:T(8,128)(2,1)}), bf16[8,256,256]{2,1,0:T(8,128)(2,1)S(1)}, u32[]{:S(2)}, u32[]{:S(2)}) async-start(bf16[8,256,256]{2,1,0:T(8,128)(2,1)} %get-tuple-element.59), calls=%async_computation.2 | async-start | bytes 2097152 | tf_op jit(solution)/shard_map/all_to_all | solution.py:453
  80.3 3.0 %collective-permute-start.5 = (f32[8,128]{1,0:T(8,128)S(1)}, f32[8,128]{1,0:T(8,128)S(1)}, u32[]{:S(2)}, u32[]{:S(2)}) collective-permute-start(f32[8,128]{1,0:T(8,128)S(1)} %get-tuple-element.56), channel_id=1, source_target_pairs={{0,32},{16,48},{32,0},{48,16},{64,96},{80,112},{96,64},{112,80},{1... | collective-permute-start | bytes 12296 | tf_op jit(solution)/shard_map/ppermute | solution.py:432
  83.3 2.1 %collective-permute-done.5 = f32[8,128]{1,0:T(8,128)S(1)} collective-permute-done((f32[8,128]{1,0:T(8,128)S(1)}, f32[8,128]{1,0:T(8,128)S(1)}, u32[]{:S(2)}, u32[]{:S(2)}) %collective-permute-start.5) | collective-permute-done | bytes 4128 | tf_op jit(solution)/shard_map/ppermute | solution.py:432
  85.4 0.6 add.10.sums_ref
  86.0 3.5 %rescale.1 = (bf16[2,128,4096]{2,1,0:T(8,128)(2,1)}, bf16[2,128,512]{2,1,0:T(8,128)(2,1)}) custom-call(bf16[2,128,4096]{2,1,0:T(8,128)(2,1)} %get-tuple-element.48.dq_ref, f32[2,128,256]{2,1,0:T(8,128)} %get-tuple-element.49.dw0_ref, f32[2,128,256]{2,1,0:T(8,128)} %get-tuple-element.50.dw1_ref, ...), custom_call_target="tpu_custom_call", output_to_operand_aliasing={{0}: (0, {})} | custom-call | tf_op jit(solution)/shard_map/rescale/pallas_call | solution.py:351
  89.5 5.5 %all-to-all-done.2.d_ref = bf16[8,256,256]{2,1,0:T(8,128)(2,1)S(1)} async-done(((bf16[8,256,256]{2,1,0:T(8,128)(2,1)}), bf16[8,256,256]{2,1,0:T(8,128)(2,1)S(1)}, u32[]{:S(2)}, u32[]{:S(2)}) %all-to-all-start.2) | async-done | bytes 1048608 | tf_op jit(solution)/shard_map/all_to_all | solution.py:453
  95.0 1.1 %settle.1 = bf16[2,64,512]{2,1,0:T(8,128)(2,1)} custom-call(bf16[8,256,256]{2,1,0:T(8,128)(2,1)S(1)} %all-to-all-done.2.d_ref, bf16[2,64,512]{2,1,0:T(8,128)(2,1)S(1)} %copy-done.2, f32[1,128]{1,0:T(1,128)S(1)} %bitcast.7, f32[1,128]{1,0:T(1,128)S(1)} %copy-done.5, s32[1]{0:T(128)} %bitcast.1.mine_ref, f32[8,128]{1,0:T(8,128)S(1)} %copy-done.3), custom_call_target="tpu_custom_call" | custom-call | tf_op jit(solution)/shard_map/settle/pallas_call | solution.py:408
  (21 shorter events, 0.3 us)
Async XLA Ops:
  2.6 16.1 %all-to-all-start = ((bf16[8,144,256]{2,1,0:T(8,128)(2,1)}), bf16[8,144,256]{2,1,0:T(8,128)(2,1)S(1)}, u32[]{:S(2)}, u32[]{:S(2)}) async-start(bf16[8,144,256]{2,1,0:T(8,128)(2,1)} %get-tuple-element.32), calls=%async_computation | async-start | bytes 1179648 | tf_op jit(solution)/shard_map/all_to_all | solution.py:437
  8.5 3.9 %collective-permute-start = (bf16[16,256]{1,0:T(8,128)(2,1)}, bf16[16,256]{1,0:T(8,128)(2,1)S(1)}, u32[]{:S(2)}, u32[]{:S(2)}) collective-permute-start(bf16[16,256]{1,0:T(8,128)(2,1)} %get-tuple-element.34.facts_ref), channel_id=1, source_target_pairs={{0,16},{16,0},{32,48},{48,32},{64,80},{80,64},{96,112},{112,96},{1... | collective-permute-start | bytes 24584 | tf_op jit(solution)/shard_map/ppermute | solution.py:432
  12.4 0.6 copy-start.8
  18.7 5.2 %copy-start.7 = (bf16[8,144,256]{2,1,0:T(8,128)(2,1)}, bf16[8,144,256]{2,1,0:T(8,128)(2,1)S(1)}, u32[]{:S(2)}) copy-start(bf16[8,144,256]{2,1,0:T(8,128)(2,1)S(1)} %all-to-all-done.ga_ref.fa_ref) | copy-start | bytes 1769476
  18.7 5.2 %collective-permute-start.1 = (bf16[8,144,256]{2,1,0:T(8,128)(2,1)S(1)}, bf16[8,144,256]{2,1,0:T(8,128)(2,1)}, u32[]{:S(2)}, u32[]{:S(2)}) collective-permute-start(bf16[8,144,256]{2,1,0:T(8,128)(2,1)S(1)} %all-to-all-done.ga_ref.fa_ref), channel_id=1, source_target_pairs={{0,1},{1,0},{2,3},{3,2},{4,5},{5,4},{6,7},{7,6},{8,9},{9,8},{10,11... | collective-permute-start | bytes 1769480 | tf_op jit(solution)/shard_map/ppermute | solution.py:429
  18.7 26.0 %all-to-all-start.1 = ((bf16[16,144,256]{2,1,0:T(8,128)(2,1)}), bf16[16,144,256]{2,1,0:T(8,128)(2,1)}, u32[]{:S(2)}, u32[]{:S(2)}) async-start(bf16[16,144,256]{2,1,0:T(8,128)(2,1)} %get-tuple-element.42), calls=%async_computation.1 | async-start | bytes 2359296 | tf_op jit(solution)/shard_map/all_to_all | solution.py:443
  44.1 26.5 %collective-permute-start.2 = (bf16[8,128,256]{2,1,0:T(8,128)(2,1)}, bf16[8,128,256]{2,1,0:T(8,128)(2,1)}, u32[]{:S(2)}, u32[]{:S(2)}) collective-permute-start(bf16[8,128,256]{2,1,0:T(8,128)(2,1)} %get-tuple-element.52), channel_id=1, source_target_pairs={{0,1},{1,0},{2,3},{3,2},{4,5},{5,4},{6,7},{7,6},{8,9},{9,8},{10,11... | collective-permute-start | bytes 1572872 | tf_op jit(solution)/shard_map/ppermute | solution.py:429
  44.7 25.9 %copy-start = (bf16[8,128,256]{2,1,0:T(8,128)(2,1)S(1)}, bf16[8,128,256]{2,1,0:T(8,128)(2,1)}, u32[]{:S(2)}) copy-start(bf16[8,128,256]{2,1,0:T(8,128)(2,1)} %get-tuple-element.51.own0) | copy-start | bytes 1572868
  65.0 5.6 %collective-permute-start.3 = (bf16[8,128,256]{2,1,0:T(8,128)(2,1)}, bf16[8,128,256]{2,1,0:T(8,128)(2,1)S(1)}, u32[]{:S(2)}, u32[]{:S(2)}) collective-permute-start(bf16[8,128,256]{2,1,0:T(8,128)(2,1)} %get-tuple-element.54), channel_id=1, source_target_pairs={{0,1},{1,0},{2,3},{3,2},{4,5},{5,4},{6,7},{7,6},{8,9},{9,8},{10,11... | collective-permute-start | bytes 1572872 | tf_op jit(solution)/shard_map/ppermute | solution.py:429
  65.2 5.4 %collective-permute-start.4 = (f32[8,128]{1,0:T(8,128)}, f32[8,128]{1,0:T(8,128)S(1)}, u32[]{:S(2)}, u32[]{:S(2)}) collective-permute-start(f32[8,128]{1,0:T(8,128)} %get-tuple-element.55.stat_ref), channel_id=1, source_target_pairs={{0,64},{16,80},{32,96},{48,112},{64,0},{80,16},{96,32},{112,48},{1... | collective-permute-start | bytes 12296 | tf_op jit(solution)/shard_map/ppermute | solution.py:432
  70.6 1.0 %copy-start.1 = (bf16[8,128,256]{2,1,0:T(8,128)(2,1)S(1)}, bf16[8,128,256]{2,1,0:T(8,128)(2,1)}, u32[]{:S(2)}) copy-start(bf16[8,128,256]{2,1,0:T(8,128)(2,1)} %get-tuple-element.53.own1) | copy-start | bytes 1572868
  71.7 0.7 copy-start.4
  74.7 20.4 %copy-start.2 = (bf16[2,64,512]{2,1,0:T(8,128)(2,1)S(1)}, bf16[2,64,512]{2,1,0:T(8,128)(2,1)}, u32[]{:S(2)}) copy-start(bf16[2,64,512]{2,1,0:T(8,128)(2,1)} %cache_ref.3) | copy-start | bytes 393220
  74.7 20.4 %copy-start.5 = (f32[1,128]{1,0:T(1,128)S(1)}, f32[1,128]{1,0:T(1,128)}, u32[]{:S(2)}) copy-start(f32[1,128]{1,0:T(1,128)} %constant.25.clone.freq_ref) | copy-start | bytes 1540
  74.7 20.4 %copy-start.6 = (f32[128]{0:T(128)S(1)}, f32[128]{0:T(128)}, u32[]{:S(2)}) copy-start(f32[128]{0:T(128)} %param.11) | copy-start | bytes 1540
  74.7 20.4 %all-to-all-start.2 = ((bf16[8,256,256]{2,1,0:T(8,128)(2,1)}), bf16[8,256,256]{2,1,0:T(8,128)(2,1)S(1)}, u32[]{:S(2)}, u32[]{:S(2)}) async-start(bf16[8,256,256]{2,1,0:T(8,128)(2,1)} %get-tuple-element.59), calls=%async_computation.2 | async-start | bytes 2097152 | tf_op jit(solution)/shard_map/all_to_all | solution.py:453
  80.3 5.1 %collective-permute-start.5 = (f32[8,128]{1,0:T(8,128)S(1)}, f32[8,128]{1,0:T(8,128)S(1)}, u32[]{:S(2)}, u32[]{:S(2)}) collective-permute-start(f32[8,128]{1,0:T(8,128)S(1)} %get-tuple-element.56), channel_id=1, source_target_pairs={{0,32},{16,48},{32,0},{48,16},{64,96},{80,112},{96,64},{112,80},{1... | collective-permute-start | bytes 12296 | tf_op jit(solution)/shard_map/ppermute | solution.py:432
  86.0 9.1 %copy-start.3 = (f32[8,128]{1,0:T(8,128)S(1)}, f32[8,128]{1,0:T(8,128)}, u32[]{:S(2)}) copy-start(f32[8,128]{1,0:T(8,128)} %add.10.sums_ref) | copy-start | bytes 12292

commit v5 on v4

--- a/solution.py
+++ b/solution.py
@@ -375,13 +375,15 @@
 
 def make_merge(own0, far0, own1, far1, stat, there):
     chips, rows, width = own0.shape
-    vmem = pl.BlockSpec(memory_space=pltpu.VMEM)
+    whole = pl.BlockSpec((chips, rows, width), lambda i: (0, 0, 0))
+    small = pl.BlockSpec((8, 128), lambda i: (0, 0))
     return pl.pallas_call(
         merge,
-        in_specs=[vmem] * 6,
-        out_specs=[vmem, vmem],
+        grid=(1,),
+        in_specs=[whole] * 4 + [small] * 2,
+        out_specs=[pl.BlockSpec((chips, 2 * rows, width), lambda i: (0, 0, 0)), small],
         out_shape=[jax.ShapeDtypeStruct((chips, 2 * rows, width), bf16), jax.ShapeDtypeStruct(stat.shape, f32)],
-        compiler_params=pltpu.CompilerParams(vmem_limit_bytes=16 * 1024 * 1024),
+        compiler_params=pltpu.CompilerParams(vmem_limit_bytes=LIMIT - 2 * 1024 * 1024),
         name="merge",
     )(own0, far0, own1, far1, stat, there)
 
@@ -444,7 +446,7 @@
 
     def attention(h, a, b, *before):
         return call(
-            h, 4, 512, scalar, qs, queries, upstream, a, b, window_cache, qgain, kgain, cw, sw, rewards, tok, prompts, *before
+            h, 2, 1024, scalar, qs, queries, upstream, a, b, window_cache, qgain, kgain, cw, sw, rewards, tok, prompts, *before
         )
 
     att, dq, dw0, _, own0, other0 = attention(0, ga, gb)

time: 96.7 us -> 96 us (level)
    unnamed x18 -> x20, local copies, waits for them, and re-layouts: 2.33 us -> 1.58 us
where the time goes in v5:
time: 96 us; the launch traced here: 95.5 us
  Pallas kernels  54.3 us (57%)
  starting transfers between devices  25.8 us (27%)
  waiting for transfers between devices  11.3 us (12%)
  other arithmetic  1.84 us (2%)
  local copies, waits for them, and re-layouts  1.58 us (2%)
    pallas_call x2, Pallas kernels, call(): pl.pallas_call(functools.partial(attend, heads=heads, subs=subs, tc=tc, t...  40 us
    ppermute x3, starting transfers between devices, far(): return lax.ppermute(x, 'prompt', [(i, i ^ step) for i in range(groups)])  8.17 us
    all_to_all x1, starting transfers between devices, local(): lax.all_to_all(first, 'roll', 0, 0, tiled=True, axis_index_groups=same_core)  5.91 us
    all_to_all x1, starting transfers between devices, local(): lax.all_to_all(merged, 'roll', 0, 0, tiled=True, axis_index_groups=same_c...  5.64 us
    all_to_all x1, waiting for transfers between devices, local(): lax.all_to_all(merged, 'roll', 0, 0, tiled=True, axis_index_groups=same_c...  5.4 us
    all_to_all x1, starting transfers between devices, local(): lax.all_to_all(copies, 'roll', 0, 0, tiled=True)  5.2 us
    ppermute x3, waiting for transfers between devices, far(): return lax.ppermute(x, 'prompt', [(i, i ^ step) for i in range(groups)])  5.01 us
    pallas_call x1, Pallas kernels, make_ready(): pl.pallas_call(functools.partial(ready, heads=heads, plen=plen), grid=(ro...  4.85 us
  transfers between devices with their start and end apart: 9, of which 5 were waited for; matrix products, arithmetic and copies ran while one was open for 2% of the time, Pallas kernels for 51%

profile of v5, /device:TPU:0, one launch (start us, length us, event | category | flops | bytes accessed | tf_op | source)
XLA Modules:
  0.0 95.5 jit_solution(9969764556858635197)
XLA Ops:
  0.6 2.0 %pack.1 = (bf16[8,144,256]{2,1,0:T(8,128)(2,1)}, bf16[128,256]{1,0:T(8,128)(2,1)}, bf16[16,256]{1,0:T(8,128)(2,1)}) custom-call(bf16[2,64,512]{2,1,0:T(8,128)(2,1)} %cache_ref.3, f32[2]{0:T(128)} %rw_ref.3, s32[2]{0:T(128)} %assign_ref.1, f32[1,128]{1,0:T(1,128)} %bitcast.4, f32[1,128]{1,0:T(1,128)} %constant.25.clone.freq_ref, s32[1]{0:T(128)} %bitcast.1.mine_ref), custom_call_target="tpu_custom_call" | custom-call | tf_op jit(solution)/shard_map/pack/pallas_call | solution.py:321
  2.6 5.9 %all-to-all-start = ((bf16[8,144,256]{2,1,0:T(8,128)(2,1)}), bf16[8,144,256]{2,1,0:T(8,128)(2,1)S(1)}, u32[]{:S(2)}, u32[]{:S(2)}) async-start(bf16[8,144,256]{2,1,0:T(8,128)(2,1)} %get-tuple-element.32), calls=%async_computation | async-start | bytes 1179648 | tf_op jit(solution)/shard_map/all_to_all | solution.py:439
  8.5 1.5 %collective-permute-start = (bf16[16,256]{1,0:T(8,128)(2,1)}, bf16[16,256]{1,0:T(8,128)(2,1)S(1)}, u32[]{:S(2)}, u32[]{:S(2)}) collective-permute-start(bf16[16,256]{1,0:T(8,128)(2,1)} %get-tuple-element.34.facts_ref), channel_id=1, source_target_pairs={{0,16},{16,0},{32,48},{48,32},{64,80},{80,64},{96,112},{112,96},{1... | collective-permute-start | bytes 24584 | tf_op jit(solution)/shard_map/ppermute | solution.py:434
  10.0 1.2 %pad_add_fusion.scalar = s32[3]{0:T(128)} fusion(s32[1]{0:T(128)S(6)} %select_n.7, s32[2]{0:T(128)} %assign_ref.1), kind=kLoop, calls=%fused_computation | loop fusion | flops 3 | bytes 24 | tf_op jit(solution)/shard_map/concatenate | solution.py:440
  11.3 1.1 %collective-permute-done.far_ref = bf16[16,256]{1,0:T(8,128)(2,1)S(1)} collective-permute-done((bf16[16,256]{1,0:T(8,128)(2,1)}, bf16[16,256]{1,0:T(8,128)(2,1)S(1)}, u32[]{:S(2)}, u32[]{:S(2)}) %collective-permute-start) | collective-permute-done | bytes 8224 | tf_op jit(solution)/shard_map/ppermute | solution.py:434
  12.4 0.6 copy-done.7
  13.0 4.9 %ready.1 = (bf16[2,32,128,128]{3,2,1,0:T(8,128)(2,1)}, f32[2,128,128]{2,1,0:T(8,128)}, f32[2,128,128]{2,1,0:T(8,128)}, bf16[16,144,256]{2,1,0:T(8,128)(2,1)}) custom-call(bf16[2,128,4096]{2,1,0:T(8,128)(2,1)} %q_ref.5, f32[1,128]{1,0:T(1,128)} %bitcast.8, f32[1,128]{1,0:T(1,128)} %constant.25.clone.freq_ref, s32[2]{0:T(128)} %off_ref.1, ...), custom_call_target="tpu_custom_call" | custom-call | tf_op jit(solution)/shard_map/ready/pallas_call | solution.py:267
  17.8 0.9 all-to-all-done.ga_ref.fa_ref
  18.7 5.2 %all-to-all-start.1 = ((bf16[16,144,256]{2,1,0:T(8,128)(2,1)}), bf16[16,144,256]{2,1,0:T(8,128)(2,1)}, u32[]{:S(2)}, u32[]{:S(2)}) async-start(bf16[16,144,256]{2,1,0:T(8,128)(2,1)} %get-tuple-element.42), calls=%async_computation.1 | async-start | bytes 2359296 | tf_op jit(solution)/shard_map/all_to_all | solution.py:445
  23.9 20.0 %attend.2 = (bf16[2,128,4096]{2,1,0:T(8,128)(2,1)}, bf16[2,128,4096]{2,1,0:T(8,128)(2,1)}, f32[2,128,256]{2,1,0:T(8,128)}, f32[8,128]{1,0:T(8,128)}, bf16[8,128,...) custom-call(s32[3]{0:T(128)} %pad_add_fusion.scalar, bf16[2,32,128,128]{3,2,1,0:T(8,128)(2,1)} %get-tuple-element.39.qs_ref, ...), custom_call_target="tpu_custom_call" | custom-call | flops 21743271936 | bytes 5242880 | tf_op jit(solution)/shard_map/attend/pallas_call | solution.py:210
  44.0 0.6 collective-permute-start.2
  44.6 20.0 %attend.3 = (bf16[2,128,4096]{2,1,0:T(8,128)(2,1)}, bf16[2,128,4096]{2,1,0:T(8,128)(2,1)}, f32[2,128,256]{2,1,0:T(8,128)}, f32[8,128]{1,0:T(8,128)}, bf16[8,128,...) custom-call(s32[3]{0:T(128)} %pad_add_fusion.scalar, ...), custom_call_target="tpu_custom_call", output_to_operand_aliasing={{0}: (15, {}), {1}: (16, {})} | custom-call | flops 21743271936 | bytes 5242880 | tf_op jit(solution)/shard_map/attend/pallas_call | solution.py:210
  64.6 0.2 collective-permute-start.3
  64.8 3.6 %collective-permute-start.4 = (f32[8,128]{1,0:T(8,128)}, f32[8,128]{1,0:T(8,128)S(1)}, u32[]{:S(2)}, u32[]{:S(2)}) collective-permute-start(f32[8,128]{1,0:T(8,128)} %get-tuple-element.55.stat_ref), channel_id=1, source_target_pairs={{0,64},{16,80},{32,96},{48,112},{64,0},{80,16},{96,32},{112,48},{1... | collective-permute-start | bytes 12296 | tf_op jit(solution)/shard_map/ppermute | solution.py:434
  68.4 1.8 %collective-permute-done.4.there_ref = f32[8,128]{1,0:T(8,128)S(1)} collective-permute-done((f32[8,128]{1,0:T(8,128)}, f32[8,128]{1,0:T(8,128)S(1)}, u32[]{:S(2)}, u32[]{:S(2)}) %collective-permute-start.4) | collective-permute-done | bytes 4128 | tf_op jit(solution)/shard_map/ppermute | solution.py:434
  70.2 0.6 copy-done.8
  71.2 2.8 %merge.1 = (bf16[8,256,256]{2,1,0:T(8,128)(2,1)}, f32[8,128]{1,0:T(8,128)}) custom-call(bf16[8,128,256]{2,1,0:T(8,128)(2,1)} %get-tuple-element.51.own0, bf16[8,128,256]{2,1,0:T(8,128)(2,1)} %copy-done.5, bf16[8,128,256]{2,1,0:T(8,128)(2,1)} %get-tuple-element.53.own1, bf16[8,128,256]{2,1,0:T(8,128)(2,1)} %copy-done.6, f32[8,128]{1,0:T(8,128)} %get-tuple-element.55.stat_ref, ...), custom_call_target="tpu_custom_call" | custom-call | tf_op jit(solution)/shard_map/merge/pallas_call | solution.py:380
  74.0 5.6 %all-to-all-start.2 = ((bf16[8,256,256]{2,1,0:T(8,128)(2,1)}), bf16[8,256,256]{2,1,0:T(8,128)(2,1)S(1)}, u32[]{:S(2)}, u32[]{:S(2)}) async-start(bf16[8,256,256]{2,1,0:T(8,128)(2,1)} %get-tuple-element.59), calls=%async_computation.2 | async-start | bytes 2097152 | tf_op jit(solution)/shard_map/all_to_all | solution.py:455
  79.7 3.1 %collective-permute-start.5 = (f32[8,128]{1,0:T(8,128)S(1)}, f32[8,128]{1,0:T(8,128)S(1)}, u32[]{:S(2)}, u32[]{:S(2)}) collective-permute-start(f32[8,128]{1,0:T(8,128)S(1)} %copy-done.9), channel_id=1, source_target_pairs={{0,32},{16,48},{32,0},{48,16},{64,96},{80,112},{96,64},{112,80},{1... | collective-permute-start | bytes 12296 | tf_op jit(solution)/shard_map/ppermute | solution.py:434
  82.7 2.1 %collective-permute-done.5 = f32[8,128]{1,0:T(8,128)S(1)} collective-permute-done((f32[8,128]{1,0:T(8,128)S(1)}, f32[8,128]{1,0:T(8,128)S(1)}, u32[]{:S(2)}, u32[]{:S(2)}) %collective-permute-start.5) | collective-permute-done | bytes 4128 | tf_op jit(solution)/shard_map/ppermute | solution.py:434
  84.8 0.6 add.10.sums_ref
  85.4 3.5 %rescale.1 = (bf16[2,128,4096]{2,1,0:T(8,128)(2,1)}, bf16[2,128,512]{2,1,0:T(8,128)(2,1)}) custom-call(bf16[2,128,4096]{2,1,0:T(8,128)(2,1)} %get-tuple-element.48.dq_ref, f32[2,128,256]{2,1,0:T(8,128)} %get-tuple-element.49.dw0_ref, f32[2,128,256]{2,1,0:T(8,128)} %get-tuple-element.50.dw1_ref, ...), custom_call_target="tpu_custom_call", output_to_operand_aliasing={{0}: (0, {})} | custom-call | tf_op jit(solution)/shard_map/rescale/pallas_call | solution.py:351
  89.0 5.4 %all-to-all-done.2.d_ref = bf16[8,256,256]{2,1,0:T(8,128)(2,1)S(1)} async-done(((bf16[8,256,256]{2,1,0:T(8,128)(2,1)}), bf16[8,256,256]{2,1,0:T(8,128)(2,1)S(1)}, u32[]{:S(2)}, u32[]{:S(2)}) %all-to-all-start.2) | async-done | bytes 1048608 | tf_op jit(solution)/shard_map/all_to_all | solution.py:455
  94.4 1.1 %settle.1 = bf16[2,64,512]{2,1,0:T(8,128)(2,1)} custom-call(bf16[8,256,256]{2,1,0:T(8,128)(2,1)S(1)} %all-to-all-done.2.d_ref, bf16[2,64,512]{2,1,0:T(8,128)(2,1)S(1)} %copy-done, f32[1,128]{1,0:T(1,128)S(1)} %bitcast.7, f32[1,128]{1,0:T(1,128)S(1)} %copy-done.2, s32[1]{0:T(128)} %bitcast.1.mine_ref, f32[8,128]{1,0:T(8,128)S(1)} %copy-done.1), custom_call_target="tpu_custom_call" | custom-call | tf_op jit(solution)/shard_map/settle/pallas_call | solution.py:410
  (23 shorter events, 0.4 us)
Async XLA Ops:
  2.6 16.1 %all-to-all-start = ((bf16[8,144,256]{2,1,0:T(8,128)(2,1)}), bf16[8,144,256]{2,1,0:T(8,128)(2,1)S(1)}, u32[]{:S(2)}, u32[]{:S(2)}) async-start(bf16[8,144,256]{2,1,0:T(8,128)(2,1)} %get-tuple-element.32), calls=%async_computation | async-start | bytes 1179648 | tf_op jit(solution)/shard_map/all_to_all | solution.py:439
  8.5 3.9 %collective-permute-start = (bf16[16,256]{1,0:T(8,128)(2,1)}, bf16[16,256]{1,0:T(8,128)(2,1)S(1)}, u32[]{:S(2)}, u32[]{:S(2)}) collective-permute-start(bf16[16,256]{1,0:T(8,128)(2,1)} %get-tuple-element.34.facts_ref), channel_id=1, source_target_pairs={{0,16},{16,0},{32,48},{48,32},{64,80},{80,64},{96,112},{112,96},{1... | collective-permute-start | bytes 24584 | tf_op jit(solution)/shard_map/ppermute | solution.py:434
  12.4 0.6 copy-start.7
  18.7 5.2 %copy-start.4 = (bf16[8,144,256]{2,1,0:T(8,128)(2,1)}, bf16[8,144,256]{2,1,0:T(8,128)(2,1)S(1)}, u32[]{:S(2)}) copy-start(bf16[8,144,256]{2,1,0:T(8,128)(2,1)S(1)} %all-to-all-done.ga_ref.fa_ref) | copy-start | bytes 1769476
  18.7 5.2 %collective-permute-start.1 = (bf16[8,144,256]{2,1,0:T(8,128)(2,1)S(1)}, bf16[8,144,256]{2,1,0:T(8,128)(2,1)}, u32[]{:S(2)}, u32[]{:S(2)}) collective-permute-start(bf16[8,144,256]{2,1,0:T(8,128)(2,1)S(1)} %all-to-all-done.ga_ref.fa_ref), channel_id=1, source_target_pairs={{0,1},{1,0},{2,3},{3,2},{4,5},{5,4},{6,7},{7,6},{8,9},{9,8},{10,11... | collective-permute-start | bytes 1769480 | tf_op jit(solution)/shard_map/ppermute | solution.py:431
  18.7 25.9 %all-to-all-start.1 = ((bf16[16,144,256]{2,1,0:T(8,128)(2,1)}), bf16[16,144,256]{2,1,0:T(8,128)(2,1)}, u32[]{:S(2)}, u32[]{:S(2)}) async-start(bf16[16,144,256]{2,1,0:T(8,128)(2,1)} %get-tuple-element.42), calls=%async_computation.1 | async-start | bytes 2359296 | tf_op jit(solution)/shard_map/all_to_all | solution.py:445
  44.0 26.3 %collective-permute-start.2 = (bf16[8,128,256]{2,1,0:T(8,128)(2,1)}, bf16[8,128,256]{2,1,0:T(8,128)(2,1)S(1)}, u32[]{:S(2)}, u32[]{:S(2)}) collective-permute-start(bf16[8,128,256]{2,1,0:T(8,128)(2,1)} %get-tuple-element.52), channel_id=1, source_target_pairs={{0,1},{1,0},{2,3},{3,2},{4,5},{5,4},{6,7},{7,6},{8,9},{9,8},{10,11... | collective-permute-start | bytes 1572872 | tf_op jit(solution)/shard_map/ppermute | solution.py:431
  64.6 5.6 %collective-permute-start.3 = (bf16[8,128,256]{2,1,0:T(8,128)(2,1)}, bf16[8,128,256]{2,1,0:T(8,128)(2,1)S(1)}, u32[]{:S(2)}, u32[]{:S(2)}) collective-permute-start(bf16[8,128,256]{2,1,0:T(8,128)(2,1)} %get-tuple-element.54), channel_id=1, source_target_pairs={{0,1},{1,0},{2,3},{3,2},{4,5},{5,4},{6,7},{7,6},{8,9},{9,8},{10,11... | collective-permute-start | bytes 1572872 | tf_op jit(solution)/shard_map/ppermute | solution.py:431
  64.8 5.4 %collective-permute-start.4 = (f32[8,128]{1,0:T(8,128)}, f32[8,128]{1,0:T(8,128)S(1)}, u32[]{:S(2)}, u32[]{:S(2)}) collective-permute-start(f32[8,128]{1,0:T(8,128)} %get-tuple-element.55.stat_ref), channel_id=1, source_target_pairs={{0,64},{16,80},{32,96},{48,112},{64,0},{80,16},{96,32},{112,48},{1... | collective-permute-start | bytes 12296 | tf_op jit(solution)/shard_map/ppermute | solution.py:434
  70.2 0.6 copy-start.8
  70.2 0.8 copy-start.5
  70.2 1.0 %copy-start.6 = (bf16[8,128,256]{2,1,0:T(8,128)(2,1)}, bf16[8,128,256]{2,1,0:T(8,128)(2,1)S(1)}, u32[]{:S(2)}) copy-start(bf16[8,128,256]{2,1,0:T(8,128)(2,1)S(1)} %collective-permute-done.3.far1) | copy-start | bytes 1572868
  74.0 5.7 %copy-start.9 = (f32[8,128]{1,0:T(8,128)S(1)}, f32[8,128]{1,0:T(8,128)}, u32[]{:S(2)}) copy-start(f32[8,128]{1,0:T(8,128)} %get-tuple-element.56) | copy-start | bytes 12292
  74.0 20.4 %copy-start = (bf16[2,64,512]{2,1,0:T(8,128)(2,1)S(1)}, bf16[2,64,512]{2,1,0:T(8,128)(2,1)}, u32[]{:S(2)}) copy-start(bf16[2,64,512]{2,1,0:T(8,128)(2,1)} %cache_ref.3) | copy-start | bytes 393220
  74.0 20.4 %copy-start.2 = (f32[1,128]{1,0:T(1,128)S(1)}, f32[1,128]{1,0:T(1,128)}, u32[]{:S(2)}) copy-start(f32[1,128]{1,0:T(1,128)} %constant.25.clone.freq_ref) | copy-start | bytes 1540
  74.0 20.4 %copy-start.3 = (f32[128]{0:T(128)S(1)}, f32[128]{0:T(128)}, u32[]{:S(2)}) copy-start(f32[128]{0:T(128)} %param.11) | copy-start | bytes 1540
  74.0 20.4 %all-to-all-start.2 = ((bf16[8,256,256]{2,1,0:T(8,128)(2,1)}), bf16[8,256,256]{2,1,0:T(8,128)(2,1)S(1)}, u32[]{:S(2)}, u32[]{:S(2)}) async-start(bf16[8,256,256]{2,1,0:T(8,128)(2,1)} %get-tuple-element.59), calls=%async_computation.2 | async-start | bytes 2097152 | tf_op jit(solution)/shard_map/all_to_all | solution.py:455
  79.7 5.2 %collective-permute-start.5 = (f32[8,128]{1,0:T(8,128)S(1)}, f32[8,128]{1,0:T(8,128)S(1)}, u32[]{:S(2)}, u32[]{:S(2)}) collective-permute-start(f32[8,128]{1,0:T(8,128)S(1)} %copy-done.9), channel_id=1, source_target_pairs={{0,32},{16,48},{32,0},{48,16},{64,96},{80,112},{96,64},{112,80},{1... | collective-permute-start | bytes 12296 | tf_op jit(solution)/shard_map/ppermute | solution.py:434
  85.4 9.0 %copy-start.1 = (f32[8,128]{1,0:T(8,128)S(1)}, f32[8,128]{1,0:T(8,128)}, u32[]{:S(2)}) copy-start(f32[8,128]{1,0:T(8,128)} %add.10.sums_ref) | copy-start | bytes 12292
